TPU v7x, 256 devices: a whole 4x4x8 slice. The times are simulated.
256 devices in a mesh: region: 16 (over z, core), chan: 16 (over x, y).
Axes of the slice: x: 4, y: 4, z: 8, core: 2. Of those that a mesh axis runs over, the one named last changes fastest.
Arguments:
- features: bfloat16 [384, 256, 256], P('chan', 'region'), may hold values from -6 to 6
- cotangent: bfloat16 [384, 256, 256], P('chan', 'region'), may hold values from -12 to 12
- neighbours: int32 [8, 256], P(None, 'region'), may hold values from 0 to 256, as said below
- kernel: float32 [384, 49], P('chan'), may hold values from -0.875 to 0.875
- norm_gain: float32 [384], replicated, may hold values from 0.25 to 1.75
- norm_shift: float32 [384], replicated, may hold values from -3 to 3
- weight_in: bfloat16 [1536, 384], replicated, may hold values from -0.3125 to 0.3125
- bias_in: float32 [1536], replicated, may hold values from -3 to 3
- weight_out: bfloat16 [384, 1536], replicated, may hold values from -0.15625 to 0.15625
- layer_scale: float32 [384], replicated, may hold values from 0.3 to 1
Outputs:
- output: bfloat16 [384, 256, 256], P('chan', 'region')
- input_grad: bfloat16 [384, 256, 256], P('chan', 'region')
- grad_weight_in: float32 [1536, 384], replicated
- grad_weight_out: float32 [384, 1536], replicated
- grad_bias_in: float32 [1536], replicated
- grad_gain: float32 [384], replicated
- grad_shift: float32 [384], replicated
- grad_scale: float32 [384], replicated
- grad_kernel: float32 [384, 49], P('chan')
Inputs may be any that keep to these rules, and one draw needn't show every extreme that they name: `neighbours`: tiles are numbered row by row over the foreground cells of a slab 8 tiles across, half of whose cells are foreground. Row d holds for each tile the tile beside it in direction d (north, south, west, east, north-west, north-east, south-west, south-east), or 256 where that cell is background or outside the slab. Every neighbour lies in the tile's own block of 16 tiles or in an adjacent one.
All inputs are finite; a program needn't handle non-finite values.
Results may differ from a plain program's by a relative error of at most 0.008.
Values may be sent and summed in bfloat16 or wider, within the bound.
No kernel may reach another device: no remote copies, remote signals or barrier semaphores. Data moves between devices by JAX's collectives and lax.ppermute only.
A program may use at most 128 MiB of HBM per device.

v0:
```python
import math

import jax
import jax.numpy as jnp
from jax import lax
from jax.experimental import pallas as pl
from jax.experimental.pallas import tpu as pltpu
from jax.sharding import PartitionSpec as P

TS = 16
CH = 24
TILE = 16
PIX = 256
ROWS = CH * TILE
C = 384
HID = 1536
PART = 96
EXTRA = 16
F32 = jnp.float32
BF = jnp.bfloat16
NT = (((1,), (1,)), ((), ()))
NN = (((1,), (0,)), ((), ()))
VMEM_LIMIT = 48 * 1024 * 1024


def iota(shape, dim):
    return lax.broadcasted_iota(jnp.int32, shape, dim)


def dot(left, right, dims=NN):
    return lax.dot_general(left, right, dims, preferred_element_type=F32)


def eye(n):
    return (iota((n, n), 0) == iota((n, n), 1)).astype(F32).astype(BF)


def tile_major():
    column = iota((ROWS, ROWS), 1)
    target = (column & 15) * CH + (column >> 4)
    return (iota((ROWS, ROWS), 0) == target).astype(F32).astype(BF)


def chan_major():
    row = iota((ROWS, ROWS), 0)
    target = (row & 15) * CH + (row >> 4)
    return (iota((ROWS, ROWS), 1) == target).astype(F32).astype(BF)


def fill_padded(pad, own, low, high, lookup):
    identity = eye(PIX)
    own_t = dot(identity, own, NT)
    own_b = own_t.astype(BF)
    low_b = dot(identity, low, NT).astype(BF)
    high_b = dot(identity, high, NT).astype(BF)
    row = iota((ROWS, 128), 0)
    lane = iota((ROWS, 128), 1)
    key = jnp.where(((row >> 4) & 7) == (lane >> 4), (row >> 7) * 16 + (row & 15), -1)

    def pick(directions):
        parts = [
            (key == lookup[d : d + 1, :]).astype(F32).astype(BF) for d in directions
        ]
        return jnp.concatenate(parts, axis=1)

    north = pick((0, 4, 5))
    south = pick((1, 6, 7))
    sides = pick((2, 3))
    for g in range(3):
        lanes = slice(g * 128, (g + 1) * 128)
        table = jnp.concatenate([low_b[:, lanes], own_b[:, lanes], high_b[:, lanes]], axis=1)
        top = dot(table[208:256], north)
        bottom = dot(table[0:48], south)
        side = dot(table, sides)
        pad[g, 3:19, 3:19, :] = own_t[:, lanes].reshape(16, 16, 128)
        pad[g, 0:3, 3:19, :] = top[:, 0:128].reshape(3, 16, 128)
        pad[g, 0:3, 0:3, :] = top[:, 128:256].reshape(3, 16, 128)[:, 13:16]
        pad[g, 0:3, 19:22, :] = top[:, 256:384].reshape(3, 16, 128)[:, 0:3]
        pad[g, 19:22, 3:19, :] = bottom[:, 0:128].reshape(3, 16, 128)
        pad[g, 19:22, 0:3, :] = bottom[:, 128:256].reshape(3, 16, 128)[:, 13:16]
        pad[g, 19:22, 19:22, :] = bottom[:, 256:384].reshape(3, 16, 128)[:, 0:3]
        pad[g, 3:19, 0:3, :] = side[:, 0:128].reshape(16, 16, 128)[:, 13:16]
        pad[g, 3:19, 19:22, :] = side[:, 128:256].reshape(16, 16, 128)[:, 0:3]


def convolve(pad, weights, result, flip):
    def group(g, carry):
        for half in range(2):
            total = [None] * TS
            for b in range(7):
                taps = [
                    weights[g, pl.ds((48 - 7 * a - b) if flip else (7 * a + b), 1), :]
                    for a in range(7)
                ]
                taps = [jnp.broadcast_to(t, (8, 128)) for t in taps]
                for r in range(22):
                    value = pad[g, r, pl.ds(b + 8 * half, 8), :]
                    for a in range(7):
                        i = r - a
                        if 0 <= i < TS:
                            term = taps[a] * value
                            total[i] = term if total[i] is None else total[i] + term
            for i in range(TS):
                result[g, i, pl.ds(8 * half, 8), :] = total[i]
        return carry

    lax.fori_loop(0, 3, group, 0)


def rows_of(result):
    return jnp.concatenate([result[g].reshape(PIX, 128) for g in range(3)], axis=1)


def forward_kernel(own, low, high, lookup, weights, conv, pad, result):
    fill_padded(pad, own[...], low[...], high[...], lookup)
    convolve(pad, weights, result, False)
    conv[...] = dot(tile_major(), rows_of(result).astype(BF), NT).astype(BF)


def backward_kernel(
    received, low, high, lookup, weights, features, cotangent, pad_x,
    output, input_grad, kernel_grad, pad, result, gradient, sums,
):
    order = chan_major()
    both = dot(order, received[...])
    output[...] = (features[...].astype(F32) + both[:, :PIX]).astype(BF)
    own = both[:, PIX:].astype(BF)
    low_rows = dot(order, low[...]).astype(BF)
    high_rows = dot(order, high[...]).astype(BF)
    fill_padded(pad, own, low_rows, high_rows, lookup)
    convolve(pad, weights, result, True)
    upstream = dot(eye(PIX), cotangent[...], NT)
    total = (upstream + rows_of(result)).astype(BF)
    input_grad[...] = dot(eye(ROWS), total, NT).astype(BF)
    for g in range(3):
        gradient[g] = pad[g, 3:19, 3:19, :]
    sums[...] = jnp.zeros_like(sums)

    def group(g, carry):
        for b in range(7):
            total = [None] * 7
            for half in range(2):
                grads = [gradient[g, i, pl.ds(8 * half, 8), :] for i in range(TS)]
                for r in range(22):
                    value = pad_x[g, r, pl.ds(b + 8 * half, 8), :]
                    for a in range(7):
                        i = r - a
                        if 0 <= i < TS:
                            term = grads[i] * value
                            total[a] = term if total[a] is None else total[a] + term
            for a in range(7):
                sums[g, pl.ds(7 * a + b, 1), :] = jnp.sum(total[a], axis=0, keepdims=True)
        return carry

    lax.fori_loop(0, 3, group, 0)
    spread = jnp.concatenate([sums[g] for g in range(3)], axis=1)
    member = (iota((32, ROWS), 0) == (iota((32, ROWS), 1) >> 4)).astype(F32)
    kernel_grad[...] = lax.dot_general(
        member, spread, NT, preferred_element_type=F32, precision=lax.Precision.HIGHEST
    )


def pixel_kernel(
    core, columns, upstream_cols, gain, shift, scale, bias,
    weight_in, weight_in_t, weight_out, weight_out_t,
    out, keep, send, mixed_ref,
):
    own = core[0]
    values = columns[...].astype(F32)
    centered = values - jnp.mean(values, axis=0, keepdims=True)
    inv_std = lax.rsqrt(jnp.mean(centered * centered, axis=0, keepdims=True) + 1e-06)
    normed = centered * inv_std
    inputs = (normed * gain[...] + shift[...]).astype(BF)
    upstream = upstream_cols[...].astype(F32)
    mixed_ref[...] = (scale[...] * upstream).astype(BF)
    grad_mixed = mixed_ref[...]
    lane = iota((C, 128), 1)
    small = jnp.zeros((C, 128), F32)
    mixed_out = jnp.zeros((C, PIX), F32)
    grad_inputs = jnp.zeros((C, PIX), F32)
    for k in range(4):
        block = (2 * own + k) if k < 2 else (2 * (1 - own) + k - 2)
        rows = pl.ds(pl.multiple_of(block * C, C), C)
        hidden = dot(weight_in[rows, :], inputs) + bias[rows, :]
        cdf = 0.5 + 0.5 * lax.erf(hidden * 0.7071067811865476)
        activation = (hidden * cdf).astype(BF)
        slope = cdf + hidden * jnp.exp(-0.5 * hidden * hidden) * 0.3989422804014327
        mixed_out = mixed_out + dot(weight_out[:, rows], activation)
        grad_hidden = dot(weight_out_t[rows, :], grad_mixed) * slope
        small = small + jnp.where(
            lane == block, jnp.sum(grad_hidden, axis=1, keepdims=True), 0.0
        )
        hidden_grad = grad_hidden.astype(BF)
        grad_inputs = grad_inputs + dot(weight_in_t[:, rows], hidden_grad)
        part = dot(hidden_grad, inputs, NT).astype(BF)
        target = keep if k < 2 else send
        for s in range(4):
            target[(k % 2) * 4 + s, 0:PART, :] = part[s * PART : (s + 1) * PART]
        for ref, side in ((keep, own), (send, 1 - own)):
            some = mixed_ref[pl.ds(pl.multiple_of(side * 192, 192), 192), :]
            part = dot(some, activation, NT).astype(BF)
            for s in range(2):
                ref[8 + 2 * block + s, 0:PART, :] = part[s * PART : (s + 1) * PART]
    branch = (scale[...] * mixed_out).astype(BF)
    grad_scale = jnp.sum(upstream * mixed_out, axis=1, keepdims=True)
    grad_gain = jnp.sum(grad_inputs * normed, axis=1, keepdims=True)
    grad_shift = jnp.sum(grad_inputs, axis=1, keepdims=True)
    grad_normed = grad_inputs * gain[...]
    grad_conv = (
        grad_normed
        - jnp.mean(grad_normed, axis=0, keepdims=True)
        - normed * jnp.mean(grad_normed * normed, axis=0, keepdims=True)
    ) * inv_std
    out[:, :PIX] = branch
    out[:, PIX:] = grad_conv.astype(BF)
    small = small + jnp.where(lane == 4, grad_gain, 0.0)
    small = small + jnp.where(lane == 5, grad_shift, 0.0)
    small = small + jnp.where(lane == 6, grad_scale, 0.0)
    small_rows = jnp.transpose(small)[0:8]
    high = small_rows.astype(BF).astype(F32)
    extra = jnp.concatenate([high, small_rows - high], axis=0).astype(BF)
    for ref in (keep, send):
        ref[0, PART:, :] = extra
        for j in range(1, 16):
            ref[j, PART:, :] = jnp.zeros((EXTRA, C), BF)


def finish_kernel(factor, core, mine, other, grad_in, grad_out):
    own = core[0]
    for ref, side in ((mine, own), (other, 1 - own)):
        for j in range(8):
            rows = pl.ds(pl.multiple_of(side * 768 + j * PART, PART), PART)
            grad_in[rows, :] = ref[j, 0:PART, :].astype(F32) * factor
        for q in range(4):
            for s in range(2):
                rows = pl.ds(pl.multiple_of(side * 192 + s * PART, PART), PART)
                grad_out[rows, q * C : (q + 1) * C] = (
                    ref[8 + 2 * q + s, 0:PART, :].astype(F32) * factor
                )


def call(body, shapes, scratch, args, name, flops, scalar_first=False):
    vmem = pl.BlockSpec(memory_space=pltpu.VMEM)
    smem = pl.BlockSpec(memory_space=pltpu.SMEM)
    specs = [smem if scalar_first and i == 0 else vmem for i in range(len(args))]
    moved = sum(a.size * a.dtype.itemsize for a in args)
    moved += sum(math.prod(s) * jnp.dtype(d).itemsize for s, d in shapes)
    return pl.pallas_call(
        body,
        out_shape=[jax.ShapeDtypeStruct(s, d) for s, d in shapes],
        in_specs=specs,
        out_specs=[vmem] * len(shapes),
        scratch_shapes=[pltpu.VMEM(s, d) for s, d in scratch],
        compiler_params=pltpu.CompilerParams(vmem_limit_bytes=VMEM_LIMIT),
        cost_estimate=pl.CostEstimate(flops=flops, bytes_accessed=moved, transcendentals=0),
        name=name,
    )(*args)


def shifted(field):
    count = lax.axis_size("region")
    forward = [(i, i + 1) for i in range(count - 1)]
    backward = [(i + 1, i) for i in range(count - 1)]
    return lax.ppermute(field, "region", forward), lax.ppermute(field, "region", backward)


def cube_pairs(count, bit):
    ring = count // 2
    label = [z ^ (z >> 1) for z in range(ring)]
    place = {g: z for z, g in enumerate(label)}
    return [(2 * z + c, 2 * place[label[z] ^ bit] + c) for z in range(ring) for c in range(2)]


def per_device(
    features, cotangent, neighbours, kernel, norm_gain, norm_shift,
    weight_in, bias_in, weight_out, layer_scale,
):
    count = lax.axis_size("region")
    peers = lax.axis_size("chan")
    region = lax.axis_index("region")
    core = (region & 1).astype(jnp.int32).reshape(1)
    total_tiles = TILE * count
    factor = 1.0 / math.sqrt(total_tiles * PIX)
    swap = [(i, i ^ 1) for i in range(count)]

    x = features.reshape(ROWS, PIX)
    upstream = cotangent.reshape(ROWS, PIX)
    x_low, x_high = shifted(x)
    first_tile = (region - 1) * TILE
    lookup = jnp.where(neighbours >= total_tiles, 3 * TILE, neighbours - first_tile)
    lookup = jnp.tile(lookup, (1, 8))
    weights = jnp.repeat(kernel.reshape(3, 8, 49).transpose(0, 2, 1), TILE, axis=2)
    upstream_cols = lax.all_to_all(
        cotangent, "chan", split_axis=1, concat_axis=0, tiled=True
    ).reshape(C, PIX)

    conv, pad_x = call(
        forward_kernel,
        [((ROWS, PIX), BF), ((3, 22, 24, 128), F32)],
        [((3, 16, 16, 128), F32)],
        (x, x_low, x_high, lookup, weights),
        "forward_conv",
        400_000_000,
    )
    columns = lax.all_to_all(conv, "chan", split_axis=0, concat_axis=0, tiled=True)

    out, keep, send = call(
        pixel_kernel,
        [((C, 2 * PIX), BF), ((16, PART + EXTRA, C), BF), ((16, PART + EXTRA, C), BF)],
        [((C, PIX), BF)],
        (
            core, columns, upstream_cols,
            norm_gain.reshape(C, 1), norm_shift.reshape(C, 1), layer_scale.reshape(C, 1),
            bias_in.reshape(HID, 1),
            weight_in, weight_in.T, weight_out, weight_out.T,
        ),
        "pixel_block",
        2_000_000_000,
        True,
    )
    partner = lax.ppermute(send, "region", swap)
    received = lax.all_to_all(out, "chan", split_axis=0, concat_axis=0, tiled=True)
    half = (keep.astype(F32) + partner.astype(F32)).astype(BF)
    half = lax.all_to_all(half, "chan", split_axis=0, concat_axis=0, tiled=True)
    half = jnp.sum(half.astype(F32), axis=0)

    grad_low, grad_high = shifted(received[:, PIX:])
    output, input_grad, kernel_part = call(
        backward_kernel,
        [((ROWS, PIX), BF), ((ROWS, PIX), BF), ((32, 64), F32)],
        [
            ((3, 22, 24, 128), F32),
            ((3, 16, 16, 128), F32),
            ((3, 16, 16, 128), F32),
            ((3, 64, 128), F32),
        ],
        (received, grad_low, grad_high, lookup, weights, x, upstream, pad_x),
        "backward_conv",
        800_000_000,
    )

    def split(value):
        high = value.astype(BF)
        return high, (value - high.astype(F32)).astype(BF)

    high, low = split(kernel_part)
    pair = jnp.concatenate([high, low], axis=1)
    other = lax.ppermute(pair, "region", swap)
    joined = pair.astype(F32) + other.astype(F32)
    kernel_part = joined[:, :64] + joined[:, 64:]

    for bit in (1, 2, 4):
        high, low = split(kernel_part)
        tail = jnp.concatenate([high, low, jnp.zeros((32, C - 128), BF)], axis=1)
        sent = jnp.concatenate([half.astype(BF), tail], axis=0)
        got = lax.ppermute(sent, "region", cube_pairs(count, bit))
        joined = sent.astype(F32) + got.astype(F32)
        half = joined[: PART + EXTRA]
        kernel_part = joined[PART + EXTRA :, :64] + joined[PART + EXTRA :, 64:128]

    mine = jnp.broadcast_to(half.astype(BF)[None], (peers, PART + EXTRA, C))
    mine = lax.all_to_all(mine, "chan", split_axis=0, concat_axis=0, tiled=True)
    other = lax.ppermute(mine, "region", swap)
    grad_weight_in, grad_weight_out = call(
        lambda *refs: finish_kernel(factor, *refs),
        [((HID, C), F32), ((C, HID), F32)],
        [],
        (core, mine, other),
        "finish",
        2_000_000,
        True,
    )
    small = (mine[0, PART : PART + 8].astype(F32) + mine[0, PART + 8 :].astype(F32)) * factor
    return (
        output.reshape(features.shape),
        input_grad.reshape(features.shape),
        grad_weight_in,
        grad_weight_out,
        small[0:4].reshape(HID),
        small[4],
        small[5],
        small[6],
        kernel_part[:CH, :49] * factor,
    )


def solution(mesh):
    block = P("chan", "region", None)
    in_specs = (block, block, P(None, "region"), P("chan", None)) + (P(),) * 6
    out_specs = (block, block) + (P(),) * 6 + (P("chan", None),)
    return jax.shard_map(
        per_device, mesh=mesh, in_specs=in_specs, out_specs=out_specs, check_vma=False
    )
```

profile of v0, /device:TPU:1, one launch (start us, length us, event | category | flops | bytes accessed | tf_op | source)
XLA Modules:
  0.0 143.9 jit_solution(12706984865470231150)
XLA Ops:
  0.7 5.1 %collective-permute-start = (bf16[384,256]{1,0:T(8,128)(2,1)}, bf16[384,256]{1,0:T(8,128)(2,1)S(1)}, u32[]{:S(2)}, u32[]{:S(2)}) collective-permute-start(bf16[384,256]{1,0:T(8,128)(2,1)} %bitcast.26), channel_id=1, source_target_pairs={{0,16},{16,32},{32,48},{48,64},{64,80},{80,96},{96,112},{112,128},... | collective-permute-start | bytes 589832 | tf_op jit(solution)/shard_map/ppermute | solution.py:264
  5.7 1.9 %collective-permute-start.1 = (bf16[384,256]{1,0:T(8,128)(2,1)}, bf16[384,256]{1,0:T(8,128)(2,1)S(1)}, u32[]{:S(2)}, u32[]{:S(2)}) collective-permute-start(bf16[384,256]{1,0:T(8,128)(2,1)} %bitcast.27), channel_id=1, source_target_pairs={{16,0},{32,16},{48,32},{64,48},{80,64},{96,80},{112,96},{128,112},... | collective-permute-start | bytes 589832 | tf_op jit(solution)/shard_map/ppermute | solution.py:264
  7.7 1.7 %copy.33 = bf16[24,16,256]{2,0,1:T(8,128)(2,1)} copy(bf16[24,16,256]{2,1,0:T(8,128)(2,1)} %param.11) | data formatting | bytes 393216 | tf_op args[1]
  9.3 6.9 %all-to-all-start.1 = ((bf16[24,16,256]{2,0,1:T(8,128)(2,1)}), bf16[24,16,256]{2,0,1:T(8,128)(2,1)S(1)}, u32[]{:S(2)}, u32[]{:S(2)}) async-start(bf16[24,16,256]{2,0,1:T(8,128)(2,1)} %copy.33), calls=%async_computation.1 | async-start | bytes 393216 | tf_op jit(solution)/shard_map/all_to_all | solution.py:293
  16.2 0.7 subtract_select_fusion
  17.0 0.7 broadcast_in_dim.14
  17.9 3.8 %forward_conv.1 = (bf16[384,256]{1,0:T(8,128)(2,1)}, f32[3,22,24,128]{3,2,1,0:T(8,128)S(1)}) custom-call(bf16[384,256]{1,0:T(8,128)(2,1)S(1)} %bitcast.28, bf16[384,256]{1,0:T(8,128)(2,1)S(1)} %collective-permute-done.low, bf16[384,256]{1,0:T(8,128)(2,1)S(1)} %collective-permute-done.1.high, s32[8,128]{1,0:T(8,128)S(1)} %tile.10.lookup, ...), custom_call_target="tpu_custom_call" | custom-call | flops 400000000 | bytes 1676800 | tf_op jit(solution)/shard_map/forward_conv/pallas_call | solution.py:248
  21.7 0.9 copy-done.14
  22.6 0.7 all-to-all-done.1
  23.2 0.7 copy-done.5
  23.9 6.2 %all-to-all-start = ((bf16[16,24,256]{2,1,0:T(8,128)(2,1)}), bf16[16,24,256]{2,1,0:T(8,128)(2,1)}, u32[]{:S(2)}, u32[]{:S(2)}) async-start(bf16[16,24,256]{2,1,0:T(8,128)(2,1)} %bitcast.5), calls=%async_computation | async-start | bytes 393216 | tf_op jit(solution)/shard_map/all_to_all | solution.py:305
  30.1 0.6 copy.34
  30.8 1.5 %copy.35 = bf16[384,1536]{0,1:T(8,128)(2,1)} copy(bf16[384,1536]{1,0:T(8,128)(2,1)S(1)} %copy-done.1) | data formatting | bytes 2359296 | tf_op args[8]
  32.3 1.1 reshape.96.bias
  33.4 0.8 reshape.93.gain
  34.2 1.5 %reshape.94.shift = f32[384,1]{1,0:T(8,128)} reshape(f32[384]{0:T(512)} %param.15) | data formatting | bytes 3072 | tf_op jit(solution)/shard_map/reshape | solution.py:313
  35.7 1.5 %reshape.95.scale = f32[384,1]{1,0:T(8,128)} reshape(f32[384]{0:T(512)} %param.19) | data formatting | bytes 3072 | tf_op jit(solution)/shard_map/reshape | solution.py:313
  37.2 0.1 all-to-all-done
  37.3 1.1 copy-done.2
  38.4 0.9 copy-done.6
  39.3 0.9 copy-done.7
  40.3 0.9 copy-done.8
  41.2 0.9 copy-done.9
  42.1 6.5 %pixel_block.1 = (bf16[384,512]{1,0:T(8,128)(2,1)S(1)}, bf16[16,112,384]{2,1,0:T(8,128)(2,1)}, bf16[16,112,384]{2,1,0:T(8,128)(2,1)}) custom-call(s32[1]{0:T(128)} %bitcast.core.refs_0_, bf16[384,256]{1,0:T(8,128)(2,1)} %bitcast.6.columns, bf16[384,256]{1,0:T(8,128)(2,1)S(1)} %bitcast.25, f32[384,1]{1,0:T(8,128)S(1)} %copy-done.7, f32[384,1]{1,0:T(8,128)S(1)} %copy-done.8, ...), custom_call_target="tpu_custom_call" | custom-call | flops 2000000000 | bytes 8268292 | tf_op jit(solution)/shard_map/pixel_block/pallas_call | solution.py:248
  48.6 0.7 copy-done.3
  49.3 6.5 %all-to-all-start.2 = ((bf16[16,24,512]{2,1,0:T(8,128)(2,1)}), bf16[16,24,512]{2,1,0:T(8,128)(2,1)S(1)}, u32[]{:S(2)}, u32[]{:S(2)}) async-start(bf16[16,24,512]{2,1,0:T(8,128)(2,1)} %bitcast.23), calls=%async_computation.2 | async-start | bytes 786432 | tf_op jit(solution)/shard_map/all_to_all | solution.py:322
  55.8 2.8 %add_convert_fusion = bf16[16,112,384]{2,1,0:T(8,128)(2,1)} fusion(bf16[16,112,384]{2,1,0:T(8,128)(2,1)S(1)} %collective-permute-done.4, bf16[16,112,384]{2,1,0:T(8,128)(2,1)} %get-tuple-element.24), kind=kLoop, calls=%fused_computation | loop fusion | flops 2752512 | bytes 4128768 | tf_op jit(solution)/shard_map/convert_element_type | solution.py:323
  58.6 5.4 %all-to-all-done.2 = bf16[16,24,512]{2,1,0:T(8,128)(2,1)S(1)} async-done(((bf16[16,24,512]{2,1,0:T(8,128)(2,1)}), bf16[16,24,512]{2,1,0:T(8,128)(2,1)S(1)}, u32[]{:S(2)}, u32[]{:S(2)}) %all-to-all-start.2) | async-done | bytes 393248 | tf_op jit(solution)/shard_map/all_to_all | solution.py:322
  64.1 4.3 %all-to-all-start.3 = ((bf16[16,112,384]{2,1,0:T(8,128)(2,1)}), bf16[16,112,384]{2,1,0:T(8,128)(2,1)S(1)}, u32[]{:S(2)}, u32[]{:S(2)}) async-start(bf16[16,112,384]{2,1,0:T(8,128)(2,1)} %add_convert_fusion), calls=%async_computation.3 | async-start | bytes 2752512 | tf_op jit(solution)/shard_map/all_to_all | solution.py:324
  68.4 6.7 %collective-permute-start.2 = (bf16[384,256]{1,0:T(8,128)(2,1)S(1)}, bf16[384,256]{1,0:T(8,128)(2,1)S(1)}, u32[]{:S(2)}, u32[]{:S(2)}) collective-permute-start(bf16[384,256]{1,0:T(8,128)(2,1)S(1)} %slice.83), channel_id=1, source_target_pairs={{0,16},{16,32},{32,48},{48,64},{64,80},{80,96},{96,112},{112,128},... | collective-permute-start | bytes 589832 | tf_op jit(solution)/shard_map/ppermute | solution.py:264
  75.1 1.9 %collective-permute-start.3 = (bf16[384,256]{1,0:T(8,128)(2,1)S(1)}, bf16[384,256]{1,0:T(8,128)(2,1)S(1)}, u32[]{:S(2)}, u32[]{:S(2)}) collective-permute-start(bf16[384,256]{1,0:T(8,128)(2,1)S(1)} %slice.83), channel_id=1, source_target_pairs={{16,0},{32,16},{48,32},{64,48},{80,64},{96,80},{112,96},{128,112},... | collective-permute-start | bytes 589832 | tf_op jit(solution)/shard_map/ppermute | solution.py:264
  77.0 0.7 collective-permute-done.2.low
  77.7 4.7 %collective-permute-done.3.high = bf16[384,256]{1,0:T(8,128)(2,1)S(1)} collective-permute-done((bf16[384,256]{1,0:T(8,128)(2,1)S(1)}, bf16[384,256]{1,0:T(8,128)(2,1)S(1)}, u32[]{:S(2)}, u32[]{:S(2)}) %collective-permute-start.3) | collective-permute-done | bytes 196640 | tf_op jit(solution)/shard_map/ppermute | solution.py:264
  82.4 5.6 %backward_conv.1 = (bf16[384,256]{1,0:T(8,128)(2,1)}, bf16[384,256]{1,0:T(8,128)(2,1)}, f32[32,64]{1,0:T(8,128)S(1)}) custom-call(bf16[384,512]{1,0:T(8,128)(2,1)S(1)} %bitcast.22, bf16[384,256]{1,0:T(8,128)(2,1)S(1)} %collective-permute-done.2.low, bf16[384,256]{1,0:T(8,128)(2,1)S(1)} %collective-permute-done.3.high, s32[8,128]{1,0:T(8,128)S(1)} %tile.10.lookup, ...), custom_call_target="tpu_custom_call" | custom-call | flops 800000000 | bytes 2471424 | tf_op jit(solution)/shard_map/backward_conv/pallas_call | solution.py:248
  88.1 1.2 collective-permute-done.5
  89.5 0.2 reduce_sum.12
  89.7 1.9 %collective-permute-start.6 = (bf16[144,384]{1,0:T(8,128)(2,1)S(1)}, bf16[144,384]{1,0:T(8,128)(2,1)S(1)}, u32[]{:S(2)}, u32[]{:S(2)}) collective-permute-start(bf16[144,384]{1,0:T(8,128)(2,1)S(1)} %fusion), channel_id=1, source_target_pairs={{0,32},{16,48},{32,0},{48,16},{64,96},{80,112},{96,64},{112,80},{1... | collective-permute-start | bytes 331784 | tf_op jit(solution)/shard_map/ppermute | solution.py:356
  91.6 2.1 %collective-permute-done.6 = bf16[144,384]{1,0:T(8,128)(2,1)S(1)} collective-permute-done((bf16[144,384]{1,0:T(8,128)(2,1)S(1)}, bf16[144,384]{1,0:T(8,128)(2,1)S(1)}, u32[]{:S(2)}, u32[]{:S(2)}) %collective-permute-start.6) | collective-permute-done | bytes 110624 | tf_op jit(solution)/shard_map/ppermute | solution.py:356
  94.0 8.7 %collective-permute-start.7 = (bf16[144,384]{1,0:T(8,128)(2,1)S(1)}, bf16[144,384]{1,0:T(8,128)(2,1)S(1)}, u32[]{:S(2)}, u32[]{:S(2)}) collective-permute-start(bf16[144,384]{1,0:T(8,128)(2,1)S(1)} %fusion.1), channel_id=1, source_target_pairs={{0,96},{16,112},{32,64},{48,80},{64,32},{80,48},{96,0},{112,16},{1... | collective-permute-start | bytes 331784 | tf_op jit(solution)/shard_map/ppermute | solution.py:356
  102.7 2.5 %collective-permute-done.7 = bf16[144,384]{1,0:T(8,128)(2,1)S(1)} collective-permute-done((bf16[144,384]{1,0:T(8,128)(2,1)S(1)}, bf16[144,384]{1,0:T(8,128)(2,1)S(1)}, u32[]{:S(2)}, u32[]{:S(2)}) %collective-permute-start.7) | collective-permute-done | bytes 110624 | tf_op jit(solution)/shard_map/ppermute | solution.py:356
  105.6 4.8 %collective-permute-done.8 = bf16[144,384]{1,0:T(8,128)(2,1)S(1)} collective-permute-done((bf16[144,384]{1,0:T(8,128)(2,1)S(1)}, bf16[144,384]{1,0:T(8,128)(2,1)S(1)}, u32[]{:S(2)}, u32[]{:S(2)}) %collective-permute-start.8) | collective-permute-done | bytes 110624 | tf_op jit(solution)/shard_map/ppermute | solution.py:356
  110.6 21.7 %all_to_all.47.refs_1_ = bf16[16,112,384]{2,1,0:T(8,128)(2,1)S(1)} all-to-all(bf16[16,112,384]{2,1,0:T(8,128)(2,1)S(1)} %broadcast_in_dim.15), channel_id=1, replica_groups=mesh['region'=16,'chan'=16] {'chan'}, dimensions={0} | all-to-all | bytes 2752512 | tf_op jit(solution)/shard_map/all_to_all | solution.py:362
  132.3 6.4 %collective-permute-start.9 = (bf16[16,112,384]{2,1,0:T(8,128)(2,1)S(1)}, bf16[16,112,384]{2,1,0:T(8,128)(2,1)S(1)}, u32[]{:S(2)}, u32[]{:S(2)}) collective-permute-start(bf16[16,112,384]{2,1,0:T(8,128)(2,1)S(1)} %all_to_all.47.refs_1_), channel_id=1, source_target_pairs={{0,16},{16,0},{32,48},{48,32},{64,80},{80,64},{96,112},{112,96},{1... | collective-permute-start | bytes 4128776 | tf_op jit(solution)/shard_map/ppermute | solution.py:363
  138.8 0.6 fusion.3
  139.4 0.6 reshape.92
  140.0 0.6 slice_reduce_fusion
  140.6 0.8 collective-permute-done.9.refs_2_
  141.4 2.5 %finish.1 = (f32[1536,384]{1,0:T(8,128)}, f32[384,1536]{1,0:T(8,128)}) custom-call(s32[1]{0:T(128)} %bitcast.core.refs_0_, bf16[16,112,384]{2,1,0:T(8,128)(2,1)S(1)} %all_to_all.47.refs_1_, bf16[16,112,384]{2,1,0:T(8,128)(2,1)S(1)} %collective-permute-done.9.refs_2_), custom_call_target="tpu_custom_call" | custom-call | flops 2000000 | bytes 7471108 | tf_op jit(solution)/shard_map/finish/pallas_call | solution.py:248
  (59 shorter events, 1.5 us)
Async XLA Ops:
  0.6 17.2 %copy-start.12 = (bf16[24,16,256]{2,1,0:T(8,128)(2,1)S(1)}, bf16[24,16,256]{2,1,0:T(8,128)(2,1)}, u32[]{:S(2)}) copy-start(bf16[24,16,256]{2,1,0:T(8,128)(2,1)} %param.10) | copy-start | bytes 589828
  0.7 17.2 %collective-permute-start = (bf16[384,256]{1,0:T(8,128)(2,1)}, bf16[384,256]{1,0:T(8,128)(2,1)S(1)}, u32[]{:S(2)}, u32[]{:S(2)}) collective-permute-start(bf16[384,256]{1,0:T(8,128)(2,1)} %bitcast.26), channel_id=1, source_target_pairs={{0,16},{16,32},{32,48},{48,64},{64,80},{80,96},{96,112},{112,128},... | collective-permute-start | bytes 589832 | tf_op jit(solution)/shard_map/ppermute | solution.py:264
  5.7 12.1 %collective-permute-start.1 = (bf16[384,256]{1,0:T(8,128)(2,1)}, bf16[384,256]{1,0:T(8,128)(2,1)S(1)}, u32[]{:S(2)}, u32[]{:S(2)}) collective-permute-start(bf16[384,256]{1,0:T(8,128)(2,1)} %bitcast.27), channel_id=1, source_target_pairs={{16,0},{32,16},{48,32},{64,48},{80,64},{96,80},{112,96},{128,112},... | collective-permute-start | bytes 589832 | tf_op jit(solution)/shard_map/ppermute | solution.py:264
  9.3 20.8 %copy-start = (bf16[1536,384]{1,0:T(8,128)(2,1)S(1)}, bf16[1536,384]{1,0:T(8,128)(2,1)}, u32[]{:S(2)}) copy-start(bf16[1536,384]{1,0:T(8,128)(2,1)} %weight_in.1) | copy-start | bytes 3538948
  9.3 13.9 %all-to-all-start.1 = ((bf16[24,16,256]{2,0,1:T(8,128)(2,1)}), bf16[24,16,256]{2,0,1:T(8,128)(2,1)S(1)}, u32[]{:S(2)}, u32[]{:S(2)}) async-start(bf16[24,16,256]{2,0,1:T(8,128)(2,1)} %copy.33), calls=%async_computation.1 | async-start | bytes 393216 | tf_op jit(solution)/shard_map/all_to_all | solution.py:293
  17.9 6.1 %copy-start.10 = (f32[3,49,128]{2,1,0:T(8,128)}, f32[3,49,128]{2,1,0:T(8,128)S(1)}, u32[]{:S(2)}) copy-start(f32[3,49,128]{2,1,0:T(8,128)S(1)} %copy.32.weights) | copy-start | bytes 225796
  21.7 0.9 copy-start.14
  23.2 0.7 copy-start.5
  23.9 6.8 %copy-start.1 = (bf16[384,1536]{1,0:T(8,128)(2,1)S(1)}, bf16[384,1536]{1,0:T(8,128)(2,1)}, u32[]{:S(2)}) copy-start(bf16[384,1536]{1,0:T(8,128)(2,1)} %weight_out.1) | copy-start | bytes 3538948
  23.9 13.4 %all-to-all-start = ((bf16[16,24,256]{2,1,0:T(8,128)(2,1)}), bf16[16,24,256]{2,1,0:T(8,128)(2,1)}, u32[]{:S(2)}, u32[]{:S(2)}) async-start(bf16[16,24,256]{2,1,0:T(8,128)(2,1)} %bitcast.5), calls=%async_computation | async-start | bytes 393216 | tf_op jit(solution)/shard_map/all_to_all | solution.py:305
  30.8 1.5 %copy-start.16 = (f32[1536]{0:T(1024)S(1)}, f32[1536]{0:T(1024)}, u32[]{:S(2)}) copy-start(f32[1536]{0:T(1024)} %param.17) | copy-start | bytes 18436
  30.8 2.6 %copy-start.17 = (f32[384]{0:T(512)S(1)}, f32[384]{0:T(512)}, u32[]{:S(2)}) copy-start(f32[384]{0:T(512)} %param.14) | copy-start | bytes 4612
  37.3 1.1 copy-start.2
  38.4 0.9 copy-start.6
  39.3 0.9 copy-start.7
  40.3 0.9 copy-start.8
  41.2 0.9 copy-start.9
  48.6 0.7 copy-start.3
  49.3 6.5 %collective-permute-start.4 = (bf16[16,112,384]{2,1,0:T(8,128)(2,1)}, bf16[16,112,384]{2,1,0:T(8,128)(2,1)S(1)}, u32[]{:S(2)}, u32[]{:S(2)}) collective-permute-start(bf16[16,112,384]{2,1,0:T(8,128)(2,1)} %get-tuple-element.25), channel_id=1, source_target_pairs={{0,16},{16,0},{32,48},{48,32},{64,80},{80,64},{96,112},{112,96},{1... | collective-permute-start | bytes 4128776 | tf_op jit(solution)/shard_map/ppermute | solution.py:321
  49.3 14.8 %all-to-all-start.2 = ((bf16[16,24,512]{2,1,0:T(8,128)(2,1)}), bf16[16,24,512]{2,1,0:T(8,128)(2,1)S(1)}, u32[]{:S(2)}, u32[]{:S(2)}) async-start(bf16[16,24,512]{2,1,0:T(8,128)(2,1)} %bitcast.23), calls=%async_computation.2 | async-start | bytes 786432 | tf_op jit(solution)/shard_map/all_to_all | solution.py:322
  58.6 23.7 %copy-start.4 = (bf16[24,16,256]{2,1,0:T(8,128)(2,1)S(1)}, bf16[24,16,256]{2,1,0:T(8,128)(2,1)}, u32[]{:S(2)}) copy-start(bf16[24,16,256]{2,1,0:T(8,128)(2,1)} %param.11) | copy-start | bytes 589828
  58.6 23.7 %copy-start.11 = (f32[3,49,128]{2,1,0:T(8,128)S(1)}, f32[3,49,128]{2,1,0:T(8,128)}, u32[]{:S(2)}) copy-start(f32[3,49,128]{2,1,0:T(8,128)} %copy-done.10) | copy-start | bytes 225796
  58.6 23.7 %copy-start.13 = (bf16[24,16,256]{2,1,0:T(8,128)(2,1)S(1)}, bf16[24,16,256]{2,1,0:T(8,128)(2,1)}, u32[]{:S(2)}) copy-start(bf16[24,16,256]{2,1,0:T(8,128)(2,1)} %param.10) | copy-start | bytes 589828
  58.6 23.7 %copy-start.15 = (f32[3,22,24,128]{3,2,1,0:T(8,128)S(1)}, f32[3,22,24,128]{3,2,1,0:T(8,128)}, u32[]{:S(2)}) copy-start(f32[3,22,24,128]{3,2,1,0:T(8,128)} %copy-done.14) | copy-start | bytes 2433028
  64.1 25.4 %all-to-all-start.3 = ((bf16[16,112,384]{2,1,0:T(8,128)(2,1)}), bf16[16,112,384]{2,1,0:T(8,128)(2,1)S(1)}, u32[]{:S(2)}, u32[]{:S(2)}) async-start(bf16[16,112,384]{2,1,0:T(8,128)(2,1)} %add_convert_fusion), calls=%async_computation.3 | async-start | bytes 2752512 | tf_op jit(solution)/shard_map/all_to_all | solution.py:324
  68.4 9.3 %collective-permute-start.2 = (bf16[384,256]{1,0:T(8,128)(2,1)S(1)}, bf16[384,256]{1,0:T(8,128)(2,1)S(1)}, u32[]{:S(2)}, u32[]{:S(2)}) collective-permute-start(bf16[384,256]{1,0:T(8,128)(2,1)S(1)} %slice.83), channel_id=1, source_target_pairs={{0,16},{16,32},{32,48},{48,64},{64,80},{80,96},{96,112},{112,128},... | collective-permute-start | bytes 589832 | tf_op jit(solution)/shard_map/ppermute | solution.py:264
  75.1 7.3 %collective-permute-start.3 = (bf16[384,256]{1,0:T(8,128)(2,1)S(1)}, bf16[384,256]{1,0:T(8,128)(2,1)S(1)}, u32[]{:S(2)}, u32[]{:S(2)}) collective-permute-start(bf16[384,256]{1,0:T(8,128)(2,1)S(1)} %slice.83), channel_id=1, source_target_pairs={{16,0},{32,16},{48,32},{64,48},{80,64},{96,80},{112,96},{128,112},... | collective-permute-start | bytes 589832 | tf_op jit(solution)/shard_map/ppermute | solution.py:264
  88.1 1.2 collective-permute-start.5
  89.7 4.0 %collective-permute-start.6 = (bf16[144,384]{1,0:T(8,128)(2,1)S(1)}, bf16[144,384]{1,0:T(8,128)(2,1)S(1)}, u32[]{:S(2)}, u32[]{:S(2)}) collective-permute-start(bf16[144,384]{1,0:T(8,128)(2,1)S(1)} %fusion), channel_id=1, source_target_pairs={{0,32},{16,48},{32,0},{48,16},{64,96},{80,112},{96,64},{112,80},{1... | collective-permute-start | bytes 331784 | tf_op jit(solution)/shard_map/ppermute | solution.py:356
  94.0 11.3 %collective-permute-start.7 = (bf16[144,384]{1,0:T(8,128)(2,1)S(1)}, bf16[144,384]{1,0:T(8,128)(2,1)S(1)}, u32[]{:S(2)}, u32[]{:S(2)}) collective-permute-start(bf16[144,384]{1,0:T(8,128)(2,1)S(1)} %fusion.1), channel_id=1, source_target_pairs={{0,96},{16,112},{32,64},{48,80},{64,32},{80,48},{96,0},{112,16},{1... | collective-permute-start | bytes 331784 | tf_op jit(solution)/shard_map/ppermute | solution.py:356
  105.5 4.8 %collective-permute-start.8 = (bf16[144,384]{1,0:T(8,128)(2,1)S(1)}, bf16[144,384]{1,0:T(8,128)(2,1)S(1)}, u32[]{:S(2)}, u32[]{:S(2)}) collective-permute-start(bf16[144,384]{1,0:T(8,128)(2,1)S(1)} %fusion.2), channel_id=1, source_target_pairs={{0,224},{16,240},{32,192},{48,208},{64,160},{80,176},{96,128},{112... | collective-permute-start | bytes 331784 | tf_op jit(solution)/shard_map/ppermute | solution.py:356
  132.3 9.1 %collective-permute-start.9 = (bf16[16,112,384]{2,1,0:T(8,128)(2,1)S(1)}, bf16[16,112,384]{2,1,0:T(8,128)(2,1)S(1)}, u32[]{:S(2)}, u32[]{:S(2)}) collective-permute-start(bf16[16,112,384]{2,1,0:T(8,128)(2,1)S(1)} %all_to_all.47.refs_1_), channel_id=1, source_target_pairs={{0,16},{16,0},{32,48},{48,32},{64,80},{80,64},{96,112},{112,96},{1... | collective-permute-start | bytes 4128776 | tf_op jit(solution)/shard_map/ppermute | solution.py:363
where the time goes:
time: 146 us; the launch traced here: 144 us
  starting transfers between devices  56.4 us (39%)
  waiting for transfers between devices  23.1 us (16%)
  blocking collectives  21.7 us (15%)
  Pallas kernels  18.3 us (13%)
  local copies, waits for them, and re-layouts  18.2 us (12%)
  other arithmetic  5.2 us (4%)
    all_to_all x1, blocking collectives, per_device(): mine = lax.all_to_all(mine, 'chan', split_axis=0, concat_axis=0, tiled=True)  21.7 us
    pallas_call x4, Pallas kernels, call(): pl.pallas_call(body, out_shape=[jax.ShapeDtypeStruct(s, d) for s, d in sh...  18.3 us
    ppermute x2, starting transfers between devices, shifted(): lax.ppermute(field, 'region', forward)  11.7 us
    unnamed x39, local copies, waits for them, and re-layouts  10.9 us
    ppermute x3, starting transfers between devices, per_device(): got = lax.ppermute(sent, 'region', cube_pairs(count, bit))  10.6 us
    ppermute x3, waiting for transfers between devices, per_device(): got = lax.ppermute(sent, 'region', cube_pairs(count, bit))  9.47 us
    all_to_all x1, starting transfers between devices, per_device(): lax.all_to_all(cotangent, 'chan', split_axis=1, concat_axis=0, tiled=True)  6.89 us
    all_to_all x1, starting transfers between devices, per_device(): lax.all_to_all(out, 'chan', split_axis=0, concat_axis=0, tiled=True)  6.48 us
  transfers between devices with their start and end apart: 14, of which 10 were waited for; matrix products, arithmetic and copies ran while one was open for 11% of the time, Pallas kernels for 7%

commit v1 on v0

v1 whole, which is shorter than its diff:
```python
import functools
import math

import jax
import jax.numpy as jnp
from jax import lax
from jax.experimental import pallas as pl
from jax.experimental.pallas import tpu as pltpu
from jax.sharding import PartitionSpec as P

TS = 16
CH = 24
TILE = 16
PIX = 256
ROWS = CH * TILE
C = 384
HID = 1536
PART = 96
EXTRA = 8
LONG = PART + EXTRA
BRANCH = 32
F32 = jnp.float32
BF = jnp.bfloat16
NT = (((1,), (1,)), ((), ()))
NN = (((1,), (0,)), ((), ()))


def iota(shape, dim):
    return lax.broadcasted_iota(jnp.int32, shape, dim)


def dot(left, right, dims=NN):
    return lax.dot_general(left, right, dims, preferred_element_type=F32)


def eye(n):
    return (iota((n, n), 0) == iota((n, n), 1)).astype(F32).astype(BF)


def tile_major():
    column = iota((ROWS, ROWS), 1)
    target = (column & 15) * CH + (column >> 4)
    return (iota((ROWS, ROWS), 0) == target).astype(F32).astype(BF)


def chan_major():
    row = iota((ROWS, ROWS), 0)
    target = (row & 15) * CH + (row >> 4)
    return (iota((ROWS, ROWS), 1) == target).astype(F32).astype(BF)


def fill_padded(pad, own, low, high, lookup):
    identity = eye(PIX)
    own_t = dot(identity, own, NT)
    own_b = own_t.astype(BF)
    low_b = dot(identity, low, NT).astype(BF)
    high_b = dot(identity, high, NT).astype(BF)
    row = iota((ROWS, 128), 0)
    lane = iota((ROWS, 128), 1)
    key = jnp.where(((row >> 4) & 7) == (lane >> 4), (row >> 7) * 16 + (row & 15), -1)

    def pick(directions):
        parts = [
            (key == lookup[d : d + 1, :]).astype(F32).astype(BF) for d in directions
        ]
        return jnp.concatenate(parts, axis=1)

    north = pick((0, 4, 5))
    south = pick((1, 6, 7))
    sides = pick((2, 3))
    for g in range(3):
        lanes = slice(g * 128, (g + 1) * 128)
        table = jnp.concatenate([low_b[:, lanes], own_b[:, lanes], high_b[:, lanes]], axis=1)
        top = dot(table[208:256], north)
        bottom = dot(table[0:48], south)
        side = dot(table, sides)
        pad[g, 3:19, 3:19, :] = own_t[:, lanes].reshape(16, 16, 128)
        pad[g, 0:3, 3:19, :] = top[:, 0:128].reshape(3, 16, 128)
        pad[g, 0:3, 0:3, :] = top[:, 128:256].reshape(3, 16, 128)[:, 13:16]
        pad[g, 0:3, 19:22, :] = top[:, 256:384].reshape(3, 16, 128)[:, 0:3]
        pad[g, 19:22, 3:19, :] = bottom[:, 0:128].reshape(3, 16, 128)
        pad[g, 19:22, 0:3, :] = bottom[:, 128:256].reshape(3, 16, 128)[:, 13:16]
        pad[g, 19:22, 19:22, :] = bottom[:, 256:384].reshape(3, 16, 128)[:, 0:3]
        pad[g, 3:19, 0:3, :] = side[:, 0:128].reshape(16, 16, 128)[:, 13:16]
        pad[g, 3:19, 19:22, :] = side[:, 128:256].reshape(16, 16, 128)[:, 0:3]


def lookup_rows(region, neighbours, total):
    raw = neighbours[...]
    place = jnp.where(raw >= total, 3 * TILE, raw - (region[0] - 1) * TILE)
    repeat = ((iota((TILE, 128), 1) & 15) == iota((TILE, 128), 0)).astype(F32)
    return dot(place.astype(F32), repeat).astype(jnp.int32)


def spread_taps(kernel, weights):
    member = (iota((CH, ROWS), 0) == (iota((CH, ROWS), 1) >> 4)).astype(F32)
    wide = lax.dot_general(
        kernel[...], member, (((0,), (0,)), ((), ())),
        preferred_element_type=F32, precision=lax.Precision.HIGHEST,
    )
    for g in range(3):
        weights[g] = wide[:, g * 128 : (g + 1) * 128]


def convolve(pad, weights, result, flip):
    def group(g, carry):
        for half in range(2):
            total = [None] * TS
            for b in range(7):
                taps = [
                    weights[g, pl.ds((48 - 7 * a - b) if flip else (7 * a + b), 1), :]
                    for a in range(7)
                ]
                taps = [jnp.broadcast_to(t, (8, 128)) for t in taps]
                for r in range(22):
                    value = pad[g, r, pl.ds(b + 8 * half, 8), :]
                    for a in range(7):
                        i = r - a
                        if 0 <= i < TS:
                            term = taps[a] * value
                            total[i] = term if total[i] is None else total[i] + term
            for i in range(TS):
                result[g, i, pl.ds(8 * half, 8), :] = total[i]
        return carry

    lax.fori_loop(0, 3, group, 0)


def rows_of(result):
    return jnp.concatenate([result[g].reshape(PIX, 128) for g in range(3)], axis=1)


def forward_kernel(
    total, region, own, low, high, neighbours, kernel, cotangent, both, pad_out,
    pad, result, weights, own_ref, low_ref, high_ref, neighbours_ref, kernel_ref,
    cotangent_ref, sems,
):
    pairs = [
        (kernel, kernel_ref), (neighbours, neighbours_ref), (own, own_ref),
        (low, low_ref), (high, high_ref), (cotangent, cotangent_ref),
    ]
    loads = [pltpu.make_async_copy(*pair, sems.at[i]) for i, pair in enumerate(pairs)]
    for load in loads:
        load.start()
    order = tile_major()
    loads[0].wait()
    spread_taps(kernel_ref, weights)
    for load in loads[1:5]:
        load.wait()
    lookup = lookup_rows(region, neighbours_ref, total)
    fill_padded(pad, own_ref[...], low_ref[...], high_ref[...], lookup)
    store = pltpu.make_async_copy(pad, pad_out, sems.at[6])
    store.start()
    convolve(pad, weights, result, False)
    both[:, :PIX] = dot(order, rows_of(result).astype(BF), NT).astype(BF)
    loads[5].wait()
    both[:, PIX:] = dot(order, cotangent_ref[...]).astype(BF)
    store.wait()


def taps_kernel(
    received, features, pad_x, output, grad, kernel_grad, unpacked, gradient, sums
):
    for t in range(TILE):
        part = received[t, 0:BRANCH, :].astype(F32)
        rows = slice(t * CH, (t + 1) * CH)
        unpacked[rows, 0:384] = part[0:CH]
        for i in range(3):
            piece = part[CH:, i * 128 : (i + 1) * 128]
            unpacked[t * CH + 8 * i : t * CH + 8 * (i + 1), 384:512] = piece
    both = dot(chan_major(), unpacked[...].astype(BF))
    output[...] = (features[...].astype(F32) + both[:, :PIX]).astype(BF)
    own_grad = both[:, PIX:].astype(BF)
    grad[...] = own_grad
    own = dot(eye(PIX), own_grad, NT)
    for g in range(3):
        gradient[g] = own[:, g * 128 : (g + 1) * 128].reshape(TS, TS, 128)
    sums[...] = jnp.zeros_like(sums)

    def group(g, carry):
        for b in range(7):
            total = [None] * 7
            for half in range(2):
                grads = [gradient[g, i, pl.ds(8 * half, 8), :] for i in range(TS)]
                for r in range(22):
                    value = pad_x[g, r, pl.ds(b + 8 * half, 8), :]
                    for a in range(7):
                        i = r - a
                        if 0 <= i < TS:
                            term = grads[i] * value
                            total[a] = term if total[a] is None else total[a] + term
            for a in range(7):
                sums[g, pl.ds(7 * a + b, 1), :] = jnp.sum(total[a], axis=0, keepdims=True)
        return carry

    lax.fori_loop(0, 3, group, 0)
    spread = jnp.concatenate([sums[g] for g in range(3)], axis=1)
    member = (iota((32, ROWS), 0) == (iota((32, ROWS), 1) >> 4)).astype(F32)
    total = lax.dot_general(
        member, spread, NT, preferred_element_type=F32, precision=lax.Precision.HIGHEST
    )
    kernel_grad[...] = halves_of(jnp.concatenate([total[8 * i : 8 * i + 8] for i in range(3)], axis=1))


def halves_of(value):
    high = value.astype(BF).astype(F32)
    return jnp.concatenate([high, value - high], axis=1).astype(BF)


def backward_kernel(
    total_tiles, region, own, low, high, neighbours, kernel, cotangent, input_grad,
    pad, result, weights,
):
    spread_taps(kernel, weights)
    lookup = lookup_rows(region, neighbours, total_tiles)
    fill_padded(pad, own[...], low[...], high[...], lookup)
    convolve(pad, weights, result, True)
    upstream = dot(eye(PIX), cotangent[...], NT)
    total = (upstream + rows_of(result)).astype(BF)
    input_grad[...] = dot(eye(ROWS), total, NT).astype(BF)


def normalize(columns):
    values = columns[:, :PIX].astype(F32)
    centered = values - jnp.mean(values, axis=0, keepdims=True)
    inv_std = lax.rsqrt(jnp.mean(centered * centered, axis=0, keepdims=True) + 1e-06)
    return centered * inv_std, inv_std


def hidden_blocks(
    side, table, inputs, grad_mixed, bias, weight_in, weight_in_t, weight_out, weight_out_t,
    parts, mixed_out, grad_inputs, small,
):
    lane = iota((C, 128), 1)
    for q in range(4):
        bias[q * C : (q + 1) * C, :] = table[:, q : q + 1]
    for k in range(2):
        block = 2 * side + k
        rows = pl.ds(pl.multiple_of(block * C, C), C)
        hidden = dot(weight_in[rows, :], inputs) + bias[rows, :]
        cdf = 0.5 + 0.5 * lax.erf(hidden * 0.7071067811865476)
        activation = (hidden * cdf).astype(BF)
        slope = cdf + hidden * jnp.exp(-0.5 * hidden * hidden) * 0.3989422804014327
        mixed_out = mixed_out + dot(weight_out[:, rows], activation)
        grad_hidden = dot(weight_out_t[rows, :], grad_mixed) * slope
        small = small + jnp.where(
            lane == block, jnp.sum(grad_hidden, axis=1, keepdims=True), 0.0
        )
        hidden_grad = grad_hidden.astype(BF)
        grad_inputs = grad_inputs + dot(weight_in_t[:, rows], hidden_grad)
        part = dot(hidden_grad, inputs, NT).astype(BF)
        for s in range(4):
            parts[4 * k + s] = part[s * PART : (s + 1) * PART]
        part = dot(grad_mixed, activation, NT).astype(BF)
        for s in range(4):
            parts[8 + 4 * k + s] = part[s * PART : (s + 1) * PART]
    return mixed_out, grad_inputs, small


def first_half_kernel(
    region, columns, vectors, weight_in, weight_in_t, weight_out, weight_out_t,
    parts, mixed_sum, grad_sum, small_sum, bias, late, sem,
):
    load = pltpu.make_async_copy(weight_out_t, late, sem)
    load.start()
    table = jnp.transpose(vectors[...])
    normed, _ = normalize(columns)
    inputs = (normed * table[:, 4:5] + table[:, 5:6]).astype(BF)
    grad_mixed = (table[:, 6:7] * columns[:, PIX:].astype(F32)).astype(BF)
    zeros = jnp.zeros((C, PIX), F32)
    load.wait()
    mixed_sum[...], grad_sum[...], small_sum[...] = hidden_blocks(
        1 - (region[0] & 1), table, inputs, grad_mixed, bias,
        weight_in, weight_in_t, weight_out, late,
        parts, zeros, zeros, jnp.zeros((C, 128), F32),
    )


def second_half_kernel(
    region, columns, vectors, weight_in, weight_in_t, weight_out, weight_out_t,
    mixed_sum, grad_sum, small_sum, out, parts, extra, bias, late, sem,
):
    load = pltpu.make_async_copy(weight_out_t, late, sem)
    load.start()
    table = jnp.transpose(vectors[...])
    gain = table[:, 4:5]
    scale = table[:, 6:7]
    normed, inv_std = normalize(columns)
    inputs = (normed * gain + table[:, 5:6]).astype(BF)
    upstream = columns[:, PIX:].astype(F32)
    grad_mixed = (scale * upstream).astype(BF)
    load.wait()
    mixed_out, grad_inputs, small = hidden_blocks(
        region[0] & 1, table, inputs, grad_mixed, bias,
        weight_in, weight_in_t, weight_out, late,
        parts, mixed_sum[...], grad_sum[...], small_sum[...],
    )
    branch = scale * mixed_out
    grad_scale = jnp.sum(upstream * mixed_out, axis=1, keepdims=True)
    grad_gain = jnp.sum(grad_inputs * normed, axis=1, keepdims=True)
    grad_shift = jnp.sum(grad_inputs, axis=1, keepdims=True)
    grad_normed = grad_inputs * gain
    grad_conv = (
        grad_normed
        - jnp.mean(grad_normed, axis=0, keepdims=True)
        - normed * jnp.mean(grad_normed * normed, axis=0, keepdims=True)
    ) * inv_std
    for j in range(16):
        rows = slice(j * CH, (j + 1) * CH)
        side = grad_conv[rows, 128:]
        first = jnp.concatenate([branch[rows], grad_conv[rows, :128]], axis=1)
        last = jnp.concatenate([side[8 * i : 8 * i + 8] for i in range(3)], axis=1)
        out[j] = jnp.concatenate([first, last], axis=0).astype(BF)
    lane = iota((C, 128), 1)
    small = small + jnp.where(lane == 4, grad_gain, 0.0)
    small = small + jnp.where(lane == 5, grad_shift, 0.0)
    small = small + jnp.where(lane == 6, grad_scale, 0.0)
    extra[...] = jnp.transpose(small)[0:EXTRA].astype(BF)


def add_kernel(out, first, second, extra, total):
    total[:, 0:BRANCH, :] = out[...]
    total[:, BRANCH : BRANCH + PART, :] = (
        first[...].astype(F32) + second[...].astype(F32)
    ).astype(BF)
    total[0, BRANCH + PART :, :] = extra[...]
    total[1:, BRANCH + PART :, :] = jnp.zeros((15, EXTRA, C), BF)


def first_step_kernel(sent, got, kernel_grad, total):
    total[0:LONG, :] = (sent[...].astype(F32) + got[...].astype(F32)).astype(BF)
    total[LONG:, :] = kernel_grad[...]


def joined(sent, got):
    value = sent[...].astype(F32) + got[...].astype(F32)
    return value[0:LONG].astype(BF), value[LONG:, :192] + value[LONG:, 192:]


def next_step_kernel(sent, got, total):
    weights, taps = joined(sent, got)
    total[0:LONG, :] = weights
    total[LONG:, :] = halves_of(taps)


def spread_kernel(sent, got, total, kernel_grad):
    weights, taps = joined(sent, got)
    kernel_grad[...] = taps
    for j in range(16):
        total[j] = weights


def place(factor, side, ref, grad_in, grad_out, tall, wide, sems):
    half = pl.multiple_of(side * 768, 768)
    for j in range(8):
        tall[j * PART : (j + 1) * PART, :] = ref[j, 0:PART, :].astype(F32) * factor
    first = pltpu.make_async_copy(tall, grad_in.at[pl.ds(half, 768), :], sems.at[0])
    first.start()
    for k in range(2):
        for s in range(4):
            wide[s * PART : (s + 1) * PART, k * C : (k + 1) * C] = (
                ref[8 + 4 * k + s, 0:PART, :].astype(F32) * factor
            )
    second = pltpu.make_async_copy(wide, grad_out.at[:, pl.ds(half, 768)], sems.at[1])
    second.start()
    first.wait()
    second.wait()


def place_own_kernel(factor, region, ref, grad_in, grad_out, tall, wide, sems):
    place(factor, region[0] & 1, ref, grad_in, grad_out, tall, wide, sems)


def place_other_kernel(factor, region, ref, in_a, out_a, grad_in, grad_out, tall, wide, sems):
    place(factor, 1 - (region[0] & 1), ref, grad_in, grad_out, tall, wide, sems)


def call(body, shapes, scratch, args, name, flops, limit, smem=(), far=(), aliases=None):
    spaces = [
        pl.BlockSpec(memory_space=pltpu.SMEM if i in smem else pltpu.HBM if i in far else pltpu.VMEM)
        for i in range(len(args) + len(shapes))
    ]
    moved = sum(a.size * a.dtype.itemsize for a in args)
    moved += sum(math.prod(s) * jnp.dtype(d).itemsize for s, d in shapes)
    return pl.pallas_call(
        body,
        out_shape=[jax.ShapeDtypeStruct(s, d) for s, d in shapes],
        in_specs=spaces[: len(args)],
        out_specs=spaces[len(args) :],
        scratch_shapes=[
            pltpu.SemaphoreType.DMA(s) if d is None else pltpu.VMEM(s, d) for s, d in scratch
        ],
        compiler_params=pltpu.CompilerParams(vmem_limit_bytes=limit * 1024 * 1024),
        cost_estimate=pl.CostEstimate(flops=flops, bytes_accessed=moved, transcendentals=0),
        input_output_aliases=aliases or {},
        name=name,
    )(*args)


def shifted(field):
    count = lax.axis_size("region")
    forward = [(i, i + 1) for i in range(count - 1)]
    backward = [(i + 1, i) for i in range(count - 1)]
    return lax.ppermute(field, "region", forward), lax.ppermute(field, "region", backward)


def cube_pairs(count, bit, core=0):
    ring = count // 2
    label = [z ^ (z >> 1) for z in range(ring)]
    place = {g: z for z, g in enumerate(label)}
    return [
        (2 * z + c, 2 * place[label[z] ^ bit] + (c ^ core)) for z in range(ring) for c in range(2)
    ]


def sum_four(value, first, second, both):
    near, far, across = (lax.ppermute(value, "region", pairs) for pairs in (first, second, both))
    return (value + near) + (far + across)


def per_device(
    features, cotangent, neighbours, kernel, norm_gain, norm_shift,
    weight_in, bias_in, weight_out, layer_scale,
):
    count = lax.axis_size("region")
    peers = lax.axis_size("chan")
    region = lax.axis_index("region").astype(jnp.int32).reshape(1)
    total_tiles = TILE * count
    factor = 1.0 / math.sqrt(total_tiles * PIX)
    swap = [(i, i ^ 1) for i in range(count)]

    x = features.reshape(ROWS, PIX)
    upstream = cotangent.reshape(ROWS, PIX)
    x_low, x_high = shifted(x)
    vectors = jnp.concatenate(
        [
            bias_in.reshape(4, C), norm_gain[None], norm_shift[None], layer_scale[None],
            jnp.zeros((1, C), F32),
        ],
        axis=0,
    )

    padded = ((3, 22, 24, 128), F32)
    square = ((3, 16, 16, 128), F32)
    taps = ((3, 49, 128), F32)
    block = ((ROWS, PIX), BF)
    columns, pad_x = call(
        functools.partial(forward_kernel, total_tiles),
        [((ROWS, 2 * PIX), BF), padded],
        [
            padded, square, taps, block, block, block, ((8, TILE), jnp.int32), ((CH, 49), F32),
            block, ((7,), None),
        ],
        (region, x, x_low, x_high, neighbours, kernel, upstream),
        "forward_conv",
        400_000_000,
        56,
        smem=(0,),
        far=(1, 2, 3, 4, 5, 6, 8),
    )
    columns = lax.all_to_all(columns, "chan", split_axis=0, concat_axis=0, tiled=True)

    halves = (16, PART, C)
    pixels = (region, columns, vectors, weight_in, weight_in.T, weight_out, weight_out.T)
    scratch = [((HID, 1), F32), ((HID, C), BF), ((), None)]
    sums = [((C, PIX), F32), ((C, PIX), F32), ((C, 128), F32)]
    send, *partial = call(
        first_half_kernel,
        [(halves, BF)] + sums,
        scratch,
        pixels,
        "pixels_first",
        1_000_000_000,
        24,
        smem=(0,),
        far=(6,),
    )
    partner = lax.ppermute(send, "region", swap)
    out, keep, extra = call(
        second_half_kernel,
        [((16, BRANCH, C), BF), (halves, BF), ((EXTRA, C), BF)],
        scratch,
        (*pixels, *partial),
        "pixels_second",
        1_000_000_000,
        24,
        smem=(0,),
        far=(6,),
    )
    (travel,) = call(
        add_kernel, [((16, BRANCH + LONG, C), BF)], [], (out, keep, partner, extra),
        "add_cores", 1_000_000, 8,
    )
    travel = lax.all_to_all(travel, "chan", split_axis=0, concat_axis=0, tiled=True)

    sent = jnp.sum(travel[:, BRANCH:].astype(F32), axis=0).astype(BF)
    got = lax.ppermute(sent, "region", cube_pairs(count, 1))
    output, grad, kernel_part = call(
        taps_kernel,
        [((ROWS, PIX), BF), ((ROWS, PIX), BF), ((8, C), BF)],
        [((ROWS, 2 * PIX), F32), square, ((3, 64, 128), F32)],
        (travel, x, pad_x),
        "kernel_taps",
        400_000_000,
        16,
    )
    step = [((LONG + 8, C), BF)]
    (sent,) = call(first_step_kernel, step, [], (sent, got, kernel_part), "step", 100_000, 4)
    got = lax.ppermute(sent, "region", cube_pairs(count, 2))
    (sent,) = call(next_step_kernel, step, [], (sent, got), "step", 100_000, 4)
    got = lax.ppermute(sent, "region", cube_pairs(count, 4))
    mine, kernel_part = call(
        spread_kernel, [((peers, LONG, C), BF), ((8, 192), F32)], [], (sent, got),
        "spread", 1_000_000, 8,
    )
    mine = lax.all_to_all(mine, "chan", split_axis=0, concat_axis=0, tiled=True)

    grad_low, grad_high = shifted(grad)
    kernel_part = sum_four(kernel_part, swap, cube_pairs(count, 1), cube_pairs(count, 1, 1))
    kernel_part = kernel_part.reshape(8, 3, 64).transpose(1, 0, 2).reshape(CH, 64)
    kernel_part = kernel_part[:, :49] * factor
    (input_grad,) = call(
        functools.partial(backward_kernel, total_tiles),
        [((ROWS, PIX), BF)],
        [padded, square, taps],
        (region, grad, grad_low, grad_high, neighbours, kernel, upstream),
        "backward_conv",
        400_000_000,
        16,
        smem=(0,),
    )

    mine, kernel_part, input_grad = lax.optimization_barrier((mine, kernel_part, input_grad))
    other = lax.ppermute(mine, "region", swap)
    grads = [((HID, C), F32), ((C, HID), F32)]
    scratch = [((768, C), F32), ((C, 768), F32), ((2,), None)]
    placed = call(
        functools.partial(place_own_kernel, factor),
        grads, scratch, (region, mine), "place_own", 1_000_000, 16, smem=(0,), far=(2, 3),
    )
    grad_weight_in, grad_weight_out = call(
        functools.partial(place_other_kernel, factor),
        grads, scratch, (region, other, *placed), "place_other", 1_000_000, 16,
        smem=(0,), far=(2, 3, 4, 5), aliases={2: 0, 3: 1},
    )

    small = (mine[0, PART:].astype(F32) + other[0, PART:].astype(F32)) * factor
    return (
        output.reshape(features.shape),
        input_grad.reshape(features.shape),
        grad_weight_in,
        grad_weight_out,
        small[0:4].reshape(HID),
        small[4],
        small[5],
        small[6],
        kernel_part,
    )


def solution(mesh):
    block = P("chan", "region", None)
    in_specs = (block, block, P(None, "region"), P("chan", None)) + (P(),) * 6
    out_specs = (block, block) + (P(),) * 6 + (P("chan", None),)
    return jax.shard_map(
        per_device, mesh=mesh, in_specs=in_specs, out_specs=out_specs, check_vma=False
    )
```

time: 146 us -> 118 us (0.81); the launches traced: 144 us -> 118 us
  waiting for transfers between devices: 23.1 us -> 11 us
  local copies, waits for them, and re-layouts: 18.2 us -> 8.38 us
  starting transfers between devices: 56.4 us -> 46.7 us
  Pallas kernels: 18.3 us -> 23.6 us
  blocking collectives: 21.7 us -> 26.4 us
  other arithmetic: 5.2 us -> 0.79 us
    all_to_all x4 -> x2, starting transfers between devices: 23.8 us -> 10.4 us  [the longest x1 6.6 us: per_device(): lax.all_to_all(columns, 'chan', split_axis=0, concat_axis=0, tiled=True)]
    ppermute x2, starting transfers between devices: 11.7 us -> 3.89 us  [shifted(): lax.ppermute(field, 'region', forward)]
    ppermute x2, starting transfers between devices: 3.84 us -> 11.6 us  [shifted(): lax.ppermute(field, 'region', backward)]
    unnamed x39 -> x30, local copies, waits for them, and re-layouts: 10.9 us -> 4.04 us
    ppermute x4 -> x6, waiting for transfers between devices: 10.6 us -> 3.9 us  [the longest x1 1.98 us: per_device(): got = lax.ppermute(sent, 'region', cube_pairs(count, 2))]
    pallas_call x4 -> x11, Pallas kernels: 18.3 us -> 23.6 us  [call(): pl.pallas_call(body, out_shape=[jax.ShapeDtypeStruct(s, d) for s, d in sh...]
    all_to_all x1, blocking collectives: 21.7 us -> 26.4 us  [per_device(): lax.all_to_all(travel, 'chan', split_axis=0, concat_axis=0, tiled=True)]
    ppermute x4 -> x6, starting transfers between devices: 10.7 us -> 15.3 us  [the longest x1 4.9 us: per_device(): got = lax.ppermute(sent, 'region', cube_pairs(count, 2))]
  transfers between devices with their start and end apart: 14 -> 14, of which waited for: 10 -> 6; matrix products, arithmetic and copies ran while one was open for 11% -> 5% of each run, Pallas kernels for 7% -> 10%
where the time goes in v1:
time: 118 us
  starting transfers between devices  46.7 us (40%)
  blocking collectives  26.4 us (22%)
  Pallas kernels  23.6 us (20%)
  waiting for transfers between devices  11 us (9%)
  local copies, waits for them, and re-layouts  8.38 us (7%)
    all_to_all x1, blocking collectives, per_device(): lax.all_to_all(travel, 'chan', split_axis=0, concat_axis=0, tiled=True)  26.4 us
    pallas_call x11, Pallas kernels, call(): pl.pallas_call(body, out_shape=[jax.ShapeDtypeStruct(s, d) for s, d in sh...  23.6 us
    ppermute x2, starting transfers between devices, shifted(): lax.ppermute(field, 'region', backward)  11.6 us
    all_to_all x1, starting transfers between devices, per_device(): lax.all_to_all(columns, 'chan', split_axis=0, concat_axis=0, tiled=True)  6.6 us
    ppermute x1, starting transfers between devices, per_device(): other = lax.ppermute(mine, 'region', swap)  5.34 us
    ppermute x1, starting transfers between devices, per_device(): got = lax.ppermute(sent, 'region', cube_pairs(count, 2))  4.9 us
    ppermute x1, starting transfers between devices, per_device(): got = lax.ppermute(sent, 'region', cube_pairs(count, 1))  4.57 us
    unnamed x30, local copies, waits for them, and re-layouts  4.04 us
  transfers between devices with their start and end apart: 14, of which 6 were waited for; matrix products, arithmetic and copies ran while one was open for 5% of the time, Pallas kernels for 10%

profile of v1, /device:TPU:1, one launch (start us, length us, event | category | flops | bytes accessed | tf_op | source)
XLA Modules:
  0.0 117.8 jit_solution(16407413364186471656)
XLA Ops:
  0.7 5.3 %collective-permute-start.1 = (bf16[384,256]{1,0:T(8,128)(2,1)}, bf16[384,256]{1,0:T(8,128)(2,1)S(1)}, u32[]{:S(2)}, u32[]{:S(2)}) collective-permute-start(bf16[384,256]{1,0:T(8,128)(2,1)} %bitcast.17), channel_id=1, source_target_pairs={{16,0},{32,16},{48,32},{64,48},{80,64},{96,80},{112,96},{128,112},... | collective-permute-start | bytes 589832 | tf_op jit(solution)/shard_map/ppermute | solution.py:404
  6.0 1.9 %collective-permute-start = (bf16[384,256]{1,0:T(8,128)(2,1)}, bf16[384,256]{1,0:T(8,128)(2,1)S(1)}, u32[]{:S(2)}, u32[]{:S(2)}) collective-permute-start(bf16[384,256]{1,0:T(8,128)(2,1)} %bitcast.18), channel_id=1, source_target_pairs={{0,16},{16,32},{32,48},{48,64},{64,80},{80,96},{96,112},{112,128},... | collective-permute-start | bytes 589832 | tf_op jit(solution)/shard_map/ppermute | solution.py:404
  7.9 1.4 %collective-permute-done.1.high = bf16[384,256]{1,0:T(8,128)(2,1)S(1)} collective-permute-done((bf16[384,256]{1,0:T(8,128)(2,1)}, bf16[384,256]{1,0:T(8,128)(2,1)S(1)}, u32[]{:S(2)}, u32[]{:S(2)}) %collective-permute-start.1) | collective-permute-done | bytes 196640 | tf_op jit(solution)/shard_map/ppermute | solution.py:404
  9.3 1.5 %collective-permute-done.low = bf16[384,256]{1,0:T(8,128)(2,1)S(1)} collective-permute-done((bf16[384,256]{1,0:T(8,128)(2,1)}, bf16[384,256]{1,0:T(8,128)(2,1)S(1)}, u32[]{:S(2)}, u32[]{:S(2)}) %collective-permute-start) | collective-permute-done | bytes 196640 | tf_op jit(solution)/shard_map/ppermute | solution.py:404
  10.8 0.7 copy-done.13
  11.5 5.3 %forward_conv.1 = (bf16[384,512]{1,0:T(8,128)(2,1)}, f32[3,22,24,128]{3,2,1,0:T(8,128)}) custom-call(s32[1]{0:T(128)} %bitcast.region, bf16[384,256]{1,0:T(8,128)(2,1)} %bitcast.19, bf16[384,256]{1,0:T(8,128)(2,1)} %copy-done.13, bf16[384,256]{1,0:T(8,128)(2,1)} %copy-done.12, s32[8,16]{1,0:T(8,128)} %neighbours.3, f32[24,49]{1,0:T(8,128)} %kernel.3, ...), custom_call_target="tpu_custom_call" | custom-call | flops 400000000 | bytes 1995876 | tf_op jit(solution)/shard_map/forward_conv/pallas_call | solution.py:385
  16.8 6.6 %all-to-all-start = ((bf16[16,24,512]{2,1,0:T(8,128)(2,1)}), bf16[16,24,512]{2,1,0:T(8,128)(2,1)}, u32[]{:S(2)}, u32[]{:S(2)}) async-start(bf16[16,24,512]{2,1,0:T(8,128)(2,1)} %bitcast.23), calls=%async_computation | async-start | bytes 786432 | tf_op jit(solution)/shard_map/all_to_all | solution.py:461
  23.4 0.0 copy-start.1
  23.5 0.6 broadcast_in_dim.13
  24.0 0.6 broadcast_in_dim.14
  24.6 0.6 reshape.63
  25.2 0.6 copy.26
  25.8 1.4 %copy.27 = bf16[384,1536]{0,1:T(8,128)(2,1)} copy(bf16[384,1536]{1,0:T(8,128)(2,1)S(1)} %copy-done.1) | data formatting | bytes 2359296 | tf_op args[8]
  27.3 0.6 broadcast_in_dim.15
  27.8 0.7 concatenate.3.vectors
  28.6 3.1 %all-to-all-done = bf16[16,24,512]{2,1,0:T(8,128)(2,1)} async-done(((bf16[16,24,512]{2,1,0:T(8,128)(2,1)}), bf16[16,24,512]{2,1,0:T(8,128)(2,1)}, u32[]{:S(2)}, u32[]{:S(2)}) %all-to-all-start) | async-done | bytes 393248 | tf_op jit(solution)/shard_map/all_to_all | solution.py:461
  31.6 1.3 %copy-done.2 = bf16[384,1536]{0,1:T(8,128)(2,1)S(1)} copy-done((bf16[384,1536]{0,1:T(8,128)(2,1)S(1)}, bf16[384,1536]{0,1:T(8,128)(2,1)}, u32[]{:S(2)}) %copy-start.2) | copy-done | bytes 1179672
  32.9 3.6 %pixels_first.1 = (bf16[16,96,384]{2,1,0:T(8,128)(2,1)S(1)}, f32[384,256]{1,0:T(8,128)S(1)}, f32[384,256]{1,0:T(8,128)S(1)}, f32[384,128]{1,0:T(8,128)S(1)}) custom-call(s32[1]{0:T(128)} %bitcast.region, bf16[384,512]{1,0:T(8,128)(2,1)} %bitcast.4.columns, f32[8,384]{1,0:T(8,128)S(1)} %concatenate.3.vectors, bf16[1536,384]{1,0:T(8,128)(2,1)S(1)} %copy-done, ...), custom_call_target="tpu_custom_call" | custom-call | flops 1000000000 | bytes 7286788 | tf_op jit(solution)/shard_map/pixels_first/pallas_call | solution.py:385
  36.5 0.1 collective-permute-start.2
  36.6 3.6 %pixels_second.1 = (bf16[16,32,384]{2,1,0:T(8,128)(2,1)S(1)}, bf16[16,96,384]{2,1,0:T(8,128)(2,1)S(1)}, bf16[8,384]{1,0:T(8,128)(2,1)S(1)}) custom-call(s32[1]{0:T(128)} %bitcast.region, bf16[384,512]{1,0:T(8,128)(2,1)} %bitcast.4.columns, f32[8,384]{1,0:T(8,128)S(1)} %concatenate.3.vectors, bf16[1536,384]{1,0:T(8,128)(2,1)S(1)} %copy-done, ...), custom_call_target="tpu_custom_call" | custom-call | flops 1000000000 | bytes 7686148 | tf_op jit(solution)/shard_map/pixels_second/pallas_call | solution.py:385
  40.2 0.3 add_cores.1
  40.5 26.4 %all_to_all.21.received = bf16[16,136,384]{2,1,0:T(8,128)(2,1)S(1)} all-to-all(bf16[16,136,384]{2,1,0:T(8,128)(2,1)S(1)} %add_cores.1), channel_id=1, replica_groups=mesh['region'=16,'chan'=16] {'chan'}, dimensions={0} | all-to-all | bytes 3342336 | tf_op jit(solution)/shard_map/all_to_all | solution.py:494
  66.9 0.2 slice_reduce_fusion.sent
  67.1 4.6 %collective-permute-start.3 = (bf16[104,384]{1,0:T(8,128)(2,1)S(1)}, bf16[104,384]{1,0:T(8,128)(2,1)S(1)}, u32[]{:S(2)}, u32[]{:S(2)}) collective-permute-start(bf16[104,384]{1,0:T(8,128)(2,1)S(1)} %slice_reduce_fusion.sent), channel_id=1, source_target_pairs={{0,32},{16,48},{32,0},{48,16},{64,96},{80,112},{96,64},{112,80},{1... | collective-permute-start | bytes 239624 | tf_op jit(solution)/shard_map/ppermute | solution.py:497
  71.7 2.4 %kernel_taps.1 = (bf16[384,256]{1,0:T(8,128)(2,1)}, bf16[384,256]{1,0:T(8,128)(2,1)S(1)}, bf16[8,384]{1,0:T(8,128)(2,1)S(1)}) custom-call(bf16[16,136,384]{2,1,0:T(8,128)(2,1)S(1)} %all_to_all.21.received, bf16[384,256]{1,0:T(8,128)(2,1)S(1)} %bitcast.20, f32[3,22,24,128]{3,2,1,0:T(8,128)S(1)} %copy-done.3), custom_call_target="tpu_custom_call" | custom-call | flops 400000000 | bytes 3078144 | tf_op jit(solution)/shard_map/kernel_taps/pallas_call | solution.py:385
  74.1 0.0 collective-permute-done.3.got
  74.1 4.9 %collective-permute-start.4 = (bf16[112,384]{1,0:T(8,128)(2,1)S(1)}, bf16[112,384]{1,0:T(8,128)(2,1)S(1)}, u32[]{:S(2)}, u32[]{:S(2)}) collective-permute-start(bf16[112,384]{1,0:T(8,128)(2,1)S(1)} %step.2.sent), channel_id=1, source_target_pairs={{0,96},{16,112},{32,64},{48,80},{64,32},{80,48},{96,0},{112,16},{1... | collective-permute-start | bytes 258056 | tf_op jit(solution)/shard_map/ppermute | solution.py:509
  79.0 2.0 %collective-permute-done.4.got = bf16[112,384]{1,0:T(8,128)(2,1)S(1)} collective-permute-done((bf16[112,384]{1,0:T(8,128)(2,1)S(1)}, bf16[112,384]{1,0:T(8,128)(2,1)S(1)}, u32[]{:S(2)}, u32[]{:S(2)}) %collective-permute-start.4) | collective-permute-done | bytes 86048 | tf_op jit(solution)/shard_map/ppermute | solution.py:509
  81.0 0.1 step.3.sent
  81.1 3.1 %collective-permute-start.5 = (bf16[112,384]{1,0:T(8,128)(2,1)S(1)}, bf16[112,384]{1,0:T(8,128)(2,1)S(1)}, u32[]{:S(2)}, u32[]{:S(2)}) collective-permute-start(bf16[112,384]{1,0:T(8,128)(2,1)S(1)} %step.3.sent), channel_id=1, source_target_pairs={{0,224},{16,240},{32,192},{48,208},{64,160},{80,176},{96,128},{112... | collective-permute-start | bytes 258056 | tf_op jit(solution)/shard_map/ppermute | solution.py:511
  84.2 1.9 %collective-permute-done.5.got = bf16[112,384]{1,0:T(8,128)(2,1)S(1)} collective-permute-done((bf16[112,384]{1,0:T(8,128)(2,1)S(1)}, bf16[112,384]{1,0:T(8,128)(2,1)S(1)}, u32[]{:S(2)}, u32[]{:S(2)}) %collective-permute-start.5) | collective-permute-done | bytes 86048 | tf_op jit(solution)/shard_map/ppermute | solution.py:511
  86.2 1.2 spread.1
  87.3 3.8 %all-to-all-start.2 = ((bf16[16,104,384]{2,1,0:T(8,128)(2,1)}), bf16[16,104,384]{2,1,0:T(8,128)(2,1)S(1)}, u32[]{:S(2)}, u32[]{:S(2)}) async-start(bf16[16,104,384]{2,1,0:T(8,128)(2,1)} %get-tuple-element.41), calls=%async_computation.2 | async-start | bytes 2555904 | tf_op jit(solution)/shard_map/all_to_all | solution.py:516
  91.2 6.4 %collective-permute-start.10 = (bf16[384,256]{1,0:T(8,128)(2,1)S(1)}, bf16[384,256]{1,0:T(8,128)(2,1)S(1)}, u32[]{:S(2)}, u32[]{:S(2)}) collective-permute-start(bf16[384,256]{1,0:T(8,128)(2,1)S(1)} %get-tuple-element.43.own), channel_id=1, source_target_pairs={{16,0},{32,16},{48,32},{64,48},{80,64},{96,80},{112,96},{128,112},... | collective-permute-start | bytes 589832 | tf_op jit(solution)/shard_map/ppermute | solution.py:404
  97.5 2.0 %collective-permute-start.9 = (bf16[384,256]{1,0:T(8,128)(2,1)S(1)}, bf16[384,256]{1,0:T(8,128)(2,1)S(1)}, u32[]{:S(2)}, u32[]{:S(2)}) collective-permute-start(bf16[384,256]{1,0:T(8,128)(2,1)S(1)} %get-tuple-element.43.own), channel_id=1, source_target_pairs={{0,16},{16,32},{32,48},{48,64},{64,80},{80,96},{96,112},{112,128},... | collective-permute-start | bytes 589832 | tf_op jit(solution)/shard_map/ppermute | solution.py:404
  99.5 0.8 collective-permute-start.8
  100.3 1.7 %collective-permute-start.7 = (f32[8,192]{1,0:T(8,128)S(1)}, f32[8,192]{1,0:T(8,128)S(1)}, u32[]{:S(2)}, u32[]{:S(2)}) collective-permute-start(f32[8,192]{1,0:T(8,128)S(1)} %get-tuple-element.42), channel_id=1, source_target_pairs={{0,32},{16,48},{32,0},{48,16},{64,96},{80,112},{96,64},{112,80},{1... | collective-permute-start | bytes 18440 | tf_op jit(solution)/shard_map/ppermute | solution.py:417
  101.9 0.3 collective-permute-start.6
  102.2 0.0 collective-permute-done.10.high
  102.3 4.0 %backward_conv.1 = bf16[384,256]{1,0:T(8,128)(2,1)} custom-call(s32[1]{0:T(128)} %bitcast.region, bf16[384,256]{1,0:T(8,128)(2,1)S(1)} %get-tuple-element.43.own, bf16[384,256]{1,0:T(8,128)(2,1)S(1)} %collective-permute-done.9.low, bf16[384,256]{1,0:T(8,128)(2,1)S(1)} %collective-permute-done.10.high, s32[8,16]{1,0:T(8,128)S(1)} %copy-done.7, ...), custom_call_target="tpu_custom_call" | custom-call | flops 400000000 | bytes 988260 | tf_op jit(solution)/shard_map/backward_conv/pallas_call | solution.py:385
  106.3 0.1 reshape.65
  106.4 0.6 slice_multiply_fusion
  107.0 5.3 %collective-permute-start.11 = (bf16[16,104,384]{2,1,0:T(8,128)(2,1)S(1)}, bf16[16,104,384]{2,1,0:T(8,128)(2,1)S(1)}, u32[]{:S(2)}, u32[]{:S(2)}) collective-permute-start(bf16[16,104,384]{2,1,0:T(8,128)(2,1)S(1)} %all-to-all-done.2.ref), channel_id=1, source_target_pairs={{0,16},{16,0},{32,48},{48,32},{64,80},{80,64},{96,112},{112,96},{1... | collective-permute-start | bytes 3833864 | tf_op jit(solution)/shard_map/ppermute | solution.py:534
  112.3 1.5 %place_own.1 = (f32[1536,384]{1,0:T(8,128)}, f32[384,1536]{1,0:T(8,128)}) custom-call(s32[1]{0:T(128)} %bitcast.region, bf16[16,104,384]{2,1,0:T(8,128)(2,1)S(1)} %all-to-all-done.2.ref), custom_call_target="tpu_custom_call" | custom-call | flops 1000000 | bytes 5996548 | tf_op jit(solution)/shard_map/place_own/pallas_call | solution.py:385
  113.8 1.1 collective-permute-done.11.ref
  114.9 0.6 slice_reduce_fusion.1
  115.6 0.6 reshape.68
  116.2 1.5 %place_other.1 = (f32[1536,384]{1,0:T(8,128)}, f32[384,1536]{1,0:T(8,128)}) custom-call(s32[1]{0:T(128)} %bitcast.region, bf16[16,104,384]{2,1,0:T(8,128)(2,1)S(1)} %collective-permute-done.11.ref, f32[1536,384]{1,0:T(8,128)} %get-tuple-element.46.in_a, f32[384,1536]{1,0:T(8,128)} %get-tuple-element.47.out_a), custom_call_target="tpu_custom_call", output_to_operand_aliasing={{0}: (2, {}), {1}: (3, {})} | custom-call | flops 1000000 | bytes 10715140 | tf_op jit(solution)/shard_map/place_other/pallas_call | solution.py:385
  (37 shorter events, 0.1 us)
Async XLA Ops:
  0.6 22.8 %copy-start.9 = (f32[384]{0:T(512)S(1)}, f32[384]{0:T(512)}, u32[]{:S(2)}) copy-start(f32[384]{0:T(512)} %param.14) | copy-start | bytes 4612
  0.7 22.8 %copy-start.10 = (f32[384]{0:T(512)S(1)}, f32[384]{0:T(512)}, u32[]{:S(2)}) copy-start(f32[384]{0:T(512)} %param.15) | copy-start | bytes 4612
  0.7 23.4 %copy-start.11 = (f32[384]{0:T(512)S(1)}, f32[384]{0:T(512)}, u32[]{:S(2)}) copy-start(f32[384]{0:T(512)} %param.19) | copy-start | bytes 4612
  0.7 23.9 %copy-start.8 = (f32[1536]{0:T(1024)S(1)}, f32[1536]{0:T(1024)}, u32[]{:S(2)}) copy-start(f32[1536]{0:T(1024)} %param.17) | copy-start | bytes 18436
  0.7 24.5 %copy-start = (bf16[1536,384]{1,0:T(8,128)(2,1)S(1)}, bf16[1536,384]{1,0:T(8,128)(2,1)}, u32[]{:S(2)}) copy-start(bf16[1536,384]{1,0:T(8,128)(2,1)} %weight_in.3) | copy-start | bytes 3538948
  0.7 8.6 %collective-permute-start.1 = (bf16[384,256]{1,0:T(8,128)(2,1)}, bf16[384,256]{1,0:T(8,128)(2,1)S(1)}, u32[]{:S(2)}, u32[]{:S(2)}) collective-permute-start(bf16[384,256]{1,0:T(8,128)(2,1)} %bitcast.17), channel_id=1, source_target_pairs={{16,0},{32,16},{48,32},{64,48},{80,64},{96,80},{112,96},{128,112},... | collective-permute-start | bytes 589832 | tf_op jit(solution)/shard_map/ppermute | solution.py:404
  6.0 4.8 %collective-permute-start = (bf16[384,256]{1,0:T(8,128)(2,1)}, bf16[384,256]{1,0:T(8,128)(2,1)S(1)}, u32[]{:S(2)}, u32[]{:S(2)}) collective-permute-start(bf16[384,256]{1,0:T(8,128)(2,1)} %bitcast.18), channel_id=1, source_target_pairs={{0,16},{16,32},{32,48},{48,64},{64,80},{80,96},{96,112},{112,128},... | collective-permute-start | bytes 589832 | tf_op jit(solution)/shard_map/ppermute | solution.py:404
  9.3 1.5 %copy-start.12 = (bf16[384,256]{1,0:T(8,128)(2,1)}, bf16[384,256]{1,0:T(8,128)(2,1)S(1)}, u32[]{:S(2)}) copy-start(bf16[384,256]{1,0:T(8,128)(2,1)S(1)} %collective-permute-done.1.high) | copy-start | bytes 589828
  10.8 0.7 copy-start.13
  16.8 14.8 %all-to-all-start = ((bf16[16,24,512]{2,1,0:T(8,128)(2,1)}), bf16[16,24,512]{2,1,0:T(8,128)(2,1)}, u32[]{:S(2)}, u32[]{:S(2)}) async-start(bf16[16,24,512]{2,1,0:T(8,128)(2,1)} %bitcast.23), calls=%async_computation | async-start | bytes 786432 | tf_op jit(solution)/shard_map/all_to_all | solution.py:461
  23.4 2.4 %copy-start.1 = (bf16[384,1536]{1,0:T(8,128)(2,1)S(1)}, bf16[384,1536]{1,0:T(8,128)(2,1)}, u32[]{:S(2)}) copy-start(bf16[384,1536]{1,0:T(8,128)(2,1)} %weight_out.3) | copy-start | bytes 3538948
  31.6 1.3 %copy-start.2 = (bf16[384,1536]{0,1:T(8,128)(2,1)S(1)}, bf16[384,1536]{0,1:T(8,128)(2,1)}, u32[]{:S(2)}) copy-start(bf16[384,1536]{0,1:T(8,128)(2,1)} %copy.27) | copy-start | bytes 3538948
  36.5 3.7 %collective-permute-start.2 = (bf16[16,96,384]{2,1,0:T(8,128)(2,1)S(1)}, bf16[16,96,384]{2,1,0:T(8,128)(2,1)S(1)}, u32[]{:S(2)}, u32[]{:S(2)}) collective-permute-start(bf16[16,96,384]{2,1,0:T(8,128)(2,1)S(1)} %get-tuple-element.36), channel_id=1, source_target_pairs={{0,16},{16,0},{32,48},{48,32},{64,80},{80,64},{96,112},{112,96},{1... | collective-permute-start | bytes 3538952 | tf_op jit(solution)/shard_map/ppermute | solution.py:478
  66.9 4.7 %copy-start.3 = (f32[3,22,24,128]{3,2,1,0:T(8,128)S(1)}, f32[3,22,24,128]{3,2,1,0:T(8,128)}, u32[]{:S(2)}) copy-start(f32[3,22,24,128]{3,2,1,0:T(8,128)} %get-tuple-element.38.pad_x) | copy-start | bytes 2433028
  66.9 4.7 %copy-start.4 = (bf16[24,16,256]{2,1,0:T(8,128)(2,1)S(1)}, bf16[24,16,256]{2,1,0:T(8,128)(2,1)}, u32[]{:S(2)}) copy-start(bf16[24,16,256]{2,1,0:T(8,128)(2,1)} %param.10) | copy-start | bytes 589828
  67.1 7.0 %collective-permute-start.3 = (bf16[104,384]{1,0:T(8,128)(2,1)S(1)}, bf16[104,384]{1,0:T(8,128)(2,1)S(1)}, u32[]{:S(2)}, u32[]{:S(2)}) collective-permute-start(bf16[104,384]{1,0:T(8,128)(2,1)S(1)} %slice_reduce_fusion.sent), channel_id=1, source_target_pairs={{0,32},{16,48},{32,0},{48,16},{64,96},{80,112},{96,64},{112,80},{1... | collective-permute-start | bytes 239624 | tf_op jit(solution)/shard_map/ppermute | solution.py:497
  74.1 6.9 %collective-permute-start.4 = (bf16[112,384]{1,0:T(8,128)(2,1)S(1)}, bf16[112,384]{1,0:T(8,128)(2,1)S(1)}, u32[]{:S(2)}, u32[]{:S(2)}) collective-permute-start(bf16[112,384]{1,0:T(8,128)(2,1)S(1)} %step.2.sent), channel_id=1, source_target_pairs={{0,96},{16,112},{32,64},{48,80},{64,32},{80,48},{96,0},{112,16},{1... | collective-permute-start | bytes 258056 | tf_op jit(solution)/shard_map/ppermute | solution.py:509
  81.1 5.0 %collective-permute-start.5 = (bf16[112,384]{1,0:T(8,128)(2,1)S(1)}, bf16[112,384]{1,0:T(8,128)(2,1)S(1)}, u32[]{:S(2)}, u32[]{:S(2)}) collective-permute-start(bf16[112,384]{1,0:T(8,128)(2,1)S(1)} %step.3.sent), channel_id=1, source_target_pairs={{0,224},{16,240},{32,192},{48,208},{64,160},{80,176},{96,128},{112... | collective-permute-start | bytes 258056 | tf_op jit(solution)/shard_map/ppermute | solution.py:511
  87.3 14.9 %copy-start.5 = (bf16[24,16,256]{2,1,0:T(8,128)(2,1)S(1)}, bf16[24,16,256]{2,1,0:T(8,128)(2,1)}, u32[]{:S(2)}) copy-start(bf16[24,16,256]{2,1,0:T(8,128)(2,1)} %param.11) | copy-start | bytes 589828
  87.3 14.9 %copy-start.6 = (f32[24,49]{1,0:T(8,128)S(1)}, f32[24,49]{1,0:T(8,128)}, u32[]{:S(2)}) copy-start(f32[24,49]{1,0:T(8,128)} %kernel.3) | copy-start | bytes 14116
  87.3 14.9 %copy-start.7 = (s32[8,16]{1,0:T(8,128)S(1)}, s32[8,16]{1,0:T(8,128)}, u32[]{:S(2)}) copy-start(s32[8,16]{1,0:T(8,128)} %neighbours.3) | copy-start | bytes 1540
  87.3 19.6 %all-to-all-start.2 = ((bf16[16,104,384]{2,1,0:T(8,128)(2,1)}), bf16[16,104,384]{2,1,0:T(8,128)(2,1)S(1)}, u32[]{:S(2)}, u32[]{:S(2)}) async-start(bf16[16,104,384]{2,1,0:T(8,128)(2,1)} %get-tuple-element.41), calls=%async_computation.2 | async-start | bytes 2555904 | tf_op jit(solution)/shard_map/all_to_all | solution.py:516
  91.2 11.1 %collective-permute-start.10 = (bf16[384,256]{1,0:T(8,128)(2,1)S(1)}, bf16[384,256]{1,0:T(8,128)(2,1)S(1)}, u32[]{:S(2)}, u32[]{:S(2)}) collective-permute-start(bf16[384,256]{1,0:T(8,128)(2,1)S(1)} %get-tuple-element.43.own), channel_id=1, source_target_pairs={{16,0},{32,16},{48,32},{64,48},{80,64},{96,80},{112,96},{128,112},... | collective-permute-start | bytes 589832 | tf_op jit(solution)/shard_map/ppermute | solution.py:404
  97.5 4.7 %collective-permute-start.9 = (bf16[384,256]{1,0:T(8,128)(2,1)S(1)}, bf16[384,256]{1,0:T(8,128)(2,1)S(1)}, u32[]{:S(2)}, u32[]{:S(2)}) collective-permute-start(bf16[384,256]{1,0:T(8,128)(2,1)S(1)} %get-tuple-element.43.own), channel_id=1, source_target_pairs={{0,16},{16,32},{32,48},{48,64},{64,80},{80,96},{96,112},{112,128},... | collective-permute-start | bytes 589832 | tf_op jit(solution)/shard_map/ppermute | solution.py:404
  99.5 6.7 %collective-permute-start.8 = (f32[8,192]{1,0:T(8,128)S(1)}, f32[8,192]{1,0:T(8,128)S(1)}, u32[]{:S(2)}, u32[]{:S(2)}) collective-permute-start(f32[8,192]{1,0:T(8,128)S(1)} %get-tuple-element.42), channel_id=1, source_target_pairs={{0,48},{16,32},{32,16},{48,0},{64,112},{80,96},{96,80},{112,64},{1... | collective-permute-start | bytes 18440 | tf_op jit(solution)/shard_map/ppermute | solution.py:417
  100.3 6.0 %collective-permute-start.7 = (f32[8,192]{1,0:T(8,128)S(1)}, f32[8,192]{1,0:T(8,128)S(1)}, u32[]{:S(2)}, u32[]{:S(2)}) collective-permute-start(f32[8,192]{1,0:T(8,128)S(1)} %get-tuple-element.42), channel_id=1, source_target_pairs={{0,32},{16,48},{32,0},{48,16},{64,96},{80,112},{96,64},{112,80},{1... | collective-permute-start | bytes 18440 | tf_op jit(solution)/shard_map/ppermute | solution.py:417
  101.9 4.3 %collective-permute-start.6 = (f32[8,192]{1,0:T(8,128)S(1)}, f32[8,192]{1,0:T(8,128)S(1)}, u32[]{:S(2)}, u32[]{:S(2)}) collective-permute-start(f32[8,192]{1,0:T(8,128)S(1)} %get-tuple-element.42), channel_id=1, source_target_pairs={{0,16},{16,0},{32,48},{48,32},{64,80},{80,64},{96,112},{112,96},{1... | collective-permute-start | bytes 18440 | tf_op jit(solution)/shard_map/ppermute | solution.py:417
  107.0 8.0 %collective-permute-start.11 = (bf16[16,104,384]{2,1,0:T(8,128)(2,1)S(1)}, bf16[16,104,384]{2,1,0:T(8,128)(2,1)S(1)}, u32[]{:S(2)}, u32[]{:S(2)}) collective-permute-start(bf16[16,104,384]{2,1,0:T(8,128)(2,1)S(1)} %all-to-all-done.2.ref), channel_id=1, source_target_pairs={{0,16},{16,0},{32,48},{48,32},{64,80},{80,64},{96,112},{112,96},{1... | collective-permute-start | bytes 3833864 | tf_op jit(solution)/shard_map/ppermute | solution.py:534

commit v2 on v1

--- a/solution.py
+++ b/solution.py
@@ -23,6 +23,7 @@
 BF = jnp.bfloat16
 NT = (((1,), (1,)), ((), ()))
 NN = (((1,), (0,)), ((), ()))
+TN = (((0,), (0,)), ((), ()))
 
 
 def iota(shape, dim):
@@ -131,13 +132,13 @@
 
 
 def forward_kernel(
-    total, region, own, low, high, neighbours, kernel, cotangent, both, pad_out,
-    pad, result, weights, own_ref, low_ref, high_ref, neighbours_ref, kernel_ref,
-    cotangent_ref, sems,
-):
+    total, region, own, near, far, neighbours, kernel, cotangent, both, pad_out,
+    pad, result, weights, own_ref, sides, neighbours_ref, kernel_ref, cotangent_ref, sems,
+):
+    core = region[0] & 1
     pairs = [
         (kernel, kernel_ref), (neighbours, neighbours_ref), (own, own_ref),
-        (low, low_ref), (high, high_ref), (cotangent, cotangent_ref),
+        (near, sides.at[1 - core]), (far, sides.at[core]), (cotangent, cotangent_ref),
     ]
     loads = [pltpu.make_async_copy(*pair, sems.at[i]) for i, pair in enumerate(pairs)]
     for load in loads:
@@ -148,7 +149,7 @@
     for load in loads[1:5]:
         load.wait()
     lookup = lookup_rows(region, neighbours_ref, total)
-    fill_padded(pad, own_ref[...], low_ref[...], high_ref[...], lookup)
+    fill_padded(pad, own_ref[...], sides[0], sides[1], lookup)
     store = pltpu.make_async_copy(pad, pad_out, sems.at[6])
     store.start()
     convolve(pad, weights, result, False)
@@ -208,12 +209,21 @@
 
 
 def backward_kernel(
-    total_tiles, region, own, low, high, neighbours, kernel, cotangent, input_grad,
-    pad, result, weights,
-):
+    total_tiles, region, own, near, far, neighbours, kernel, cotangent, input_grad,
+    pad, result, weights, sides, sems,
+):
+    core = region[0] & 1
+    loads = [
+        pltpu.make_async_copy(near, sides.at[1 - core], sems.at[0]),
+        pltpu.make_async_copy(far, sides.at[core], sems.at[1]),
+    ]
+    for load in loads:
+        load.start()
     spread_taps(kernel, weights)
     lookup = lookup_rows(region, neighbours, total_tiles)
-    fill_padded(pad, own[...], low[...], high[...], lookup)
+    for load in loads:
+        load.wait()
+    fill_padded(pad, own[...], sides[0], sides[1], lookup)
     convolve(pad, weights, result, True)
     upstream = dot(eye(PIX), cotangent[...], NT)
     total = (upstream + rows_of(result)).astype(BF)
@@ -227,9 +237,12 @@
     return centered * inv_std, inv_std
 
 
+def stage_kernel(weight_out, copied):
+    copied[...] = weight_out[...]
+
+
 def hidden_blocks(
-    side, table, inputs, grad_mixed, bias, weight_in, weight_in_t, weight_out, weight_out_t,
-    parts, mixed_out, grad_inputs, small,
+    side, table, inputs, grad_mixed, bias, weight_in, weight_out, parts, mixed_out, grad_inputs, small,
 ):
     lane = iota((C, 128), 1)
     for q in range(4):
@@ -242,12 +255,12 @@
         activation = (hidden * cdf).astype(BF)
         slope = cdf + hidden * jnp.exp(-0.5 * hidden * hidden) * 0.3989422804014327
         mixed_out = mixed_out + dot(weight_out[:, rows], activation)
-        grad_hidden = dot(weight_out_t[rows, :], grad_mixed) * slope
+        grad_hidden = dot(weight_out[:, rows], grad_mixed, TN) * slope
         small = small + jnp.where(
             lane == block, jnp.sum(grad_hidden, axis=1, keepdims=True), 0.0
         )
         hidden_grad = grad_hidden.astype(BF)
-        grad_inputs = grad_inputs + dot(weight_in_t[:, rows], hidden_grad)
+        grad_inputs = grad_inputs + dot(weight_in[rows, :], hidden_grad, TN)
         part = dot(hidden_grad, inputs, NT).astype(BF)
         for s in range(4):
             parts[4 * k + s] = part[s * PART : (s + 1) * PART]
@@ -258,30 +271,24 @@
 
 
 def first_half_kernel(
-    region, columns, vectors, weight_in, weight_in_t, weight_out, weight_out_t,
-    parts, mixed_sum, grad_sum, small_sum, bias, late, sem,
-):
-    load = pltpu.make_async_copy(weight_out_t, late, sem)
-    load.start()
+    region, columns, vectors, weight_in, weight_out,
+    parts, mixed_sum, grad_sum, small_sum, bias,
+):
     table = jnp.transpose(vectors[...])
     normed, _ = normalize(columns)
     inputs = (normed * table[:, 4:5] + table[:, 5:6]).astype(BF)
     grad_mixed = (table[:, 6:7] * columns[:, PIX:].astype(F32)).astype(BF)
     zeros = jnp.zeros((C, PIX), F32)
-    load.wait()
     mixed_sum[...], grad_sum[...], small_sum[...] = hidden_blocks(
         1 - (region[0] & 1), table, inputs, grad_mixed, bias,
-        weight_in, weight_in_t, weight_out, late,
-        parts, zeros, zeros, jnp.zeros((C, 128), F32),
+        weight_in, weight_out, parts, zeros, zeros, jnp.zeros((C, 128), F32),
     )
 
 
 def second_half_kernel(
-    region, columns, vectors, weight_in, weight_in_t, weight_out, weight_out_t,
-    mixed_sum, grad_sum, small_sum, out, parts, extra, bias, late, sem,
-):
-    load = pltpu.make_async_copy(weight_out_t, late, sem)
-    load.start()
+    region, columns, vectors, weight_in, weight_out,
+    mixed_sum, grad_sum, small_sum, out, parts, extra, bias,
+):
     table = jnp.transpose(vectors[...])
     gain = table[:, 4:5]
     scale = table[:, 6:7]
@@ -289,11 +296,9 @@
     inputs = (normed * gain + table[:, 5:6]).astype(BF)
     upstream = columns[:, PIX:].astype(F32)
     grad_mixed = (scale * upstream).astype(BF)
-    load.wait()
     mixed_out, grad_inputs, small = hidden_blocks(
         region[0] & 1, table, inputs, grad_mixed, bias,
-        weight_in, weight_in_t, weight_out, late,
-        parts, mixed_sum[...], grad_sum[...], small_sum[...],
+        weight_in, weight_out, parts, mixed_sum[...], grad_sum[...], small_sum[...],
     )
     branch = scale * mixed_out
     grad_scale = jnp.sum(upstream * mixed_out, axis=1, keepdims=True)
@@ -343,43 +348,62 @@
     total[LONG:, :] = halves_of(taps)
 
 
-def spread_kernel(sent, got, total, kernel_grad):
-    weights, taps = joined(sent, got)
-    kernel_grad[...] = taps
-    for j in range(16):
-        total[j] = weights
+def spread_kernel(sent, got, total, kernel_grad, value, sems):
+    value[...], kernel_grad[...] = joined(sent, got)
+    stores = [pltpu.make_async_copy(value, total.at[j], sems.at[j]) for j in range(16)]
+    for store in stores:
+        store.start()
+    for store in stores:
+        store.wait()
 
 
 def place(factor, side, ref, grad_in, grad_out, tall, wide, sems):
     half = pl.multiple_of(side * 768, 768)
+    stores = []
     for j in range(8):
-        tall[j * PART : (j + 1) * PART, :] = ref[j, 0:PART, :].astype(F32) * factor
-    first = pltpu.make_async_copy(tall, grad_in.at[pl.ds(half, 768), :], sems.at[0])
-    first.start()
-    for k in range(2):
-        for s in range(4):
-            wide[s * PART : (s + 1) * PART, k * C : (k + 1) * C] = (
-                ref[8 + 4 * k + s, 0:PART, :].astype(F32) * factor
-            )
-    second = pltpu.make_async_copy(wide, grad_out.at[:, pl.ds(half, 768)], sems.at[1])
-    second.start()
-    first.wait()
-    second.wait()
+        rows = pl.ds(j * PART, PART)
+        tall[rows, :] = ref[j, 0:PART, :].astype(F32) * factor
+        target = grad_in.at[pl.ds(half + j * PART, PART), :]
+        stores.append(pltpu.make_async_copy(tall.at[rows, :], target, sems.at[j]))
+        stores[-1].start()
+    for s in range(4):
+        rows = pl.ds(s * PART, PART)
+        for k in range(2):
+            wide[rows, k * C : (k + 1) * C] = ref[8 + 4 * k + s, 0:PART, :].astype(F32) * factor
+        target = grad_out.at[rows, pl.ds(half, 768)]
+        stores.append(pltpu.make_async_copy(wide.at[rows, :], target, sems.at[8 + s]))
+        stores[-1].start()
+    return stores
 
 
 def place_own_kernel(factor, region, ref, grad_in, grad_out, tall, wide, sems):
-    place(factor, region[0] & 1, ref, grad_in, grad_out, tall, wide, sems)
-
-
-def place_other_kernel(factor, region, ref, in_a, out_a, grad_in, grad_out, tall, wide, sems):
-    place(factor, 1 - (region[0] & 1), ref, grad_in, grad_out, tall, wide, sems)
-
-
-def call(body, shapes, scratch, args, name, flops, limit, smem=(), far=(), aliases=None):
-    spaces = [
-        pl.BlockSpec(memory_space=pltpu.SMEM if i in smem else pltpu.HBM if i in far else pltpu.VMEM)
-        for i in range(len(args) + len(shapes))
-    ]
+    for store in place(factor, region[0] & 1, ref, grad_in, grad_out, tall, wide, sems):
+        store.wait()
+
+
+def place_other_kernel(
+    factor, region, ref, in_a, out_a, own_extra, grad_in, grad_out, bias, gain, shift, scale,
+    tall, wide, sems,
+):
+    stores = place(factor, 1 - (region[0] & 1), ref, grad_in, grad_out, tall, wide, sems)
+    small = (own_extra[...].astype(F32) + ref[0, PART:, :].astype(F32)) * factor
+    for q in range(4):
+        bias[q * C : (q + 1) * C] = small[q]
+    gain[...] = small[4]
+    shift[...] = small[5]
+    scale[...] = small[6]
+    for store in stores:
+        store.wait()
+
+
+def call(
+    body, shapes, scratch, args, name, flops, limit, smem=(), far=(), anywhere=(), aliases=None
+):
+    spaces = [pltpu.VMEM] * (len(args) + len(shapes))
+    for space, places in ((pltpu.SMEM, smem), (pltpu.HBM, far), (pl.ANY, anywhere)):
+        for i in places:
+            spaces[i] = space
+    spaces = [pl.BlockSpec(memory_space=space) for space in spaces]
     moved = sum(a.size * a.dtype.itemsize for a in args)
     moved += sum(math.prod(s) * jnp.dtype(d).itemsize for s, d in shapes)
     return pl.pallas_call(
@@ -397,11 +421,11 @@
     )(*args)
 
 
-def shifted(field):
+def both_sides(field):
     count = lax.axis_size("region")
-    forward = [(i, i + 1) for i in range(count - 1)]
-    backward = [(i + 1, i) for i in range(count - 1)]
-    return lax.ppermute(field, "region", forward), lax.ppermute(field, "region", backward)
+    near = [(i, i ^ 1) for i in range(count)]
+    far = [(i, ((i + 1) ^ 1) - 1) for i in range(1, count - 1)]
+    return lax.ppermute(field, "region", near), lax.ppermute(field, "region", far)
 
 
 def cube_pairs(count, bit, core=0):
@@ -431,7 +455,7 @@
 
     x = features.reshape(ROWS, PIX)
     upstream = cotangent.reshape(ROWS, PIX)
-    x_low, x_high = shifted(x)
+    x_near, x_far = both_sides(x)
     vectors = jnp.concatenate(
         [
             bias_in.reshape(4, C), norm_gain[None], norm_shift[None], layer_scale[None],
@@ -444,25 +468,28 @@
     square = ((3, 16, 16, 128), F32)
     taps = ((3, 49, 128), F32)
     block = ((ROWS, PIX), BF)
+    pair = ((2, ROWS, PIX), BF)
     columns, pad_x = call(
         functools.partial(forward_kernel, total_tiles),
         [((ROWS, 2 * PIX), BF), padded],
         [
-            padded, square, taps, block, block, block, ((8, TILE), jnp.int32), ((CH, 49), F32),
+            padded, square, taps, block, pair, ((8, TILE), jnp.int32), ((CH, 49), F32),
             block, ((7,), None),
         ],
-        (region, x, x_low, x_high, neighbours, kernel, upstream),
+        (region, x, x_near, x_far, neighbours, kernel, upstream),
         "forward_conv",
         400_000_000,
         56,
         smem=(0,),
-        far=(1, 2, 3, 4, 5, 6, 8),
+        far=(1, 4, 5, 6, 8),
+        anywhere=(2, 3),
     )
     columns = lax.all_to_all(columns, "chan", split_axis=0, concat_axis=0, tiled=True)
 
+    (staged,) = call(stage_kernel, [((C, HID), BF)], [], (weight_out,), "stage", 1_000_000, 6)
     halves = (16, PART, C)
-    pixels = (region, columns, vectors, weight_in, weight_in.T, weight_out, weight_out.T)
-    scratch = [((HID, 1), F32), ((HID, C), BF), ((), None)]
+    pixels = (region, columns, vectors, weight_in, staged)
+    scratch = [((HID, 1), F32)]
     sums = [((C, PIX), F32), ((C, PIX), F32), ((C, 128), F32)]
     send, *partial = call(
         first_half_kernel,
@@ -473,7 +500,6 @@
         1_000_000_000,
         24,
         smem=(0,),
-        far=(6,),
     )
     partner = lax.ppermute(send, "region", swap)
     out, keep, extra = call(
@@ -485,7 +511,6 @@
         1_000_000_000,
         24,
         smem=(0,),
-        far=(6,),
     )
     (travel,) = call(
         add_kernel, [((16, BRANCH + LONG, C), BF)], [], (out, keep, partner, extra),
@@ -510,50 +535,51 @@
     (sent,) = call(next_step_kernel, step, [], (sent, got), "step", 100_000, 4)
     got = lax.ppermute(sent, "region", cube_pairs(count, 4))
     mine, kernel_part = call(
-        spread_kernel, [((peers, LONG, C), BF), ((8, 192), F32)], [], (sent, got),
-        "spread", 1_000_000, 8,
+        spread_kernel, [((peers, LONG, C), BF), ((8, 192), F32)],
+        [((LONG, C), BF), ((16,), None)], (sent, got), "spread", 1_000_000, 8, far=(2,),
     )
     mine = lax.all_to_all(mine, "chan", split_axis=0, concat_axis=0, tiled=True)
 
-    grad_low, grad_high = shifted(grad)
+    grad_near, grad_far = both_sides(grad)
     kernel_part = sum_four(kernel_part, swap, cube_pairs(count, 1), cube_pairs(count, 1, 1))
     kernel_part = kernel_part.reshape(8, 3, 64).transpose(1, 0, 2).reshape(CH, 64)
     kernel_part = kernel_part[:, :49] * factor
     (input_grad,) = call(
         functools.partial(backward_kernel, total_tiles),
         [((ROWS, PIX), BF)],
-        [padded, square, taps],
-        (region, grad, grad_low, grad_high, neighbours, kernel, upstream),
+        [padded, square, taps, pair, ((2,), None)],
+        (region, grad, grad_near, grad_far, neighbours, kernel, upstream),
         "backward_conv",
         400_000_000,
         16,
         smem=(0,),
+        anywhere=(2, 3),
     )
 
     mine, kernel_part, input_grad = lax.optimization_barrier((mine, kernel_part, input_grad))
     other = lax.ppermute(mine, "region", swap)
     grads = [((HID, C), F32), ((C, HID), F32)]
-    scratch = [((768, C), F32), ((C, 768), F32), ((2,), None)]
+    scratch = [((768, C), F32), ((C, 768), F32), ((12,), None)]
     placed = call(
         functools.partial(place_own_kernel, factor),
         grads, scratch, (region, mine), "place_own", 1_000_000, 16, smem=(0,), far=(2, 3),
     )
-    grad_weight_in, grad_weight_out = call(
+    vector = ((C,), F32)
+    grad_weight_in, grad_weight_out, grad_bias, grad_gain, grad_shift, grad_scale = call(
         functools.partial(place_other_kernel, factor),
-        grads, scratch, (region, other, *placed), "place_other", 1_000_000, 16,
-        smem=(0,), far=(2, 3, 4, 5), aliases={2: 0, 3: 1},
-    )
-
-    small = (mine[0, PART:].astype(F32) + other[0, PART:].astype(F32)) * factor
+        grads + [((HID,), F32), vector, vector, vector],
+        scratch, (region, other, *placed, mine[0, PART:]), "place_other", 1_000_000, 16,
+        smem=(0,), far=(2, 3, 5, 6), aliases={2: 0, 3: 1},
+    )
     return (
         output.reshape(features.shape),
         input_grad.reshape(features.shape),
         grad_weight_in,
         grad_weight_out,
-        small[0:4].reshape(HID),
-        small[4],
-        small[5],
-        small[6],
+        grad_bias,
+        grad_gain,
+        grad_shift,
+        grad_scale,
         kernel_part,
     )
 

time: 118 us -> 112 us (0.949)
  waiting for transfers between devices: 11 us -> 17.9 us
  local copies, waits for them, and re-layouts: 8.38 us -> 2.26 us
  starting transfers between devices: 46.7 us -> 40.6 us
  Pallas kernels: 23.6 us -> 22.3 us
    all_to_all x1, waiting for transfers between devices: 3.05 us -> 7.53 us  [per_device(): lax.all_to_all(columns, 'chan', split_axis=0, concat_axis=0, tiled=True)]
    ppermute x4, starting transfers between devices: 15.5 us -> 12.9 us  [the longest x2 12.5 us: both_sides(): lax.ppermute(field, 'region', far)]
    unnamed x30 -> x26, local copies, waits for them, and re-layouts: 4.04 us -> 2.12 us
    ppermute x4, waiting for transfers between devices: 2.91 us -> 4.66 us  [the longest x2 4.65 us: both_sides(): lax.ppermute(field, 'region', far)]
    ppermute x1, starting transfers between devices: 4.57 us -> 2.82 us  [per_device(): got = lax.ppermute(sent, 'region', cube_pairs(count, 1))]
    pallas_call x11 -> x12, Pallas kernels: 23.6 us -> 22.3 us  [call(): pl.pallas_call(body, out_shape=[jax.ShapeDtypeStruct(s, d) for s, d in sh...]
  transfers between devices with their start and end apart: 14 -> 14, of which waited for: 6 -> 7; matrix products, arithmetic and copies ran while one was open for 5% -> 1% of each run, Pallas kernels for 10% -> 10%
where the time goes in v2:
time: 112 us; the launch traced here: 111 us
  starting transfers between devices  40.6 us (36%)
  blocking collectives  26.4 us (24%)
  Pallas kernels  22.3 us (20%)
  waiting for transfers between devices  17.9 us (16%)
  local copies, waits for them, and re-layouts  2.26 us (2%)
  between operations  1.12 us (1%)
    all_to_all x1, blocking collectives, per_device(): lax.all_to_all(travel, 'chan', split_axis=0, concat_axis=0, tiled=True)  26.4 us
    pallas_call x12, Pallas kernels, call(): pl.pallas_call(body, out_shape=[jax.ShapeDtypeStruct(s, d) for s, d in sh...  22.3 us
    ppermute x2, starting transfers between devices, both_sides(): lax.ppermute(field, 'region', far)  12.5 us
    all_to_all x1, waiting for transfers between devices, per_device(): lax.all_to_all(columns, 'chan', split_axis=0, concat_axis=0, tiled=True)  7.53 us
    all_to_all x1, starting transfers between devices, per_device(): lax.all_to_all(columns, 'chan', split_axis=0, concat_axis=0, tiled=True)  6.77 us
    ppermute x2, waiting for transfers between devices, both_sides(): lax.ppermute(field, 'region', far)  4.65 us
    ppermute x1, starting transfers between devices, per_device(): got = lax.ppermute(sent, 'region', cube_pairs(count, 2))  4.39 us
    ppermute x1, starting transfers between devices, per_device(): other = lax.ppermute(mine, 'region', swap)  4.17 us
  transfers between devices with their start and end apart: 14, of which 7 were waited for; matrix products, arithmetic and copies ran while one was open for 1% of the time, Pallas kernels for 10%

profile of v2, /device:TPU:1, one launch (start us, length us, event | category | flops | bytes accessed | tf_op | source)
XLA Modules:
  0.0 111.4 jit_solution(5945852371620197682)
XLA Ops:
  0.7 5.1 %collective-permute-start.1 = (bf16[384,256]{1,0:T(8,128)(2,1)}, bf16[384,256]{1,0:T(8,128)(2,1)S(1)}, u32[]{:S(2)}, u32[]{:S(2)}) collective-permute-start(bf16[384,256]{1,0:T(8,128)(2,1)} %bitcast.15), channel_id=1, source_target_pairs={{16,32},{32,16},{48,64},{64,48},{80,96},{96,80},{112,128},{128,112... | collective-permute-start | bytes 589832 | tf_op jit(solution)/shard_map/ppermute | solution.py:428
  5.8 0.1 collective-permute-start
  5.9 3.4 %collective-permute-done.1.far = bf16[384,256]{1,0:T(8,128)(2,1)S(1)} collective-permute-done((bf16[384,256]{1,0:T(8,128)(2,1)}, bf16[384,256]{1,0:T(8,128)(2,1)S(1)}, u32[]{:S(2)}, u32[]{:S(2)}) %collective-permute-start.1) | collective-permute-done | bytes 196640 | tf_op jit(solution)/shard_map/ppermute | solution.py:428
  9.3 0.0 collective-permute-done.near
  9.3 0.7 copy-done.11
  10.0 0.1 copy-done.12
  10.1 5.3 %forward_conv.1 = (bf16[384,512]{1,0:T(8,128)(2,1)}, f32[3,22,24,128]{3,2,1,0:T(8,128)}) custom-call(s32[1]{0:T(128)} %bitcast.region, bf16[384,256]{1,0:T(8,128)(2,1)} %bitcast.17, bf16[384,256]{1,0:T(8,128)(2,1)} %copy-done.12, bf16[384,256]{1,0:T(8,128)(2,1)} %copy-done.11, s32[8,16]{1,0:T(8,128)} %neighbours.3, f32[24,49]{1,0:T(8,128)} %kernel.3, ...), custom_call_target="tpu_custom_call" | custom-call | flops 400000000 | bytes 1995876 | tf_op jit(solution)/shard_map/forward_conv/pallas_call | solution.py:409
  15.4 6.8 %all-to-all-start = ((bf16[16,24,512]{2,1,0:T(8,128)(2,1)}), bf16[16,24,512]{2,1,0:T(8,128)(2,1)S(1)}, u32[]{:S(2)}, u32[]{:S(2)}) async-start(bf16[16,24,512]{2,1,0:T(8,128)(2,1)} %bitcast.21), calls=%async_computation | async-start | bytes 786432 | tf_op jit(solution)/shard_map/all_to_all | solution.py:487
  22.1 0.0 copy-start
  22.3 1.3 %copy-done.1 = bf16[384,1536]{1,0:T(8,128)(2,1)S(1)} copy-done((bf16[384,1536]{1,0:T(8,128)(2,1)S(1)}, bf16[384,1536]{1,0:T(8,128)(2,1)}, u32[]{:S(2)}) %copy-start.1) | copy-done | bytes 1179672
  23.6 0.1 stage.1.weight_out
  23.7 7.5 %all-to-all-done = bf16[16,24,512]{2,1,0:T(8,128)(2,1)S(1)} async-done(((bf16[16,24,512]{2,1,0:T(8,128)(2,1)}), bf16[16,24,512]{2,1,0:T(8,128)(2,1)S(1)}, u32[]{:S(2)}, u32[]{:S(2)}) %all-to-all-start) | async-done | bytes 393248 | tf_op jit(solution)/shard_map/all_to_all | solution.py:487
  31.2 2.3 %pixels_first.1 = (bf16[16,96,384]{2,1,0:T(8,128)(2,1)S(1)}, f32[384,256]{1,0:T(8,128)S(1)}, f32[384,256]{1,0:T(8,128)S(1)}, f32[384,128]{1,0:T(8,128)S(1)}) custom-call(s32[1]{0:T(128)} %bitcast.region, bf16[384,512]{1,0:T(8,128)(2,1)S(1)} %bitcast.13, f32[8,384]{1,0:T(8,128)S(1)} %concatenate.3.vectors, bf16[1536,384]{1,0:T(8,128)(2,1)S(1)} %copy-done, ...), custom_call_target="tpu_custom_call" | custom-call | flops 1000000000 | bytes 4927492 | tf_op jit(solution)/shard_map/pixels_first/pallas_call | solution.py:409
  33.6 0.1 collective-permute-start.2
  33.7 2.2 %pixels_second.1 = (bf16[16,32,384]{2,1,0:T(8,128)(2,1)S(1)}, bf16[16,96,384]{2,1,0:T(8,128)(2,1)S(1)}, bf16[8,384]{1,0:T(8,128)(2,1)S(1)}) custom-call(s32[1]{0:T(128)} %bitcast.region, bf16[384,512]{1,0:T(8,128)(2,1)S(1)} %bitcast.14, f32[8,384]{1,0:T(8,128)S(1)} %concatenate.3.vectors, bf16[1536,384]{1,0:T(8,128)(2,1)S(1)} %copy-done, ...), custom_call_target="tpu_custom_call" | custom-call | flops 1000000000 | bytes 5326852 | tf_op jit(solution)/shard_map/pixels_second/pallas_call | solution.py:409
  35.9 0.6 collective-permute-done.2.second
  36.5 0.3 add_cores.1
  36.8 26.4 %all_to_all.21.received = bf16[16,136,384]{2,1,0:T(8,128)(2,1)S(1)} all-to-all(bf16[16,136,384]{2,1,0:T(8,128)(2,1)S(1)} %add_cores.1), channel_id=1, replica_groups=mesh['region'=16,'chan'=16] {'chan'}, dimensions={0} | all-to-all | bytes 3342336 | tf_op jit(solution)/shard_map/all_to_all | solution.py:519
  63.3 0.2 slice_reduce_fusion.sent
  63.4 2.8 %collective-permute-start.3 = (bf16[104,384]{1,0:T(8,128)(2,1)S(1)}, bf16[104,384]{1,0:T(8,128)(2,1)S(1)}, u32[]{:S(2)}, u32[]{:S(2)}) collective-permute-start(bf16[104,384]{1,0:T(8,128)(2,1)S(1)} %slice_reduce_fusion.sent), channel_id=1, source_target_pairs={{0,32},{16,48},{32,0},{48,16},{64,96},{80,112},{96,64},{112,80},{1... | collective-permute-start | bytes 239624 | tf_op jit(solution)/shard_map/ppermute | solution.py:522
  66.3 2.4 %kernel_taps.1 = (bf16[384,256]{1,0:T(8,128)(2,1)}, bf16[384,256]{1,0:T(8,128)(2,1)S(1)}, bf16[8,384]{1,0:T(8,128)(2,1)S(1)}) custom-call(bf16[16,136,384]{2,1,0:T(8,128)(2,1)S(1)} %all_to_all.21.received, bf16[384,256]{1,0:T(8,128)(2,1)S(1)} %bitcast.18, f32[3,22,24,128]{3,2,1,0:T(8,128)S(1)} %copy-done.2), custom_call_target="tpu_custom_call" | custom-call | flops 400000000 | bytes 3078144 | tf_op jit(solution)/shard_map/kernel_taps/pallas_call | solution.py:409
  68.7 0.0 collective-permute-done.3.got
  68.7 4.4 %collective-permute-start.4 = (bf16[112,384]{1,0:T(8,128)(2,1)S(1)}, bf16[112,384]{1,0:T(8,128)(2,1)S(1)}, u32[]{:S(2)}, u32[]{:S(2)}) collective-permute-start(bf16[112,384]{1,0:T(8,128)(2,1)S(1)} %step.2.sent), channel_id=1, source_target_pairs={{0,96},{16,112},{32,64},{48,80},{64,32},{80,48},{96,0},{112,16},{1... | collective-permute-start | bytes 258056 | tf_op jit(solution)/shard_map/ppermute | solution.py:534
  73.1 2.0 %collective-permute-done.4.got = bf16[112,384]{1,0:T(8,128)(2,1)S(1)} collective-permute-done((bf16[112,384]{1,0:T(8,128)(2,1)S(1)}, bf16[112,384]{1,0:T(8,128)(2,1)S(1)}, u32[]{:S(2)}, u32[]{:S(2)}) %collective-permute-start.4) | collective-permute-done | bytes 86048 | tf_op jit(solution)/shard_map/ppermute | solution.py:534
  75.1 0.1 step.3.sent
  75.2 3.4 %collective-permute-start.5 = (bf16[112,384]{1,0:T(8,128)(2,1)S(1)}, bf16[112,384]{1,0:T(8,128)(2,1)S(1)}, u32[]{:S(2)}, u32[]{:S(2)}) collective-permute-start(bf16[112,384]{1,0:T(8,128)(2,1)S(1)} %step.3.sent), channel_id=1, source_target_pairs={{0,224},{16,240},{32,192},{48,208},{64,160},{80,176},{96,128},{112... | collective-permute-start | bytes 258056 | tf_op jit(solution)/shard_map/ppermute | solution.py:536
  78.6 2.1 %collective-permute-done.5.got = bf16[112,384]{1,0:T(8,128)(2,1)S(1)} collective-permute-done((bf16[112,384]{1,0:T(8,128)(2,1)S(1)}, bf16[112,384]{1,0:T(8,128)(2,1)S(1)}, u32[]{:S(2)}, u32[]{:S(2)}) %collective-permute-start.5) | collective-permute-done | bytes 86048 | tf_op jit(solution)/shard_map/ppermute | solution.py:536
  80.7 1.2 %spread.1 = (bf16[16,104,384]{2,1,0:T(8,128)(2,1)}, f32[8,192]{1,0:T(8,128)S(1)}) custom-call(bf16[112,384]{1,0:T(8,128)(2,1)S(1)} %step.3.sent, bf16[112,384]{1,0:T(8,128)(2,1)S(1)} %collective-permute-done.5.got), custom_call_target="tpu_custom_call" | custom-call | flops 1000000 | bytes 1456128 | tf_op jit(solution)/shard_map/spread/pallas_call | solution.py:409
  81.9 0.0 copy-start.4
  81.9 0.0 copy-start.5
  81.9 0.0 copy-start.6
  81.9 3.8 %all-to-all-start.2 = ((bf16[16,104,384]{2,1,0:T(8,128)(2,1)}), bf16[16,104,384]{2,1,0:T(8,128)(2,1)S(1)}, u32[]{:S(2)}, u32[]{:S(2)}) async-start(bf16[16,104,384]{2,1,0:T(8,128)(2,1)} %get-tuple-element.45), calls=%async_computation.2 | async-start | bytes 2555904 | tf_op jit(solution)/shard_map/all_to_all | solution.py:541
  85.8 7.4 %collective-permute-start.10 = (bf16[384,256]{1,0:T(8,128)(2,1)S(1)}, bf16[384,256]{1,0:T(8,128)(2,1)S(1)}, u32[]{:S(2)}, u32[]{:S(2)}) collective-permute-start(bf16[384,256]{1,0:T(8,128)(2,1)S(1)} %get-tuple-element.47.own), channel_id=1, source_target_pairs={{16,32},{32,16},{48,64},{64,48},{80,96},{96,80},{112,128},{128,112... | collective-permute-start | bytes 589832 | tf_op jit(solution)/shard_map/ppermute | solution.py:428
  93.2 0.3 collective-permute-start.9
  93.5 1.0 collective-permute-start.8
  94.5 0.9 collective-permute-start.7
  95.4 0.4 collective-permute-start.6
  95.7 1.2 %collective-permute-done.10.far = bf16[384,256]{1,0:T(8,128)(2,1)S(1)} collective-permute-done((bf16[384,256]{1,0:T(8,128)(2,1)S(1)}, bf16[384,256]{1,0:T(8,128)(2,1)S(1)}, u32[]{:S(2)}, u32[]{:S(2)}) %collective-permute-start.10) | collective-permute-done | bytes 196640 | tf_op jit(solution)/shard_map/ppermute | solution.py:428
  96.9 0.0 collective-permute-done.9.near
  97.0 4.7 %backward_conv.1 = bf16[384,256]{1,0:T(8,128)(2,1)} custom-call(s32[1]{0:T(128)} %bitcast.region, bf16[384,256]{1,0:T(8,128)(2,1)S(1)} %get-tuple-element.47.own, bf16[384,256]{1,0:T(8,128)(2,1)S(1)} %collective-permute-done.9.near, bf16[384,256]{1,0:T(8,128)(2,1)S(1)} %collective-permute-done.10.far, s32[8,16]{1,0:T(8,128)S(1)} %copy-done.6, ...), custom_call_target="tpu_custom_call" | custom-call | flops 400000000 | bytes 988260 | tf_op jit(solution)/shard_map/backward_conv/pallas_call | solution.py:409
  101.6 0.0 collective-permute-done.8
  101.6 0.0 collective-permute-done.7
  101.7 0.1 reshape.49
  101.8 0.6 slice_multiply_fusion
  102.4 4.2 %collective-permute-start.11 = (bf16[16,104,384]{2,1,0:T(8,128)(2,1)S(1)}, bf16[16,104,384]{2,1,0:T(8,128)(2,1)S(1)}, u32[]{:S(2)}, u32[]{:S(2)}) collective-permute-start(bf16[16,104,384]{2,1,0:T(8,128)(2,1)S(1)} %all-to-all-done.2.ref), channel_id=1, source_target_pairs={{0,16},{16,0},{32,48},{48,32},{64,80},{80,64},{96,112},{112,96},{1... | collective-permute-start | bytes 3833864 | tf_op jit(solution)/shard_map/ppermute | solution.py:560
  106.5 1.5 %place_own.1 = (f32[1536,384]{1,0:T(8,128)}, f32[384,1536]{1,0:T(8,128)}) custom-call(s32[1]{0:T(128)} %bitcast.region, bf16[16,104,384]{2,1,0:T(8,128)(2,1)S(1)} %all-to-all-done.2.ref), custom_call_target="tpu_custom_call" | custom-call | flops 1000000 | bytes 5996548 | tf_op jit(solution)/shard_map/place_own/pallas_call | solution.py:409
  108.1 1.1 collective-permute-done.11.ref
  109.2 2.1 %place_other.1 = (f32[1536,384]{1,0:T(8,128)}, f32[384,1536]{1,0:T(8,128)}, f32[1536]{0:T(1024)}, f32[384]{0:T(512)}, f32[384]{0:T(512)}, /*index=5*/f32[384]{0:T(512)}) custom-call(s32[1]{0:T(128)} %bitcast.region, bf16[16,104,384]{2,1,0:T(8,128)(2,1)S(1)} %collective-permute-done.11.ref, ...), custom_call_target="tpu_custom_call", output_to_operand_aliasing={{0}: (2, {}), {1}: (3, {})} | custom-call | flops 1000000 | bytes 10732036 | tf_op jit(solution)/shard_map/place_other/pallas_call | solution.py:409
  (31 shorter events, 0.1 us)
Async XLA Ops:
  0.6 21.5 %copy-start.8 = (f32[384]{0:T(512)S(1)}, f32[384]{0:T(512)}, u32[]{:S(2)}) copy-start(f32[384]{0:T(512)} %param.14) | copy-start | bytes 4612
  0.7 21.5 %copy-start.9 = (f32[384]{0:T(512)S(1)}, f32[384]{0:T(512)}, u32[]{:S(2)}) copy-start(f32[384]{0:T(512)} %param.15) | copy-start | bytes 4612
  0.7 21.5 %copy-start.10 = (f32[384]{0:T(512)S(1)}, f32[384]{0:T(512)}, u32[]{:S(2)}) copy-start(f32[384]{0:T(512)} %param.19) | copy-start | bytes 4612
  0.7 21.5 %copy-start.7 = (f32[1536]{0:T(1024)S(1)}, f32[1536]{0:T(1024)}, u32[]{:S(2)}) copy-start(f32[1536]{0:T(1024)} %param.17) | copy-start | bytes 18436
  0.7 8.6 %collective-permute-start.1 = (bf16[384,256]{1,0:T(8,128)(2,1)}, bf16[384,256]{1,0:T(8,128)(2,1)S(1)}, u32[]{:S(2)}, u32[]{:S(2)}) collective-permute-start(bf16[384,256]{1,0:T(8,128)(2,1)} %bitcast.15), channel_id=1, source_target_pairs={{16,32},{32,16},{48,64},{64,48},{80,96},{96,80},{112,128},{128,112... | collective-permute-start | bytes 589832 | tf_op jit(solution)/shard_map/ppermute | solution.py:428
  5.8 3.6 %collective-permute-start = (bf16[384,256]{1,0:T(8,128)(2,1)}, bf16[384,256]{1,0:T(8,128)(2,1)S(1)}, u32[]{:S(2)}, u32[]{:S(2)}) collective-permute-start(bf16[384,256]{1,0:T(8,128)(2,1)} %bitcast.16), channel_id=1, source_target_pairs={{0,16},{16,0},{32,48},{48,32},{64,80},{80,64},{96,112},{112,96},{1... | collective-permute-start | bytes 589832 | tf_op jit(solution)/shard_map/ppermute | solution.py:428
  9.3 0.7 copy-start.11
  9.3 0.7 copy-start.12
  15.4 15.9 %all-to-all-start = ((bf16[16,24,512]{2,1,0:T(8,128)(2,1)}), bf16[16,24,512]{2,1,0:T(8,128)(2,1)S(1)}, u32[]{:S(2)}, u32[]{:S(2)}) async-start(bf16[16,24,512]{2,1,0:T(8,128)(2,1)} %bitcast.21), calls=%async_computation | async-start | bytes 786432 | tf_op jit(solution)/shard_map/all_to_all | solution.py:487
  22.1 9.1 %copy-start = (bf16[1536,384]{1,0:T(8,128)(2,1)S(1)}, bf16[1536,384]{1,0:T(8,128)(2,1)}, u32[]{:S(2)}) copy-start(bf16[1536,384]{1,0:T(8,128)(2,1)} %weight_in.3) | copy-start | bytes 3538948
  22.3 1.3 %copy-start.1 = (bf16[384,1536]{1,0:T(8,128)(2,1)S(1)}, bf16[384,1536]{1,0:T(8,128)(2,1)}, u32[]{:S(2)}) copy-start(bf16[384,1536]{1,0:T(8,128)(2,1)} %weight_out.1) | copy-start | bytes 3538948
  33.6 2.9 %collective-permute-start.2 = (bf16[16,96,384]{2,1,0:T(8,128)(2,1)S(1)}, bf16[16,96,384]{2,1,0:T(8,128)(2,1)S(1)}, u32[]{:S(2)}, u32[]{:S(2)}) collective-permute-start(bf16[16,96,384]{2,1,0:T(8,128)(2,1)S(1)} %get-tuple-element.40), channel_id=1, source_target_pairs={{0,16},{16,0},{32,48},{48,32},{64,80},{80,64},{96,112},{112,96},{1... | collective-permute-start | bytes 3538952 | tf_op jit(solution)/shard_map/ppermute | solution.py:504
  63.3 3.0 %copy-start.2 = (f32[3,22,24,128]{3,2,1,0:T(8,128)S(1)}, f32[3,22,24,128]{3,2,1,0:T(8,128)}, u32[]{:S(2)}) copy-start(f32[3,22,24,128]{3,2,1,0:T(8,128)} %get-tuple-element.42.pad_x) | copy-start | bytes 2433028
  63.3 3.0 %copy-start.3 = (bf16[24,16,256]{2,1,0:T(8,128)(2,1)S(1)}, bf16[24,16,256]{2,1,0:T(8,128)(2,1)}, u32[]{:S(2)}) copy-start(bf16[24,16,256]{2,1,0:T(8,128)(2,1)} %param.10) | copy-start | bytes 589828
  63.4 5.2 %collective-permute-start.3 = (bf16[104,384]{1,0:T(8,128)(2,1)S(1)}, bf16[104,384]{1,0:T(8,128)(2,1)S(1)}, u32[]{:S(2)}, u32[]{:S(2)}) collective-permute-start(bf16[104,384]{1,0:T(8,128)(2,1)S(1)} %slice_reduce_fusion.sent), channel_id=1, source_target_pairs={{0,32},{16,48},{32,0},{48,16},{64,96},{80,112},{96,64},{112,80},{1... | collective-permute-start | bytes 239624 | tf_op jit(solution)/shard_map/ppermute | solution.py:522
  68.7 6.4 %collective-permute-start.4 = (bf16[112,384]{1,0:T(8,128)(2,1)S(1)}, bf16[112,384]{1,0:T(8,128)(2,1)S(1)}, u32[]{:S(2)}, u32[]{:S(2)}) collective-permute-start(bf16[112,384]{1,0:T(8,128)(2,1)S(1)} %step.2.sent), channel_id=1, source_target_pairs={{0,96},{16,112},{32,64},{48,80},{64,32},{80,48},{96,0},{112,16},{1... | collective-permute-start | bytes 258056 | tf_op jit(solution)/shard_map/ppermute | solution.py:534
  75.2 5.4 %collective-permute-start.5 = (bf16[112,384]{1,0:T(8,128)(2,1)S(1)}, bf16[112,384]{1,0:T(8,128)(2,1)S(1)}, u32[]{:S(2)}, u32[]{:S(2)}) collective-permute-start(bf16[112,384]{1,0:T(8,128)(2,1)S(1)} %step.3.sent), channel_id=1, source_target_pairs={{0,224},{16,240},{32,192},{48,208},{64,160},{80,176},{96,128},{112... | collective-permute-start | bytes 258056 | tf_op jit(solution)/shard_map/ppermute | solution.py:536
  81.9 15.1 %copy-start.4 = (bf16[24,16,256]{2,1,0:T(8,128)(2,1)S(1)}, bf16[24,16,256]{2,1,0:T(8,128)(2,1)}, u32[]{:S(2)}) copy-start(bf16[24,16,256]{2,1,0:T(8,128)(2,1)} %param.11) | copy-start | bytes 589828
  81.9 15.1 %copy-start.5 = (f32[24,49]{1,0:T(8,128)S(1)}, f32[24,49]{1,0:T(8,128)}, u32[]{:S(2)}) copy-start(f32[24,49]{1,0:T(8,128)} %kernel.3) | copy-start | bytes 14116
  81.9 15.1 %copy-start.6 = (s32[8,16]{1,0:T(8,128)S(1)}, s32[8,16]{1,0:T(8,128)}, u32[]{:S(2)}) copy-start(s32[8,16]{1,0:T(8,128)} %neighbours.3) | copy-start | bytes 1540
  81.9 20.5 %all-to-all-start.2 = ((bf16[16,104,384]{2,1,0:T(8,128)(2,1)}), bf16[16,104,384]{2,1,0:T(8,128)(2,1)S(1)}, u32[]{:S(2)}, u32[]{:S(2)}) async-start(bf16[16,104,384]{2,1,0:T(8,128)(2,1)} %get-tuple-element.45), calls=%async_computation.2 | async-start | bytes 2555904 | tf_op jit(solution)/shard_map/all_to_all | solution.py:541
  85.8 11.2 %collective-permute-start.10 = (bf16[384,256]{1,0:T(8,128)(2,1)S(1)}, bf16[384,256]{1,0:T(8,128)(2,1)S(1)}, u32[]{:S(2)}, u32[]{:S(2)}) collective-permute-start(bf16[384,256]{1,0:T(8,128)(2,1)S(1)} %get-tuple-element.47.own), channel_id=1, source_target_pairs={{16,32},{32,16},{48,64},{64,48},{80,96},{96,80},{112,128},{128,112... | collective-permute-start | bytes 589832 | tf_op jit(solution)/shard_map/ppermute | solution.py:428
  93.2 3.7 %collective-permute-start.9 = (bf16[384,256]{1,0:T(8,128)(2,1)S(1)}, bf16[384,256]{1,0:T(8,128)(2,1)S(1)}, u32[]{:S(2)}, u32[]{:S(2)}) collective-permute-start(bf16[384,256]{1,0:T(8,128)(2,1)S(1)} %get-tuple-element.47.own), channel_id=1, source_target_pairs={{0,16},{16,0},{32,48},{48,32},{64,80},{80,64},{96,112},{112,96},{1... | collective-permute-start | bytes 589832 | tf_op jit(solution)/shard_map/ppermute | solution.py:428
  93.5 8.1 %collective-permute-start.8 = (f32[8,192]{1,0:T(8,128)S(1)}, f32[8,192]{1,0:T(8,128)S(1)}, u32[]{:S(2)}, u32[]{:S(2)}) collective-permute-start(f32[8,192]{1,0:T(8,128)S(1)} %get-tuple-element.46), channel_id=1, source_target_pairs={{0,48},{16,32},{32,16},{48,0},{64,112},{80,96},{96,80},{112,64},{1... | collective-permute-start | bytes 18440 | tf_op jit(solution)/shard_map/ppermute | solution.py:441
  94.5 7.2 %collective-permute-start.7 = (f32[8,192]{1,0:T(8,128)S(1)}, f32[8,192]{1,0:T(8,128)S(1)}, u32[]{:S(2)}, u32[]{:S(2)}) collective-permute-start(f32[8,192]{1,0:T(8,128)S(1)} %get-tuple-element.46), channel_id=1, source_target_pairs={{0,32},{16,48},{32,0},{48,16},{64,96},{80,112},{96,64},{112,80},{1... | collective-permute-start | bytes 18440 | tf_op jit(solution)/shard_map/ppermute | solution.py:441
  95.4 6.3 %collective-permute-start.6 = (f32[8,192]{1,0:T(8,128)S(1)}, f32[8,192]{1,0:T(8,128)S(1)}, u32[]{:S(2)}, u32[]{:S(2)}) collective-permute-start(f32[8,192]{1,0:T(8,128)S(1)} %get-tuple-element.46), channel_id=1, source_target_pairs={{0,16},{16,0},{32,48},{48,32},{64,80},{80,64},{96,112},{112,96},{1... | collective-permute-start | bytes 18440 | tf_op jit(solution)/shard_map/ppermute | solution.py:441
  102.4 6.8 %collective-permute-start.11 = (bf16[16,104,384]{2,1,0:T(8,128)(2,1)S(1)}, bf16[16,104,384]{2,1,0:T(8,128)(2,1)S(1)}, u32[]{:S(2)}, u32[]{:S(2)}) collective-permute-start(bf16[16,104,384]{2,1,0:T(8,128)(2,1)S(1)} %all-to-all-done.2.ref), channel_id=1, source_target_pairs={{0,16},{16,0},{32,48},{48,32},{64,80},{80,64},{96,112},{112,96},{1... | collective-permute-start | bytes 3833864 | tf_op jit(solution)/shard_map/ppermute | solution.py:560

commit v3 on v2

--- a/solution.py
+++ b/solution.py
@@ -50,32 +50,24 @@
     return (iota((ROWS, ROWS), 1) == target).astype(F32).astype(BF)
 
 
-def fill_padded(pad, own, low, high, lookup):
-    identity = eye(PIX)
-    own_t = dot(identity, own, NT)
-    own_b = own_t.astype(BF)
-    low_b = dot(identity, low, NT).astype(BF)
-    high_b = dot(identity, high, NT).astype(BF)
+def one_hots(lookup):
     row = iota((ROWS, 128), 0)
     lane = iota((ROWS, 128), 1)
     key = jnp.where(((row >> 4) & 7) == (lane >> 4), (row >> 7) * 16 + (row & 15), -1)
-
-    def pick(directions):
-        parts = [
-            (key == lookup[d : d + 1, :]).astype(F32).astype(BF) for d in directions
-        ]
-        return jnp.concatenate(parts, axis=1)
-
-    north = pick((0, 4, 5))
-    south = pick((1, 6, 7))
-    sides = pick((2, 3))
+    parts = [
+        (key == lookup[d : d + 1, :]).astype(F32).astype(BF) for d in (0, 4, 5, 1, 6, 7, 2, 3)
+    ]
+    return jnp.concatenate(parts, axis=1)
+
+
+def fill_padded(pad, own, low, high, picks):
     for g in range(3):
         lanes = slice(g * 128, (g + 1) * 128)
-        table = jnp.concatenate([low_b[:, lanes], own_b[:, lanes], high_b[:, lanes]], axis=1)
-        top = dot(table[208:256], north)
-        bottom = dot(table[0:48], south)
-        side = dot(table, sides)
-        pad[g, 3:19, 3:19, :] = own_t[:, lanes].reshape(16, 16, 128)
+        table = jnp.concatenate([low[:, lanes], own[:, lanes], high[:, lanes]], axis=1)
+        top = dot(table[208:256], picks[:, 0:384])
+        bottom = dot(table[0:48], picks[:, 384:768])
+        side = dot(table, picks[:, 768:1024])
+        pad[g, 3:19, 3:19, :] = own[:, lanes].astype(F32).reshape(16, 16, 128)
         pad[g, 0:3, 3:19, :] = top[:, 0:128].reshape(3, 16, 128)
         pad[g, 0:3, 0:3, :] = top[:, 128:256].reshape(3, 16, 128)[:, 13:16]
         pad[g, 0:3, 19:22, :] = top[:, 256:384].reshape(3, 16, 128)[:, 0:3]
@@ -96,8 +88,7 @@
 def spread_taps(kernel, weights):
     member = (iota((CH, ROWS), 0) == (iota((CH, ROWS), 1) >> 4)).astype(F32)
     wide = lax.dot_general(
-        kernel[...], member, (((0,), (0,)), ((), ())),
-        preferred_element_type=F32, precision=lax.Precision.HIGHEST,
+        kernel, member, TN, preferred_element_type=F32, precision=lax.Precision.HIGHEST
     )
     for g in range(3):
         weights[g] = wide[:, g * 128 : (g + 1) * 128]
@@ -131,36 +122,43 @@
     return jnp.concatenate([result[g].reshape(PIX, 128) for g in range(3)], axis=1)
 
 
+def prepare_kernel(
+    total, region, neighbours, own, kernel, cotangent, own_t, upstream, weights, picks, order
+):
+    spread_taps(kernel[...], weights)
+    picks[...] = one_hots(lookup_rows(region, neighbours, total))
+    order[...] = tile_major()
+    own_t[...] = dot(eye(PIX), own[...], NT).astype(BF)
+    upstream[...] = dot(order[...], cotangent[...]).astype(BF)
+
+
+def sides_of(region, near, far):
+    first = region[0] & 1 == 0
+    near_t = dot(eye(PIX), near[...], NT)
+    far_t = dot(eye(PIX), far[...], NT)
+    low = jnp.where(first, far_t, near_t).astype(BF)
+    high = jnp.where(first, near_t, far_t).astype(BF)
+    return low, high
+
+
 def forward_kernel(
-    total, region, own, near, far, neighbours, kernel, cotangent, both, pad_out,
-    pad, result, weights, own_ref, sides, neighbours_ref, kernel_ref, cotangent_ref, sems,
-):
-    core = region[0] & 1
-    pairs = [
-        (kernel, kernel_ref), (neighbours, neighbours_ref), (own, own_ref),
-        (near, sides.at[1 - core]), (far, sides.at[core]), (cotangent, cotangent_ref),
-    ]
-    loads = [pltpu.make_async_copy(*pair, sems.at[i]) for i, pair in enumerate(pairs)]
-    for load in loads:
-        load.start()
-    order = tile_major()
-    loads[0].wait()
-    spread_taps(kernel_ref, weights)
-    for load in loads[1:5]:
-        load.wait()
-    lookup = lookup_rows(region, neighbours_ref, total)
-    fill_padded(pad, own_ref[...], sides[0], sides[1], lookup)
-    store = pltpu.make_async_copy(pad, pad_out, sems.at[6])
-    store.start()
+    region, near, far, own_t, upstream, weights, picks, order, both, pad_out,
+    pad, result, conv, sems,
+):
+    stores = [pltpu.make_async_copy(upstream, both.at[:, pl.ds(PIX, PIX)], sems.at[0])]
+    stores[0].start()
+    fill_padded(pad, own_t[...], *sides_of(region, near, far), picks)
+    pad_out[...] = pad[...].astype(BF)
     convolve(pad, weights, result, False)
-    both[:, :PIX] = dot(order, rows_of(result).astype(BF), NT).astype(BF)
-    loads[5].wait()
-    both[:, PIX:] = dot(order, cotangent_ref[...]).astype(BF)
-    store.wait()
+    conv[...] = dot(order[...], rows_of(result).astype(BF), NT).astype(BF)
+    stores.append(pltpu.make_async_copy(conv, both.at[:, pl.ds(0, PIX)], sems.at[1]))
+    stores[1].start()
+    for store in stores:
+        store.wait()
 
 
 def taps_kernel(
-    received, features, pad_x, output, grad, kernel_grad, unpacked, gradient, sums
+    received, features, pad_x, output, grad, kernel_grad, unpacked, gradient, sums, pad
 ):
     for t in range(TILE):
         part = received[t, 0:BRANCH, :].astype(F32)
@@ -177,6 +175,7 @@
     for g in range(3):
         gradient[g] = own[:, g * 128 : (g + 1) * 128].reshape(TS, TS, 128)
     sums[...] = jnp.zeros_like(sums)
+    pad[...] = pad_x[...].astype(F32)
 
     def group(g, carry):
         for b in range(7):
@@ -184,7 +183,7 @@
             for half in range(2):
                 grads = [gradient[g, i, pl.ds(8 * half, 8), :] for i in range(TS)]
                 for r in range(22):
-                    value = pad_x[g, r, pl.ds(b + 8 * half, 8), :]
+                    value = pad[g, r, pl.ds(b + 8 * half, 8), :]
                     for a in range(7):
                         i = r - a
                         if 0 <= i < TS:
@@ -209,21 +208,13 @@
 
 
 def backward_kernel(
-    total_tiles, region, own, near, far, neighbours, kernel, cotangent, input_grad,
-    pad, result, weights, sides, sems,
-):
-    core = region[0] & 1
-    loads = [
-        pltpu.make_async_copy(near, sides.at[1 - core], sems.at[0]),
-        pltpu.make_async_copy(far, sides.at[core], sems.at[1]),
-    ]
-    for load in loads:
-        load.start()
-    spread_taps(kernel, weights)
-    lookup = lookup_rows(region, neighbours, total_tiles)
-    for load in loads:
-        load.wait()
-    fill_padded(pad, own[...], sides[0], sides[1], lookup)
+    total, region, neighbours, own, near, far, kernel, cotangent, input_grad,
+    pad, result, weights, picks,
+):
+    spread_taps(kernel[...], weights)
+    picks[...] = one_hots(lookup_rows(region, neighbours, total))
+    own_t = dot(eye(PIX), own[...], NT).astype(BF)
+    fill_padded(pad, own_t, *sides_of(region, near, far), picks)
     convolve(pad, weights, result, True)
     upstream = dot(eye(PIX), cotangent[...], NT)
     total = (upstream + rows_of(result)).astype(BF)
@@ -237,12 +228,14 @@
     return centered * inv_std, inv_std
 
 
-def stage_kernel(weight_out, copied):
-    copied[...] = weight_out[...]
+def stage_kernel(weight_in, weight_out, both):
+    both[0:HID, :] = weight_in[...]
+    for q in range(4):
+        both[HID + q * C : HID + (q + 1) * C, :] = weight_out[:, q * C : (q + 1) * C]
 
 
 def hidden_blocks(
-    side, table, inputs, grad_mixed, bias, weight_in, weight_out, parts, mixed_out, grad_inputs, small,
+    side, table, inputs, grad_mixed, bias, matrices, parts, mixed_out, grad_inputs, small,
 ):
     lane = iota((C, 128), 1)
     for q in range(4):
@@ -250,17 +243,19 @@
     for k in range(2):
         block = 2 * side + k
         rows = pl.ds(pl.multiple_of(block * C, C), C)
-        hidden = dot(weight_in[rows, :], inputs) + bias[rows, :]
+        weight_in = matrices[rows, :]
+        weight_out = matrices[pl.ds(pl.multiple_of(HID + block * C, C), C), :]
+        hidden = dot(weight_in, inputs) + bias[rows, :]
         cdf = 0.5 + 0.5 * lax.erf(hidden * 0.7071067811865476)
         activation = (hidden * cdf).astype(BF)
         slope = cdf + hidden * jnp.exp(-0.5 * hidden * hidden) * 0.3989422804014327
-        mixed_out = mixed_out + dot(weight_out[:, rows], activation)
-        grad_hidden = dot(weight_out[:, rows], grad_mixed, TN) * slope
+        mixed_out = mixed_out + dot(weight_out, activation)
+        grad_hidden = dot(weight_out, grad_mixed, TN) * slope
         small = small + jnp.where(
             lane == block, jnp.sum(grad_hidden, axis=1, keepdims=True), 0.0
         )
         hidden_grad = grad_hidden.astype(BF)
-        grad_inputs = grad_inputs + dot(weight_in[rows, :], hidden_grad, TN)
+        grad_inputs = grad_inputs + dot(weight_in, hidden_grad, TN)
         part = dot(hidden_grad, inputs, NT).astype(BF)
         for s in range(4):
             parts[4 * k + s] = part[s * PART : (s + 1) * PART]
@@ -271,7 +266,7 @@
 
 
 def first_half_kernel(
-    region, columns, vectors, weight_in, weight_out,
+    region, columns, vectors, matrices,
     parts, mixed_sum, grad_sum, small_sum, bias,
 ):
     table = jnp.transpose(vectors[...])
@@ -281,12 +276,12 @@
     zeros = jnp.zeros((C, PIX), F32)
     mixed_sum[...], grad_sum[...], small_sum[...] = hidden_blocks(
         1 - (region[0] & 1), table, inputs, grad_mixed, bias,
-        weight_in, weight_out, parts, zeros, zeros, jnp.zeros((C, 128), F32),
+        matrices, parts, zeros, zeros, jnp.zeros((C, 128), F32),
     )
 
 
 def second_half_kernel(
-    region, columns, vectors, weight_in, weight_out,
+    region, columns, vectors, matrices,
     mixed_sum, grad_sum, small_sum, out, parts, extra, bias,
 ):
     table = jnp.transpose(vectors[...])
@@ -298,7 +293,7 @@
     grad_mixed = (scale * upstream).astype(BF)
     mixed_out, grad_inputs, small = hidden_blocks(
         region[0] & 1, table, inputs, grad_mixed, bias,
-        weight_in, weight_out, parts, mixed_sum[...], grad_sum[...], small_sum[...],
+        matrices, parts, mixed_sum[...], grad_sum[...], small_sum[...],
     )
     branch = scale * mixed_out
     grad_scale = jnp.sum(upstream * mixed_out, axis=1, keepdims=True)
@@ -383,15 +378,19 @@
 
 def place_other_kernel(
     factor, region, ref, in_a, out_a, own_extra, grad_in, grad_out, bias, gain, shift, scale,
-    tall, wide, sems,
+    tall, wide, bias_ref, gain_ref, shift_ref, scale_ref, sems,
 ):
     stores = place(factor, 1 - (region[0] & 1), ref, grad_in, grad_out, tall, wide, sems)
     small = (own_extra[...].astype(F32) + ref[0, PART:, :].astype(F32)) * factor
     for q in range(4):
-        bias[q * C : (q + 1) * C] = small[q]
-    gain[...] = small[4]
-    shift[...] = small[5]
-    scale[...] = small[6]
+        bias_ref[q * C : (q + 1) * C] = small[q]
+    gain_ref[...] = small[4]
+    shift_ref[...] = small[5]
+    scale_ref[...] = small[6]
+    pairs = [(bias_ref, bias), (gain_ref, gain), (shift_ref, shift), (scale_ref, scale)]
+    for i, pair in enumerate(pairs):
+        stores.append(pltpu.make_async_copy(*pair, sems.at[12 + i]))
+        stores[-1].start()
     for store in stores:
         store.wait()
 
@@ -414,7 +413,7 @@
         scratch_shapes=[
             pltpu.SemaphoreType.DMA(s) if d is None else pltpu.VMEM(s, d) for s, d in scratch
         ],
-        compiler_params=pltpu.CompilerParams(vmem_limit_bytes=limit * 1024 * 1024),
+        compiler_params=pltpu.CompilerParams(vmem_limit_bytes=int(limit * 1024 * 1024)),
         cost_estimate=pl.CostEstimate(flops=flops, bytes_accessed=moved, transcendentals=0),
         input_output_aliases=aliases or {},
         name=name,
@@ -468,27 +467,35 @@
     square = ((3, 16, 16, 128), F32)
     taps = ((3, 49, 128), F32)
     block = ((ROWS, PIX), BF)
-    pair = ((2, ROWS, PIX), BF)
+    ready = call(
+        functools.partial(prepare_kernel, total_tiles),
+        [((PIX, ROWS), BF), block, taps, ((ROWS, 1024), BF), ((ROWS, ROWS), BF)],
+        [],
+        (region, neighbours, x, kernel, upstream),
+        "prepare",
+        200_000_000,
+        16,
+        smem=(0,),
+    )
     columns, pad_x = call(
-        functools.partial(forward_kernel, total_tiles),
-        [((ROWS, 2 * PIX), BF), padded],
-        [
-            padded, square, taps, block, pair, ((8, TILE), jnp.int32), ((CH, 49), F32),
-            block, ((7,), None),
-        ],
-        (region, x, x_near, x_far, neighbours, kernel, upstream),
+        forward_kernel,
+        [((ROWS, 2 * PIX), BF), (padded[0], BF)],
+        [padded, square, block, ((2,), None)],
+        (region, x_near, x_far, *ready),
         "forward_conv",
         400_000_000,
-        56,
+        16,
         smem=(0,),
-        far=(1, 4, 5, 6, 8),
-        anywhere=(2, 3),
+        far=(8,),
     )
     columns = lax.all_to_all(columns, "chan", split_axis=0, concat_axis=0, tiled=True)
 
-    (staged,) = call(stage_kernel, [((C, HID), BF)], [], (weight_out,), "stage", 1_000_000, 6)
+    staged = call(
+        stage_kernel, [((2 * HID, C), BF)], [], (weight_in, weight_out),
+        "stage", 1_000_000, 8,
+    )
     halves = (16, PART, C)
-    pixels = (region, columns, vectors, weight_in, staged)
+    pixels = (region, columns, vectors, *staged)
     scratch = [((HID, 1), F32)]
     sums = [((C, PIX), F32), ((C, PIX), F32), ((C, 128), F32)]
     send, *partial = call(
@@ -523,7 +530,7 @@
     output, grad, kernel_part = call(
         taps_kernel,
         [((ROWS, PIX), BF), ((ROWS, PIX), BF), ((8, C), BF)],
-        [((ROWS, 2 * PIX), F32), square, ((3, 64, 128), F32)],
+        [((ROWS, 2 * PIX), F32), square, ((3, 64, 128), F32), padded],
         (travel, x, pad_x),
         "kernel_taps",
         400_000_000,
@@ -546,14 +553,13 @@
     kernel_part = kernel_part[:, :49] * factor
     (input_grad,) = call(
         functools.partial(backward_kernel, total_tiles),
-        [((ROWS, PIX), BF)],
-        [padded, square, taps, pair, ((2,), None)],
-        (region, grad, grad_near, grad_far, neighbours, kernel, upstream),
+        [block],
+        [padded, square, taps, ((ROWS, 1024), BF)],
+        (region, neighbours, grad, grad_near, grad_far, kernel, upstream),
         "backward_conv",
         400_000_000,
         16,
         smem=(0,),
-        anywhere=(2, 3),
     )
 
     mine, kernel_part, input_grad = lax.optimization_barrier((mine, kernel_part, input_grad))
@@ -564,12 +570,13 @@
         functools.partial(place_own_kernel, factor),
         grads, scratch, (region, mine), "place_own", 1_000_000, 16, smem=(0,), far=(2, 3),
     )
-    vector = ((C,), F32)
+    vectors = [((HID,), F32)] + [((C,), F32)] * 3
     grad_weight_in, grad_weight_out, grad_bias, grad_gain, grad_shift, grad_scale = call(
         functools.partial(place_other_kernel, factor),
-        grads + [((HID,), F32), vector, vector, vector],
-        scratch, (region, other, *placed, mine[0, PART:]), "place_other", 1_000_000, 16,
-        smem=(0,), far=(2, 3, 5, 6), aliases={2: 0, 3: 1},
+        grads + vectors,
+        scratch[:2] + vectors + [((16,), None)],
+        (region, other, *placed, mine[0, PART:]), "place_other", 1_000_000, 16,
+        smem=(0,), far=(2, 3, 5, 6, 7, 8, 9, 10), aliases={2: 0, 3: 1},
     )
     return (
         output.reshape(features.shape),

time: 112 us -> 109 us (0.973)
  waiting for transfers between devices: 17.9 us -> 12.6 us
  local copies, waits for them, and re-layouts: 2.26 us -> 5.96 us
  Pallas kernels: 22.3 us -> 20.6 us
    ppermute x2, waiting for transfers between devices: 4.65 us -> 0.94 us  [both_sides(): lax.ppermute(field, 'region', far)]
    unnamed x26 -> x28, local copies, waits for them, and re-layouts: 2.12 us -> 5.82 us
    pallas_call x12 -> x13, Pallas kernels: 22.3 us -> 20.6 us  [call(): pl.pallas_call(body, out_shape=[jax.ShapeDtypeStruct(s, d) for s, d in sh...]
    ppermute x1, starting transfers between devices: 0.09 us -> 1.85 us  [per_device(): partner = lax.ppermute(send, 'region', swap)]
    all_to_all x1, waiting for transfers between devices: 7.53 us -> 6.17 us  [per_device(): lax.all_to_all(columns, 'chan', split_axis=0, concat_axis=0, tiled=True)]
  transfers between devices with their start and end apart: 14 -> 14, of which waited for: 7 -> 6; matrix products, arithmetic and copies ran while one was open for 1% -> 1% of each run, Pallas kernels for 10% -> 10%
where the time goes in v3:
time: 109 us
  starting transfers between devices  41.4 us (38%)
  blocking collectives  26.2 us (24%)
  Pallas kernels  20.6 us (19%)
  waiting for transfers between devices  12.6 us (12%)
  local copies, waits for them, and re-layouts  5.96 us (5%)
  between operations  1.1 us (1%)
    all_to_all x1, blocking collectives, per_device(): lax.all_to_all(travel, 'chan', split_axis=0, concat_axis=0, tiled=True)  26.2 us
    pallas_call x13, Pallas kernels, call(): pl.pallas_call(body, out_shape=[jax.ShapeDtypeStruct(s, d) for s, d in sh...  20.6 us
    ppermute x2, starting transfers between devices, both_sides(): lax.ppermute(field, 'region', far)  12.4 us
    all_to_all x1, starting transfers between devices, per_device(): lax.all_to_all(columns, 'chan', split_axis=0, concat_axis=0, tiled=True)  6.76 us
    all_to_all x1, waiting for transfers between devices, per_device(): lax.all_to_all(columns, 'chan', split_axis=0, concat_axis=0, tiled=True)  6.17 us
    unnamed x28, local copies, waits for them, and re-layouts  5.82 us
    ppermute x1, starting transfers between devices, per_device(): other = lax.ppermute(mine, 'region', swap)  4.89 us
    ppermute x1, starting transfers between devices, per_device(): got = lax.ppermute(sent, 'region', cube_pairs(count, 2))  4.83 us
  transfers between devices with their start and end apart: 14, of which 6 were waited for; matrix products, arithmetic and copies ran while one was open for 1% of the time, Pallas kernels for 10%

profile of v3, /device:TPU:1, one launch (start us, length us, event | category | flops | bytes accessed | tf_op | source)
XLA Modules:
  0.0 108.6 jit_solution(9499236476725946494)
XLA Ops:
  0.6 4.9 %collective-permute-start.1 = (bf16[384,256]{1,0:T(8,128)(2,1)}, bf16[384,256]{1,0:T(8,128)(2,1)S(1)}, u32[]{:S(2)}, u32[]{:S(2)}) collective-permute-start(bf16[384,256]{1,0:T(8,128)(2,1)} %bitcast.15), channel_id=1, source_target_pairs={{16,32},{32,16},{48,64},{64,48},{80,96},{96,80},{112,128},{128,112... | collective-permute-start | bytes 589832 | tf_op jit(solution)/shard_map/ppermute | solution.py:427
  5.6 0.1 collective-permute-start
  5.7 0.9 copy-done.2
  6.6 0.9 copy-done.4
  7.6 0.7 copy-done.6
  8.3 0.7 copy-done.8
  8.9 0.7 prepare.1
  9.7 0.0 copy-start.11
  9.7 0.0 copy-start.12
  9.7 0.0 copy-start.13
  9.7 0.0 copy-start.10
  9.7 3.9 %forward_conv.1 = (bf16[384,512]{1,0:T(8,128)(2,1)}, bf16[3,22,24,128]{3,2,1,0:T(8,128)(2,1)S(1)}) custom-call(s32[1]{0:T(128)} %bitcast.region, bf16[384,256]{1,0:T(8,128)(2,1)S(1)} %collective-permute-done.near, bf16[384,256]{1,0:T(8,128)(2,1)S(1)} %collective-permute-done.1.far, bf16[256,384]{1,0:T(8,128)(2,1)S(1)} %get-tuple-element.39.own_t, ...), custom_call_target="tpu_custom_call" | custom-call | flops 400000000 | bytes 2741764 | tf_op jit(solution)/shard_map/forward_conv/pallas_call | solution.py:408
  13.6 6.8 %all-to-all-start = ((bf16[16,24,512]{2,1,0:T(8,128)(2,1)}), bf16[16,24,512]{2,1,0:T(8,128)(2,1)S(1)}, u32[]{:S(2)}, u32[]{:S(2)}) async-start(bf16[16,24,512]{2,1,0:T(8,128)(2,1)} %bitcast.3), calls=%async_computation | async-start | bytes 786432 | tf_op jit(solution)/shard_map/all_to_all | solution.py:491
  20.5 1.3 %copy-done = bf16[1536,384]{1,0:T(8,128)(2,1)S(1)} copy-done((bf16[1536,384]{1,0:T(8,128)(2,1)S(1)}, bf16[1536,384]{1,0:T(8,128)(2,1)}, u32[]{:S(2)}) %copy-start) | copy-done | bytes 1179672
  21.8 1.3 %copy-done.1 = bf16[384,1536]{1,0:T(8,128)(2,1)S(1)} copy-done((bf16[384,1536]{1,0:T(8,128)(2,1)S(1)}, bf16[384,1536]{1,0:T(8,128)(2,1)}, u32[]{:S(2)}) %copy-start.1) | copy-done | bytes 1179672
  23.0 0.2 stage.1.matrices
  23.2 6.2 %all-to-all-done = bf16[16,24,512]{2,1,0:T(8,128)(2,1)S(1)} async-done(((bf16[16,24,512]{2,1,0:T(8,128)(2,1)}), bf16[16,24,512]{2,1,0:T(8,128)(2,1)S(1)}, u32[]{:S(2)}, u32[]{:S(2)}) %all-to-all-start) | async-done | bytes 393248 | tf_op jit(solution)/shard_map/all_to_all | solution.py:491
  29.4 2.3 %pixels_first.1 = (bf16[16,96,384]{2,1,0:T(8,128)(2,1)S(1)}, f32[384,256]{1,0:T(8,128)S(1)}, f32[384,256]{1,0:T(8,128)S(1)}, f32[384,128]{1,0:T(8,128)S(1)}) custom-call(s32[1]{0:T(128)} %bitcast.region, bf16[384,512]{1,0:T(8,128)(2,1)S(1)} %bitcast.13, f32[8,384]{1,0:T(8,128)S(1)} %concatenate.3.vectors, bf16[3072,384]{1,0:T(8,128)(2,1)S(1)} %stage.1.matrices), custom_call_target="tpu_custom_call" | custom-call | flops 1000000000 | bytes 4927492 | tf_op jit(solution)/shard_map/pixels_first/pallas_call | solution.py:408
  31.7 1.9 %collective-permute-start.2 = (bf16[16,96,384]{2,1,0:T(8,128)(2,1)S(1)}, bf16[16,96,384]{2,1,0:T(8,128)(2,1)S(1)}, u32[]{:S(2)}, u32[]{:S(2)}) collective-permute-start(bf16[16,96,384]{2,1,0:T(8,128)(2,1)S(1)} %get-tuple-element.50), channel_id=1, source_target_pairs={{0,16},{16,0},{32,48},{48,32},{64,80},{80,64},{96,112},{112,96},{1... | collective-permute-start | bytes 3538952 | tf_op jit(solution)/shard_map/ppermute | solution.py:511
  33.6 2.3 %pixels_second.1 = (bf16[16,32,384]{2,1,0:T(8,128)(2,1)S(1)}, bf16[16,96,384]{2,1,0:T(8,128)(2,1)S(1)}, bf16[8,384]{1,0:T(8,128)(2,1)S(1)}) custom-call(s32[1]{0:T(128)} %bitcast.region, bf16[384,512]{1,0:T(8,128)(2,1)S(1)} %bitcast.14, f32[8,384]{1,0:T(8,128)S(1)} %concatenate.3.vectors, bf16[3072,384]{1,0:T(8,128)(2,1)S(1)} %stage.1.matrices, ...), custom_call_target="tpu_custom_call" | custom-call | flops 1000000000 | bytes 5326852 | tf_op jit(solution)/shard_map/pixels_second/pallas_call | solution.py:408
  35.8 0.2 collective-permute-done.2.second
  36.1 0.4 add_cores.1
  36.4 26.2 %all_to_all.21.received = bf16[16,136,384]{2,1,0:T(8,128)(2,1)S(1)} all-to-all(bf16[16,136,384]{2,1,0:T(8,128)(2,1)S(1)} %add_cores.1), channel_id=1, replica_groups=mesh['region'=16,'chan'=16] {'chan'}, dimensions={0} | all-to-all | bytes 3342336 | tf_op jit(solution)/shard_map/all_to_all | solution.py:526
  62.6 0.2 slice_reduce_fusion.sent
  62.8 1.7 %collective-permute-start.3 = (bf16[104,384]{1,0:T(8,128)(2,1)S(1)}, bf16[104,384]{1,0:T(8,128)(2,1)S(1)}, u32[]{:S(2)}, u32[]{:S(2)}) collective-permute-start(bf16[104,384]{1,0:T(8,128)(2,1)S(1)} %slice_reduce_fusion.sent), channel_id=1, source_target_pairs={{0,32},{16,48},{32,0},{48,16},{64,96},{80,112},{96,64},{112,80},{1... | collective-permute-start | bytes 239624 | tf_op jit(solution)/shard_map/ppermute | solution.py:529
  64.5 2.4 %kernel_taps.1 = (bf16[384,256]{1,0:T(8,128)(2,1)}, bf16[384,256]{1,0:T(8,128)(2,1)S(1)}, bf16[8,384]{1,0:T(8,128)(2,1)S(1)}) custom-call(bf16[16,136,384]{2,1,0:T(8,128)(2,1)S(1)} %all_to_all.21.received, bf16[384,256]{1,0:T(8,128)(2,1)S(1)} %bitcast.18, bf16[3,22,24,128]{3,2,1,0:T(8,128)(2,1)S(1)} %get-tuple-element.52.pad_x), custom_call_target="tpu_custom_call" | custom-call | flops 400000000 | bytes 2672640 | tf_op jit(solution)/shard_map/kernel_taps/pallas_call | solution.py:408
  67.0 4.8 %collective-permute-start.4 = (bf16[112,384]{1,0:T(8,128)(2,1)S(1)}, bf16[112,384]{1,0:T(8,128)(2,1)S(1)}, u32[]{:S(2)}, u32[]{:S(2)}) collective-permute-start(bf16[112,384]{1,0:T(8,128)(2,1)S(1)} %step.2.sent), channel_id=1, source_target_pairs={{0,96},{16,112},{32,64},{48,80},{64,32},{80,48},{96,0},{112,16},{1... | collective-permute-start | bytes 258056 | tf_op jit(solution)/shard_map/ppermute | solution.py:541
  71.8 2.0 %collective-permute-done.4.got = bf16[112,384]{1,0:T(8,128)(2,1)S(1)} collective-permute-done((bf16[112,384]{1,0:T(8,128)(2,1)S(1)}, bf16[112,384]{1,0:T(8,128)(2,1)S(1)}, u32[]{:S(2)}, u32[]{:S(2)}) %collective-permute-start.4) | collective-permute-done | bytes 86048 | tf_op jit(solution)/shard_map/ppermute | solution.py:541
  73.8 0.1 step.3.sent
  73.9 2.3 %collective-permute-start.5 = (bf16[112,384]{1,0:T(8,128)(2,1)S(1)}, bf16[112,384]{1,0:T(8,128)(2,1)S(1)}, u32[]{:S(2)}, u32[]{:S(2)}) collective-permute-start(bf16[112,384]{1,0:T(8,128)(2,1)S(1)} %step.3.sent), channel_id=1, source_target_pairs={{0,224},{16,240},{32,192},{48,208},{64,160},{80,176},{96,128},{112... | collective-permute-start | bytes 258056 | tf_op jit(solution)/shard_map/ppermute | solution.py:543
  76.3 2.2 %collective-permute-done.5.got = bf16[112,384]{1,0:T(8,128)(2,1)S(1)} collective-permute-done((bf16[112,384]{1,0:T(8,128)(2,1)S(1)}, bf16[112,384]{1,0:T(8,128)(2,1)S(1)}, u32[]{:S(2)}, u32[]{:S(2)}) %collective-permute-start.5) | collective-permute-done | bytes 86048 | tf_op jit(solution)/shard_map/ppermute | solution.py:543
  78.5 1.2 %spread.1 = (bf16[16,104,384]{2,1,0:T(8,128)(2,1)}, f32[8,192]{1,0:T(8,128)S(1)}) custom-call(bf16[112,384]{1,0:T(8,128)(2,1)S(1)} %step.3.sent, bf16[112,384]{1,0:T(8,128)(2,1)S(1)} %collective-permute-done.5.got), custom_call_target="tpu_custom_call" | custom-call | flops 1000000 | bytes 1456128 | tf_op jit(solution)/shard_map/spread/pallas_call | solution.py:408
  79.7 0.0 copy-start.5
  79.7 0.0 copy-start.7
  79.7 0.0 copy-start.9
  79.7 3.8 %all-to-all-start.2 = ((bf16[16,104,384]{2,1,0:T(8,128)(2,1)}), bf16[16,104,384]{2,1,0:T(8,128)(2,1)S(1)}, u32[]{:S(2)}, u32[]{:S(2)}) async-start(bf16[16,104,384]{2,1,0:T(8,128)(2,1)} %get-tuple-element.55), calls=%async_computation.2 | async-start | bytes 2555904 | tf_op jit(solution)/shard_map/all_to_all | solution.py:548
  83.6 7.5 %collective-permute-start.10 = (bf16[384,256]{1,0:T(8,128)(2,1)S(1)}, bf16[384,256]{1,0:T(8,128)(2,1)S(1)}, u32[]{:S(2)}, u32[]{:S(2)}) collective-permute-start(bf16[384,256]{1,0:T(8,128)(2,1)S(1)} %get-tuple-element.57.own), channel_id=1, source_target_pairs={{16,32},{32,16},{48,64},{64,48},{80,96},{96,80},{112,128},{128,112... | collective-permute-start | bytes 589832 | tf_op jit(solution)/shard_map/ppermute | solution.py:427
  91.1 0.1 collective-permute-start.9
  91.2 2.1 %collective-permute-start.8 = (f32[8,192]{1,0:T(8,128)S(1)}, f32[8,192]{1,0:T(8,128)S(1)}, u32[]{:S(2)}, u32[]{:S(2)}) collective-permute-start(f32[8,192]{1,0:T(8,128)S(1)} %get-tuple-element.56), channel_id=1, source_target_pairs={{0,48},{16,32},{32,16},{48,0},{64,112},{80,96},{96,80},{112,64},{1... | collective-permute-start | bytes 18440 | tf_op jit(solution)/shard_map/ppermute | solution.py:440
  93.2 0.4 collective-permute-start.6
  93.7 0.9 collective-permute-done.10.far
  94.6 4.0 %backward_conv.1 = bf16[384,256]{1,0:T(8,128)(2,1)} custom-call(s32[1]{0:T(128)} %bitcast.region, s32[8,16]{1,0:T(8,128)S(1)} %copy-done.9, bf16[384,256]{1,0:T(8,128)(2,1)S(1)} %get-tuple-element.57.own, bf16[384,256]{1,0:T(8,128)(2,1)S(1)} %collective-permute-done.9.near, bf16[384,256]{1,0:T(8,128)(2,1)S(1)} %collective-permute-done.10.far, ...), custom_call_target="tpu_custom_call" | custom-call | flops 400000000 | bytes 988260 | tf_op jit(solution)/shard_map/backward_conv/pallas_call | solution.py:408
  98.7 0.1 reshape.49
  98.7 0.6 slice_multiply_fusion
  99.4 4.9 %collective-permute-start.11 = (bf16[16,104,384]{2,1,0:T(8,128)(2,1)S(1)}, bf16[16,104,384]{2,1,0:T(8,128)(2,1)S(1)}, u32[]{:S(2)}, u32[]{:S(2)}) collective-permute-start(bf16[16,104,384]{2,1,0:T(8,128)(2,1)S(1)} %all-to-all-done.2.ref), channel_id=1, source_target_pairs={{0,16},{16,0},{32,48},{48,32},{64,80},{80,64},{96,112},{112,96},{1... | collective-permute-start | bytes 3833864 | tf_op jit(solution)/shard_map/ppermute | solution.py:566
  104.2 1.5 %place_own.1 = (f32[1536,384]{1,0:T(8,128)}, f32[384,1536]{1,0:T(8,128)}) custom-call(s32[1]{0:T(128)} %bitcast.region, bf16[16,104,384]{2,1,0:T(8,128)(2,1)S(1)} %all-to-all-done.2.ref), custom_call_target="tpu_custom_call" | custom-call | flops 1000000 | bytes 5996548 | tf_op jit(solution)/shard_map/place_own/pallas_call | solution.py:408
  105.8 1.1 %collective-permute-done.11.ref = bf16[16,104,384]{2,1,0:T(8,128)(2,1)S(1)} collective-permute-done((bf16[16,104,384]{2,1,0:T(8,128)(2,1)S(1)}, bf16[16,104,384]{2,1,0:T(8,128)(2,1)S(1)}, u32[]{:S(2)}, u32[]{:S(2)}) %collective-permute-start.11) | collective-permute-done | bytes 1277984 | tf_op jit(solution)/shard_map/ppermute | solution.py:566
  106.9 1.6 %place_other.1 = (f32[1536,384]{1,0:T(8,128)}, f32[384,1536]{1,0:T(8,128)}, f32[1536]{0:T(1024)}, f32[384]{0:T(512)}, f32[384]{0:T(512)}, /*index=5*/f32[384]{0:T(512)}) custom-call(s32[1]{0:T(128)} %bitcast.region, bf16[16,104,384]{2,1,0:T(8,128)(2,1)S(1)} %collective-permute-done.11.ref, ...), custom_call_target="tpu_custom_call", output_to_operand_aliasing={{0}: (2, {}), {1}: (3, {})} | custom-call | flops 1000000 | bytes 10732036 | tf_op jit(solution)/shard_map/place_other/pallas_call | solution.py:408
  (34 shorter events, 0.2 us)
Async XLA Ops:
  0.6 9.0 %collective-permute-start.1 = (bf16[384,256]{1,0:T(8,128)(2,1)}, bf16[384,256]{1,0:T(8,128)(2,1)S(1)}, u32[]{:S(2)}, u32[]{:S(2)}) collective-permute-start(bf16[384,256]{1,0:T(8,128)(2,1)} %bitcast.15), channel_id=1, source_target_pairs={{16,32},{32,16},{48,64},{64,48},{80,96},{96,80},{112,128},{128,112... | collective-permute-start | bytes 589832 | tf_op jit(solution)/shard_map/ppermute | solution.py:427
  5.6 4.1 %collective-permute-start = (bf16[384,256]{1,0:T(8,128)(2,1)}, bf16[384,256]{1,0:T(8,128)(2,1)S(1)}, u32[]{:S(2)}, u32[]{:S(2)}) collective-permute-start(bf16[384,256]{1,0:T(8,128)(2,1)} %bitcast.16), channel_id=1, source_target_pairs={{0,16},{16,0},{32,48},{48,32},{64,80},{80,64},{96,112},{112,96},{1... | collective-permute-start | bytes 589832 | tf_op jit(solution)/shard_map/ppermute | solution.py:427
  5.7 0.9 copy-start.2
  6.6 0.9 copy-start.4
  7.5 0.7 copy-start.6
  8.3 0.7 copy-start.8
  9.7 10.7 %copy-start.11 = (f32[384]{0:T(512)S(1)}, f32[384]{0:T(512)}, u32[]{:S(2)}) copy-start(f32[384]{0:T(512)} %param.14) | copy-start | bytes 4612
  9.7 10.7 %copy-start.12 = (f32[384]{0:T(512)S(1)}, f32[384]{0:T(512)}, u32[]{:S(2)}) copy-start(f32[384]{0:T(512)} %param.15) | copy-start | bytes 4612
  9.7 10.7 %copy-start.13 = (f32[384]{0:T(512)S(1)}, f32[384]{0:T(512)}, u32[]{:S(2)}) copy-start(f32[384]{0:T(512)} %param.19) | copy-start | bytes 4612
  9.7 10.7 %copy-start.10 = (f32[1536]{0:T(1024)S(1)}, f32[1536]{0:T(1024)}, u32[]{:S(2)}) copy-start(f32[1536]{0:T(1024)} %param.17) | copy-start | bytes 18436
  13.6 15.8 %all-to-all-start = ((bf16[16,24,512]{2,1,0:T(8,128)(2,1)}), bf16[16,24,512]{2,1,0:T(8,128)(2,1)S(1)}, u32[]{:S(2)}, u32[]{:S(2)}) async-start(bf16[16,24,512]{2,1,0:T(8,128)(2,1)} %bitcast.3), calls=%async_computation | async-start | bytes 786432 | tf_op jit(solution)/shard_map/all_to_all | solution.py:491
  20.5 1.3 %copy-start = (bf16[1536,384]{1,0:T(8,128)(2,1)S(1)}, bf16[1536,384]{1,0:T(8,128)(2,1)}, u32[]{:S(2)}) copy-start(bf16[1536,384]{1,0:T(8,128)(2,1)} %weight_in.1) | copy-start | bytes 3538948
  21.8 1.3 %copy-start.1 = (bf16[384,1536]{1,0:T(8,128)(2,1)S(1)}, bf16[384,1536]{1,0:T(8,128)(2,1)}, u32[]{:S(2)}) copy-start(bf16[384,1536]{1,0:T(8,128)(2,1)} %weight_out.1) | copy-start | bytes 3538948
  31.7 4.3 %collective-permute-start.2 = (bf16[16,96,384]{2,1,0:T(8,128)(2,1)S(1)}, bf16[16,96,384]{2,1,0:T(8,128)(2,1)S(1)}, u32[]{:S(2)}, u32[]{:S(2)}) collective-permute-start(bf16[16,96,384]{2,1,0:T(8,128)(2,1)S(1)} %get-tuple-element.50), channel_id=1, source_target_pairs={{0,16},{16,0},{32,48},{48,32},{64,80},{80,64},{96,112},{112,96},{1... | collective-permute-start | bytes 3538952 | tf_op jit(solution)/shard_map/ppermute | solution.py:511
  62.6 1.9 %copy-start.3 = (bf16[24,16,256]{2,1,0:T(8,128)(2,1)S(1)}, bf16[24,16,256]{2,1,0:T(8,128)(2,1)}, u32[]{:S(2)}) copy-start(bf16[24,16,256]{2,1,0:T(8,128)(2,1)} %param.10) | copy-start | bytes 589828
  62.8 4.2 %collective-permute-start.3 = (bf16[104,384]{1,0:T(8,128)(2,1)S(1)}, bf16[104,384]{1,0:T(8,128)(2,1)S(1)}, u32[]{:S(2)}, u32[]{:S(2)}) collective-permute-start(bf16[104,384]{1,0:T(8,128)(2,1)S(1)} %slice_reduce_fusion.sent), channel_id=1, source_target_pairs={{0,32},{16,48},{32,0},{48,16},{64,96},{80,112},{96,64},{112,80},{1... | collective-permute-start | bytes 239624 | tf_op jit(solution)/shard_map/ppermute | solution.py:529
  67.0 6.8 %collective-permute-start.4 = (bf16[112,384]{1,0:T(8,128)(2,1)S(1)}, bf16[112,384]{1,0:T(8,128)(2,1)S(1)}, u32[]{:S(2)}, u32[]{:S(2)}) collective-permute-start(bf16[112,384]{1,0:T(8,128)(2,1)S(1)} %step.2.sent), channel_id=1, source_target_pairs={{0,96},{16,112},{32,64},{48,80},{64,32},{80,48},{96,0},{112,16},{1... | collective-permute-start | bytes 258056 | tf_op jit(solution)/shard_map/ppermute | solution.py:541
  73.9 4.6 %collective-permute-start.5 = (bf16[112,384]{1,0:T(8,128)(2,1)S(1)}, bf16[112,384]{1,0:T(8,128)(2,1)S(1)}, u32[]{:S(2)}, u32[]{:S(2)}) collective-permute-start(bf16[112,384]{1,0:T(8,128)(2,1)S(1)} %step.3.sent), channel_id=1, source_target_pairs={{0,224},{16,240},{32,192},{48,208},{64,160},{80,176},{96,128},{112... | collective-permute-start | bytes 258056 | tf_op jit(solution)/shard_map/ppermute | solution.py:543
  79.7 14.9 %copy-start.5 = (bf16[24,16,256]{2,1,0:T(8,128)(2,1)S(1)}, bf16[24,16,256]{2,1,0:T(8,128)(2,1)}, u32[]{:S(2)}) copy-start(bf16[24,16,256]{2,1,0:T(8,128)(2,1)} %param.11) | copy-start | bytes 589828
  79.7 14.9 %copy-start.7 = (f32[24,49]{1,0:T(8,128)S(1)}, f32[24,49]{1,0:T(8,128)}, u32[]{:S(2)}) copy-start(f32[24,49]{1,0:T(8,128)} %kernel.3) | copy-start | bytes 14116
  79.7 14.9 %copy-start.9 = (s32[8,16]{1,0:T(8,128)S(1)}, s32[8,16]{1,0:T(8,128)}, u32[]{:S(2)}) copy-start(s32[8,16]{1,0:T(8,128)} %neighbours.3) | copy-start | bytes 1540
  79.7 19.6 %all-to-all-start.2 = ((bf16[16,104,384]{2,1,0:T(8,128)(2,1)}), bf16[16,104,384]{2,1,0:T(8,128)(2,1)S(1)}, u32[]{:S(2)}, u32[]{:S(2)}) async-start(bf16[16,104,384]{2,1,0:T(8,128)(2,1)} %get-tuple-element.55), calls=%async_computation.2 | async-start | bytes 2555904 | tf_op jit(solution)/shard_map/all_to_all | solution.py:548
  83.6 11.0 %collective-permute-start.10 = (bf16[384,256]{1,0:T(8,128)(2,1)S(1)}, bf16[384,256]{1,0:T(8,128)(2,1)S(1)}, u32[]{:S(2)}, u32[]{:S(2)}) collective-permute-start(bf16[384,256]{1,0:T(8,128)(2,1)S(1)} %get-tuple-element.57.own), channel_id=1, source_target_pairs={{16,32},{32,16},{48,64},{64,48},{80,96},{96,80},{112,128},{128,112... | collective-permute-start | bytes 589832 | tf_op jit(solution)/shard_map/ppermute | solution.py:427
  91.1 3.5 %collective-permute-start.9 = (bf16[384,256]{1,0:T(8,128)(2,1)S(1)}, bf16[384,256]{1,0:T(8,128)(2,1)S(1)}, u32[]{:S(2)}, u32[]{:S(2)}) collective-permute-start(bf16[384,256]{1,0:T(8,128)(2,1)S(1)} %get-tuple-element.57.own), channel_id=1, source_target_pairs={{0,16},{16,0},{32,48},{48,32},{64,80},{80,64},{96,112},{112,96},{1... | collective-permute-start | bytes 589832 | tf_op jit(solution)/shard_map/ppermute | solution.py:427
  91.2 7.5 %collective-permute-start.8 = (f32[8,192]{1,0:T(8,128)S(1)}, f32[8,192]{1,0:T(8,128)S(1)}, u32[]{:S(2)}, u32[]{:S(2)}) collective-permute-start(f32[8,192]{1,0:T(8,128)S(1)} %get-tuple-element.56), channel_id=1, source_target_pairs={{0,48},{16,32},{32,16},{48,0},{64,112},{80,96},{96,80},{112,64},{1... | collective-permute-start | bytes 18440 | tf_op jit(solution)/shard_map/ppermute | solution.py:440
  93.2 5.4 %collective-permute-start.7 = (f32[8,192]{1,0:T(8,128)S(1)}, f32[8,192]{1,0:T(8,128)S(1)}, u32[]{:S(2)}, u32[]{:S(2)}) collective-permute-start(f32[8,192]{1,0:T(8,128)S(1)} %get-tuple-element.56), channel_id=1, source_target_pairs={{0,32},{16,48},{32,0},{48,16},{64,96},{80,112},{96,64},{112,80},{1... | collective-permute-start | bytes 18440 | tf_op jit(solution)/shard_map/ppermute | solution.py:440
  93.2 5.4 %collective-permute-start.6 = (f32[8,192]{1,0:T(8,128)S(1)}, f32[8,192]{1,0:T(8,128)S(1)}, u32[]{:S(2)}, u32[]{:S(2)}) collective-permute-start(f32[8,192]{1,0:T(8,128)S(1)} %get-tuple-element.56), channel_id=1, source_target_pairs={{0,16},{16,0},{32,48},{48,32},{64,80},{80,64},{96,112},{112,96},{1... | collective-permute-start | bytes 18440 | tf_op jit(solution)/shard_map/ppermute | solution.py:440
  99.4 7.5 %collective-permute-start.11 = (bf16[16,104,384]{2,1,0:T(8,128)(2,1)S(1)}, bf16[16,104,384]{2,1,0:T(8,128)(2,1)S(1)}, u32[]{:S(2)}, u32[]{:S(2)}) collective-permute-start(bf16[16,104,384]{2,1,0:T(8,128)(2,1)S(1)} %all-to-all-done.2.ref), channel_id=1, source_target_pairs={{0,16},{16,0},{32,48},{48,32},{64,80},{80,64},{96,112},{112,96},{1... | collective-permute-start | bytes 3833864 | tf_op jit(solution)/shard_map/ppermute | solution.py:566

commit v4 on v3

--- a/solution.py
+++ b/solution.py
@@ -318,13 +318,9 @@
     extra[...] = jnp.transpose(small)[0:EXTRA].astype(BF)
 
 
-def add_kernel(out, first, second, extra, total):
+def add_kernel(out, first, second, total):
     total[:, 0:BRANCH, :] = out[...]
-    total[:, BRANCH : BRANCH + PART, :] = (
-        first[...].astype(F32) + second[...].astype(F32)
-    ).astype(BF)
-    total[0, BRANCH + PART :, :] = extra[...]
-    total[1:, BRANCH + PART :, :] = jnp.zeros((15, EXTRA, C), BF)
+    total[:, BRANCH:, :] = (first[...].astype(F32) + second[...].astype(F32)).astype(BF)
 
 
 def first_step_kernel(sent, got, kernel_grad, total):
@@ -381,7 +377,10 @@
     tall, wide, bias_ref, gain_ref, shift_ref, scale_ref, sems,
 ):
     stores = place(factor, 1 - (region[0] & 1), ref, grad_in, grad_out, tall, wide, sems)
-    small = (own_extra[...].astype(F32) + ref[0, PART:, :].astype(F32)) * factor
+    small = ref[0, PART:, :].astype(F32)
+    for j in range(1, 16):
+        small = small + ref[j, PART:, :].astype(F32)
+    small = (own_extra[...] + small) * factor
     for q in range(4):
         bias_ref[q * C : (q + 1) * C] = small[q]
     gain_ref[...] = small[4]
@@ -520,12 +519,12 @@
         smem=(0,),
     )
     (travel,) = call(
-        add_kernel, [((16, BRANCH + LONG, C), BF)], [], (out, keep, partner, extra),
-        "add_cores", 1_000_000, 8,
+        add_kernel, [((16, BRANCH + PART, C), BF)], [], (out, keep, partner), "add_cores", 1_000_000, 8
     )
     travel = lax.all_to_all(travel, "chan", split_axis=0, concat_axis=0, tiled=True)
 
     sent = jnp.sum(travel[:, BRANCH:].astype(F32), axis=0).astype(BF)
+    sent = jnp.concatenate([sent, extra], axis=0)
     got = lax.ppermute(sent, "region", cube_pairs(count, 1))
     output, grad, kernel_part = call(
         taps_kernel,
@@ -549,8 +548,6 @@
 
     grad_near, grad_far = both_sides(grad)
     kernel_part = sum_four(kernel_part, swap, cube_pairs(count, 1), cube_pairs(count, 1, 1))
-    kernel_part = kernel_part.reshape(8, 3, 64).transpose(1, 0, 2).reshape(CH, 64)
-    kernel_part = kernel_part[:, :49] * factor
     (input_grad,) = call(
         functools.partial(backward_kernel, total_tiles),
         [block],
@@ -564,18 +561,23 @@
 
     mine, kernel_part, input_grad = lax.optimization_barrier((mine, kernel_part, input_grad))
     other = lax.ppermute(mine, "region", swap)
+    kernel_part = kernel_part.reshape(8, 3, 64).transpose(1, 0, 2).reshape(CH, 64)
+    kernel_part = kernel_part[:, :49] * factor
     grads = [((HID, C), F32), ((C, HID), F32)]
     scratch = [((768, C), F32), ((C, 768), F32), ((12,), None)]
     placed = call(
         functools.partial(place_own_kernel, factor),
         grads, scratch, (region, mine), "place_own", 1_000_000, 16, smem=(0,), far=(2, 3),
     )
+    own_extra = mine[0, PART:].astype(F32)
+    for j in range(1, peers):
+        own_extra = own_extra + mine[j, PART:].astype(F32)
     vectors = [((HID,), F32)] + [((C,), F32)] * 3
     grad_weight_in, grad_weight_out, grad_bias, grad_gain, grad_shift, grad_scale = call(
         functools.partial(place_other_kernel, factor),
         grads + vectors,
         scratch[:2] + vectors + [((16,), None)],
-        (region, other, *placed, mine[0, PART:]), "place_other", 1_000_000, 16,
+        (region, other, *placed, own_extra), "place_other", 1_000_000, 16,
         smem=(0,), far=(2, 3, 5, 6, 7, 8, 9, 10), aliases={2: 0, 3: 1},
     )
     return (

time: 109 us -> 109 us (level)
  waiting for transfers between devices: 12.6 us -> 14.8 us
  blocking collectives: 26.2 us -> 24.6 us
    ppermute x2, starting transfers between devices: 0.19 us -> 8.4 us  [both_sides(): lax.ppermute(field, 'region', near)]
    ppermute x2, starting transfers between devices: 12.4 us -> 4.52 us  [both_sides(): lax.ppermute(field, 'region', far)]
    ppermute x2, waiting for transfers between devices: 0.94 us -> 4.18 us  [both_sides(): lax.ppermute(field, 'region', far)]
    ppermute x1, starting transfers between devices: 1.73 us -> 4.29 us  [per_device(): got = lax.ppermute(sent, 'region', cube_pairs(count, 1))]
    ppermute x1, starting transfers between devices: 1.85 us -> 0.09 us  [per_device(): partner = lax.ppermute(send, 'region', swap)]
    ppermute x1, starting transfers between devices: 2.34 us -> 3.94 us  [per_device(): got = lax.ppermute(sent, 'region', cube_pairs(count, 4))]
    all_to_all x1, blocking collectives: 26.2 us -> 24.6 us  [per_device(): lax.all_to_all(travel, 'chan', split_axis=0, concat_axis=0, tiled=True)]
    all_to_all x1, starting transfers between devices: 6.76 us -> 5.32 us  [per_device(): lax.all_to_all(columns, 'chan', split_axis=0, concat_axis=0, tiled=True)]
  transfers between devices with their start and end apart: 14 -> 14, of which waited for: 6 -> 7; matrix products, arithmetic and copies ran while one was open for 1% -> 1% of each run, Pallas kernels for 10% -> 10%
where the time goes in v4:
time: 109 us; the launch traced here: 108 us
  starting transfers between devices  40.4 us (37%)
  blocking collectives  24.6 us (23%)
  Pallas kernels  20.6 us (19%)
  waiting for transfers between devices  14.8 us (14%)
  local copies, waits for them, and re-layouts  5.95 us (5%)
    all_to_all x1, blocking collectives, per_device(): lax.all_to_all(travel, 'chan', split_axis=0, concat_axis=0, tiled=True)  24.6 us
    pallas_call x13, Pallas kernels, call(): pl.pallas_call(body, out_shape=[jax.ShapeDtypeStruct(s, d) for s, d in sh...  20.6 us
    ppermute x2, starting transfers between devices, both_sides(): lax.ppermute(field, 'region', near)  8.4 us
    unnamed x28, local copies, waits for them, and re-layouts  5.82 us
    all_to_all x1, starting transfers between devices, per_device(): lax.all_to_all(columns, 'chan', split_axis=0, concat_axis=0, tiled=True)  5.32 us
    all_to_all x1, waiting for transfers between devices, per_device(): lax.all_to_all(columns, 'chan', split_axis=0, concat_axis=0, tiled=True)  5.19 us
    ppermute x2, starting transfers between devices, both_sides(): lax.ppermute(field, 'region', far)  4.52 us
    ppermute x1, starting transfers between devices, per_device(): other = lax.ppermute(mine, 'region', swap)  4.31 us
  transfers between devices with their start and end apart: 14, of which 7 were waited for; matrix products, arithmetic and copies ran while one was open for 1% of the time, Pallas kernels for 10%

profile of v4, /device:TPU:1, one launch (start us, length us, event | category | flops | bytes accessed | tf_op | source)
XLA Modules:
  0.0 108.2 jit_solution(17702138408619865621)
XLA Ops:
  0.6 3.3 %collective-permute-start = (bf16[384,256]{1,0:T(8,128)(2,1)}, bf16[384,256]{1,0:T(8,128)(2,1)S(1)}, u32[]{:S(2)}, u32[]{:S(2)}) collective-permute-start(bf16[384,256]{1,0:T(8,128)(2,1)} %bitcast.18), channel_id=1, source_target_pairs={{0,16},{16,0},{32,48},{48,32},{64,80},{80,64},{96,112},{112,96},{1... | collective-permute-start | bytes 589832 | tf_op jit(solution)/shard_map/ppermute | solution.py:426
  4.0 1.9 %collective-permute-start.1 = (bf16[384,256]{1,0:T(8,128)(2,1)}, bf16[384,256]{1,0:T(8,128)(2,1)S(1)}, u32[]{:S(2)}, u32[]{:S(2)}) collective-permute-start(bf16[384,256]{1,0:T(8,128)(2,1)} %bitcast.19), channel_id=1, source_target_pairs={{16,32},{32,16},{48,64},{64,48},{80,96},{96,80},{112,128},{128,112... | collective-permute-start | bytes 589832 | tf_op jit(solution)/shard_map/ppermute | solution.py:426
  5.9 0.0 copy-start.2
  5.9 0.9 copy-done.2
  6.8 0.9 copy-done.4
  7.8 0.7 copy-done.6
  8.5 0.7 copy-done.8
  9.1 0.7 prepare.1
  9.9 0.0 collective-permute-done.near
  9.9 1.3 %collective-permute-done.1.far = bf16[384,256]{1,0:T(8,128)(2,1)S(1)} collective-permute-done((bf16[384,256]{1,0:T(8,128)(2,1)}, bf16[384,256]{1,0:T(8,128)(2,1)S(1)}, u32[]{:S(2)}, u32[]{:S(2)}) %collective-permute-start.1) | collective-permute-done | bytes 196640 | tf_op jit(solution)/shard_map/ppermute | solution.py:426
  11.2 3.9 %forward_conv.1 = (bf16[384,512]{1,0:T(8,128)(2,1)}, bf16[3,22,24,128]{3,2,1,0:T(8,128)(2,1)S(1)}) custom-call(s32[1]{0:T(128)} %bitcast.region, bf16[384,256]{1,0:T(8,128)(2,1)S(1)} %collective-permute-done.near, bf16[384,256]{1,0:T(8,128)(2,1)S(1)} %collective-permute-done.1.far, bf16[256,384]{1,0:T(8,128)(2,1)S(1)} %get-tuple-element.39.own_t, ...), custom_call_target="tpu_custom_call" | custom-call | flops 400000000 | bytes 2741764 | tf_op jit(solution)/shard_map/forward_conv/pallas_call | solution.py:407
  15.0 5.3 %all-to-all-start = ((bf16[16,24,512]{2,1,0:T(8,128)(2,1)}), bf16[16,24,512]{2,1,0:T(8,128)(2,1)S(1)}, u32[]{:S(2)}, u32[]{:S(2)}) async-start(bf16[16,24,512]{2,1,0:T(8,128)(2,1)} %bitcast.3), calls=%async_computation | async-start | bytes 786432 | tf_op jit(solution)/shard_map/all_to_all | solution.py:490
  20.5 1.3 %copy-done = bf16[1536,384]{1,0:T(8,128)(2,1)S(1)} copy-done((bf16[1536,384]{1,0:T(8,128)(2,1)S(1)}, bf16[1536,384]{1,0:T(8,128)(2,1)}, u32[]{:S(2)}) %copy-start) | copy-done | bytes 1179672
  21.8 1.3 %copy-done.1 = bf16[384,1536]{1,0:T(8,128)(2,1)S(1)} copy-done((bf16[384,1536]{1,0:T(8,128)(2,1)S(1)}, bf16[384,1536]{1,0:T(8,128)(2,1)}, u32[]{:S(2)}) %copy-start.1) | copy-done | bytes 1179672
  23.0 0.2 stage.1.matrices
  23.2 5.2 %all-to-all-done = bf16[16,24,512]{2,1,0:T(8,128)(2,1)S(1)} async-done(((bf16[16,24,512]{2,1,0:T(8,128)(2,1)}), bf16[16,24,512]{2,1,0:T(8,128)(2,1)S(1)}, u32[]{:S(2)}, u32[]{:S(2)}) %all-to-all-start) | async-done | bytes 393248 | tf_op jit(solution)/shard_map/all_to_all | solution.py:490
  28.4 2.3 %pixels_first.1 = (bf16[16,96,384]{2,1,0:T(8,128)(2,1)S(1)}, f32[384,256]{1,0:T(8,128)S(1)}, f32[384,256]{1,0:T(8,128)S(1)}, f32[384,128]{1,0:T(8,128)S(1)}) custom-call(s32[1]{0:T(128)} %bitcast.region, bf16[384,512]{1,0:T(8,128)(2,1)S(1)} %bitcast.16, f32[8,384]{1,0:T(8,128)S(1)} %concatenate.6.vectors, bf16[3072,384]{1,0:T(8,128)(2,1)S(1)} %stage.1.matrices), custom_call_target="tpu_custom_call" | custom-call | flops 1000000000 | bytes 4927492 | tf_op jit(solution)/shard_map/pixels_first/pallas_call | solution.py:407
  30.8 0.1 collective-permute-start.2
  30.9 2.3 %pixels_second.1 = (bf16[16,32,384]{2,1,0:T(8,128)(2,1)S(1)}, bf16[16,96,384]{2,1,0:T(8,128)(2,1)S(1)}, bf16[8,384]{1,0:T(8,128)(2,1)S(1)}) custom-call(s32[1]{0:T(128)} %bitcast.region, bf16[384,512]{1,0:T(8,128)(2,1)S(1)} %bitcast.17, f32[8,384]{1,0:T(8,128)S(1)} %concatenate.6.vectors, bf16[3072,384]{1,0:T(8,128)(2,1)S(1)} %stage.1.matrices, ...), custom_call_target="tpu_custom_call" | custom-call | flops 1000000000 | bytes 5326852 | tf_op jit(solution)/shard_map/pixels_second/pallas_call | solution.py:407
  33.1 0.6 collective-permute-done.2.second
  33.7 0.3 add_cores.1
  34.0 24.6 %all_to_all.21.received = bf16[16,128,384]{2,1,0:T(8,128)(2,1)S(1)} all-to-all(bf16[16,128,384]{2,1,0:T(8,128)(2,1)S(1)} %add_cores.1), channel_id=1, replica_groups=mesh['region'=16,'chan'=16] {'chan'}, dimensions={0} | all-to-all | bytes 3145728 | tf_op jit(solution)/shard_map/all_to_all | solution.py:524
  58.7 0.2 slice_reduce_fusion
  58.9 4.3 %collective-permute-start.3 = (bf16[104,384]{1,0:T(8,128)(2,1)S(1)}, bf16[104,384]{1,0:T(8,128)(2,1)S(1)}, u32[]{:S(2)}, u32[]{:S(2)}) collective-permute-start(bf16[104,384]{1,0:T(8,128)(2,1)S(1)} %pad_maximum_fusion.sent), channel_id=1, source_target_pairs={{0,32},{16,48},{32,0},{48,16},{64,96},{80,112},{96,64},{112,80},{1... | collective-permute-start | bytes 239624 | tf_op jit(solution)/shard_map/ppermute | solution.py:528
  63.1 2.4 %kernel_taps.1 = (bf16[384,256]{1,0:T(8,128)(2,1)}, bf16[384,256]{1,0:T(8,128)(2,1)S(1)}, bf16[8,384]{1,0:T(8,128)(2,1)S(1)}) custom-call(bf16[16,128,384]{2,1,0:T(8,128)(2,1)S(1)} %all_to_all.21.received, bf16[384,256]{1,0:T(8,128)(2,1)S(1)} %bitcast.21, bf16[3,22,24,128]{3,2,1,0:T(8,128)(2,1)S(1)} %get-tuple-element.51.pad_x), custom_call_target="tpu_custom_call" | custom-call | flops 400000000 | bytes 2574336 | tf_op jit(solution)/shard_map/kernel_taps/pallas_call | solution.py:407
  65.6 3.7 %collective-permute-start.4 = (bf16[112,384]{1,0:T(8,128)(2,1)S(1)}, bf16[112,384]{1,0:T(8,128)(2,1)S(1)}, u32[]{:S(2)}, u32[]{:S(2)}) collective-permute-start(bf16[112,384]{1,0:T(8,128)(2,1)S(1)} %step.2.sent), channel_id=1, source_target_pairs={{0,96},{16,112},{32,64},{48,80},{64,32},{80,48},{96,0},{112,16},{1... | collective-permute-start | bytes 258056 | tf_op jit(solution)/shard_map/ppermute | solution.py:540
  69.3 2.0 %collective-permute-done.4.got = bf16[112,384]{1,0:T(8,128)(2,1)S(1)} collective-permute-done((bf16[112,384]{1,0:T(8,128)(2,1)S(1)}, bf16[112,384]{1,0:T(8,128)(2,1)S(1)}, u32[]{:S(2)}, u32[]{:S(2)}) %collective-permute-start.4) | collective-permute-done | bytes 86048 | tf_op jit(solution)/shard_map/ppermute | solution.py:540
  71.3 0.1 step.3.sent
  71.4 3.9 %collective-permute-start.5 = (bf16[112,384]{1,0:T(8,128)(2,1)S(1)}, bf16[112,384]{1,0:T(8,128)(2,1)S(1)}, u32[]{:S(2)}, u32[]{:S(2)}) collective-permute-start(bf16[112,384]{1,0:T(8,128)(2,1)S(1)} %step.3.sent), channel_id=1, source_target_pairs={{0,224},{16,240},{32,192},{48,208},{64,160},{80,176},{96,128},{112... | collective-permute-start | bytes 258056 | tf_op jit(solution)/shard_map/ppermute | solution.py:542
  75.4 2.5 %collective-permute-done.5.got = bf16[112,384]{1,0:T(8,128)(2,1)S(1)} collective-permute-done((bf16[112,384]{1,0:T(8,128)(2,1)S(1)}, bf16[112,384]{1,0:T(8,128)(2,1)S(1)}, u32[]{:S(2)}, u32[]{:S(2)}) %collective-permute-start.5) | collective-permute-done | bytes 86048 | tf_op jit(solution)/shard_map/ppermute | solution.py:542
  77.9 1.2 %spread.1 = (bf16[16,104,384]{2,1,0:T(8,128)(2,1)}, f32[8,192]{1,0:T(8,128)S(1)}) custom-call(bf16[112,384]{1,0:T(8,128)(2,1)S(1)} %step.3.sent, bf16[112,384]{1,0:T(8,128)(2,1)S(1)} %collective-permute-done.5.got), custom_call_target="tpu_custom_call" | custom-call | flops 1000000 | bytes 1456128 | tf_op jit(solution)/shard_map/spread/pallas_call | solution.py:407
  79.1 0.0 copy-start.5
  79.1 0.0 copy-start.7
  79.1 0.0 copy-start.9
  79.1 3.8 %all-to-all-start.2 = ((bf16[16,104,384]{2,1,0:T(8,128)(2,1)}), bf16[16,104,384]{2,1,0:T(8,128)(2,1)S(1)}, u32[]{:S(2)}, u32[]{:S(2)}) async-start(bf16[16,104,384]{2,1,0:T(8,128)(2,1)} %get-tuple-element.55), calls=%async_computation.2 | async-start | bytes 2555904 | tf_op jit(solution)/shard_map/all_to_all | solution.py:547
  83.0 5.1 %collective-permute-start.9 = (bf16[384,256]{1,0:T(8,128)(2,1)S(1)}, bf16[384,256]{1,0:T(8,128)(2,1)S(1)}, u32[]{:S(2)}, u32[]{:S(2)}) collective-permute-start(bf16[384,256]{1,0:T(8,128)(2,1)S(1)} %get-tuple-element.57.own), channel_id=1, source_target_pairs={{0,16},{16,0},{32,48},{48,32},{64,80},{80,64},{96,112},{112,96},{1... | collective-permute-start | bytes 589832 | tf_op jit(solution)/shard_map/ppermute | solution.py:426
  88.0 2.6 %collective-permute-start.10 = (bf16[384,256]{1,0:T(8,128)(2,1)S(1)}, bf16[384,256]{1,0:T(8,128)(2,1)S(1)}, u32[]{:S(2)}, u32[]{:S(2)}) collective-permute-start(bf16[384,256]{1,0:T(8,128)(2,1)S(1)} %get-tuple-element.57.own), channel_id=1, source_target_pairs={{16,32},{32,16},{48,64},{64,48},{80,96},{96,80},{112,128},{128,112... | collective-permute-start | bytes 589832 | tf_op jit(solution)/shard_map/ppermute | solution.py:426
  90.6 0.2 collective-permute-start.7
  90.9 1.0 collective-permute-start.8
  91.9 0.7 collective-permute-start.6
  92.6 2.9 %collective-permute-done.10.far = bf16[384,256]{1,0:T(8,128)(2,1)S(1)} collective-permute-done((bf16[384,256]{1,0:T(8,128)(2,1)S(1)}, bf16[384,256]{1,0:T(8,128)(2,1)S(1)}, u32[]{:S(2)}, u32[]{:S(2)}) %collective-permute-start.10) | collective-permute-done | bytes 196640 | tf_op jit(solution)/shard_map/ppermute | solution.py:426
  95.5 4.0 %backward_conv.1 = bf16[384,256]{1,0:T(8,128)(2,1)} custom-call(s32[1]{0:T(128)} %bitcast.region, s32[8,16]{1,0:T(8,128)S(1)} %copy-done.9, bf16[384,256]{1,0:T(8,128)(2,1)S(1)} %get-tuple-element.57.own, bf16[384,256]{1,0:T(8,128)(2,1)S(1)} %collective-permute-done.9.near, bf16[384,256]{1,0:T(8,128)(2,1)S(1)} %collective-permute-done.10.far, ...), custom_call_target="tpu_custom_call" | custom-call | flops 400000000 | bytes 988260 | tf_op jit(solution)/shard_map/backward_conv/pallas_call | solution.py:407
  99.5 4.3 %collective-permute-start.11 = (bf16[16,104,384]{2,1,0:T(8,128)(2,1)S(1)}, bf16[16,104,384]{2,1,0:T(8,128)(2,1)S(1)}, u32[]{:S(2)}, u32[]{:S(2)}) collective-permute-start(bf16[16,104,384]{2,1,0:T(8,128)(2,1)S(1)} %all-to-all-done.2.ref), channel_id=1, source_target_pairs={{0,16},{16,0},{32,48},{48,32},{64,80},{80,64},{96,112},{112,96},{1... | collective-permute-start | bytes 3833864 | tf_op jit(solution)/shard_map/ppermute | solution.py:563
  103.9 0.1 reshape.81
  103.9 1.5 %place_own.1 = (f32[1536,384]{1,0:T(8,128)}, f32[384,1536]{1,0:T(8,128)}) custom-call(s32[1]{0:T(128)} %bitcast.region, bf16[16,104,384]{2,1,0:T(8,128)(2,1)S(1)} %all-to-all-done.2.ref), custom_call_target="tpu_custom_call" | custom-call | flops 1000000 | bytes 5996548 | tf_op jit(solution)/shard_map/place_own/pallas_call | solution.py:407
  105.5 0.6 slice_multiply_fusion
  106.1 0.4 collective-permute-done.11.ref
  106.5 1.6 %place_other.1 = (f32[1536,384]{1,0:T(8,128)}, f32[384,1536]{1,0:T(8,128)}, f32[1536]{0:T(1024)}, f32[384]{0:T(512)}, f32[384]{0:T(512)}, /*index=5*/f32[384]{0:T(512)}) custom-call(s32[1]{0:T(128)} %bitcast.region, bf16[16,104,384]{2,1,0:T(8,128)(2,1)S(1)} %collective-permute-done.11.ref, ...), custom_call_target="tpu_custom_call", output_to_operand_aliasing={{0}: (2, {}), {1}: (3, {})} | custom-call | flops 1000000 | bytes 10738180 | tf_op jit(solution)/shard_map/place_other/pallas_call | solution.py:407
  (35 shorter events, 0.2 us)
Async XLA Ops:
  0.6 9.2 %collective-permute-start = (bf16[384,256]{1,0:T(8,128)(2,1)}, bf16[384,256]{1,0:T(8,128)(2,1)S(1)}, u32[]{:S(2)}, u32[]{:S(2)}) collective-permute-start(bf16[384,256]{1,0:T(8,128)(2,1)} %bitcast.18), channel_id=1, source_target_pairs={{0,16},{16,0},{32,48},{48,32},{64,80},{80,64},{96,112},{112,96},{1... | collective-permute-start | bytes 589832 | tf_op jit(solution)/shard_map/ppermute | solution.py:426
  4.0 7.2 %collective-permute-start.1 = (bf16[384,256]{1,0:T(8,128)(2,1)}, bf16[384,256]{1,0:T(8,128)(2,1)S(1)}, u32[]{:S(2)}, u32[]{:S(2)}) collective-permute-start(bf16[384,256]{1,0:T(8,128)(2,1)} %bitcast.19), channel_id=1, source_target_pairs={{16,32},{32,16},{48,64},{64,48},{80,96},{96,80},{112,128},{128,112... | collective-permute-start | bytes 589832 | tf_op jit(solution)/shard_map/ppermute | solution.py:426
  5.9 0.9 copy-start.2
  6.8 0.9 copy-start.4
  7.8 0.7 copy-start.6
  8.5 0.7 copy-start.8
  11.2 9.2 %copy-start.10 = (f32[1536]{0:T(1024)S(1)}, f32[1536]{0:T(1024)}, u32[]{:S(2)}) copy-start(f32[1536]{0:T(1024)} %param.17) | copy-start | bytes 18436
  11.2 9.2 %copy-start.11 = (f32[384]{0:T(512)S(1)}, f32[384]{0:T(512)}, u32[]{:S(2)}) copy-start(f32[384]{0:T(512)} %param.14) | copy-start | bytes 4612
  11.2 9.2 %copy-start.12 = (f32[384]{0:T(512)S(1)}, f32[384]{0:T(512)}, u32[]{:S(2)}) copy-start(f32[384]{0:T(512)} %param.15) | copy-start | bytes 4612
  11.2 9.3 %copy-start.13 = (f32[384]{0:T(512)S(1)}, f32[384]{0:T(512)}, u32[]{:S(2)}) copy-start(f32[384]{0:T(512)} %param.19) | copy-start | bytes 4612
  15.0 13.4 %all-to-all-start = ((bf16[16,24,512]{2,1,0:T(8,128)(2,1)}), bf16[16,24,512]{2,1,0:T(8,128)(2,1)S(1)}, u32[]{:S(2)}, u32[]{:S(2)}) async-start(bf16[16,24,512]{2,1,0:T(8,128)(2,1)} %bitcast.3), calls=%async_computation | async-start | bytes 786432 | tf_op jit(solution)/shard_map/all_to_all | solution.py:490
  20.5 1.3 %copy-start = (bf16[1536,384]{1,0:T(8,128)(2,1)S(1)}, bf16[1536,384]{1,0:T(8,128)(2,1)}, u32[]{:S(2)}) copy-start(bf16[1536,384]{1,0:T(8,128)(2,1)} %weight_in.1) | copy-start | bytes 3538948
  21.8 1.3 %copy-start.1 = (bf16[384,1536]{1,0:T(8,128)(2,1)S(1)}, bf16[384,1536]{1,0:T(8,128)(2,1)}, u32[]{:S(2)}) copy-start(bf16[384,1536]{1,0:T(8,128)(2,1)} %weight_out.1) | copy-start | bytes 3538948
  30.8 2.9 %collective-permute-start.2 = (bf16[16,96,384]{2,1,0:T(8,128)(2,1)S(1)}, bf16[16,96,384]{2,1,0:T(8,128)(2,1)S(1)}, u32[]{:S(2)}, u32[]{:S(2)}) collective-permute-start(bf16[16,96,384]{2,1,0:T(8,128)(2,1)S(1)} %get-tuple-element.50), channel_id=1, source_target_pairs={{0,16},{16,0},{32,48},{48,32},{64,80},{80,64},{96,112},{112,96},{1... | collective-permute-start | bytes 3538952 | tf_op jit(solution)/shard_map/ppermute | solution.py:510
  58.7 4.5 %copy-start.3 = (bf16[24,16,256]{2,1,0:T(8,128)(2,1)S(1)}, bf16[24,16,256]{2,1,0:T(8,128)(2,1)}, u32[]{:S(2)}) copy-start(bf16[24,16,256]{2,1,0:T(8,128)(2,1)} %param.10) | copy-start | bytes 589828
  58.9 6.7 %collective-permute-start.3 = (bf16[104,384]{1,0:T(8,128)(2,1)S(1)}, bf16[104,384]{1,0:T(8,128)(2,1)S(1)}, u32[]{:S(2)}, u32[]{:S(2)}) collective-permute-start(bf16[104,384]{1,0:T(8,128)(2,1)S(1)} %pad_maximum_fusion.sent), channel_id=1, source_target_pairs={{0,32},{16,48},{32,0},{48,16},{64,96},{80,112},{96,64},{112,80},{1... | collective-permute-start | bytes 239624 | tf_op jit(solution)/shard_map/ppermute | solution.py:528
  65.6 5.7 %collective-permute-start.4 = (bf16[112,384]{1,0:T(8,128)(2,1)S(1)}, bf16[112,384]{1,0:T(8,128)(2,1)S(1)}, u32[]{:S(2)}, u32[]{:S(2)}) collective-permute-start(bf16[112,384]{1,0:T(8,128)(2,1)S(1)} %step.2.sent), channel_id=1, source_target_pairs={{0,96},{16,112},{32,64},{48,80},{64,32},{80,48},{96,0},{112,16},{1... | collective-permute-start | bytes 258056 | tf_op jit(solution)/shard_map/ppermute | solution.py:540
  71.4 6.4 %collective-permute-start.5 = (bf16[112,384]{1,0:T(8,128)(2,1)S(1)}, bf16[112,384]{1,0:T(8,128)(2,1)S(1)}, u32[]{:S(2)}, u32[]{:S(2)}) collective-permute-start(bf16[112,384]{1,0:T(8,128)(2,1)S(1)} %step.3.sent), channel_id=1, source_target_pairs={{0,224},{16,240},{32,192},{48,208},{64,160},{80,176},{96,128},{112... | collective-permute-start | bytes 258056 | tf_op jit(solution)/shard_map/ppermute | solution.py:542
  79.1 16.4 %copy-start.5 = (bf16[24,16,256]{2,1,0:T(8,128)(2,1)S(1)}, bf16[24,16,256]{2,1,0:T(8,128)(2,1)}, u32[]{:S(2)}) copy-start(bf16[24,16,256]{2,1,0:T(8,128)(2,1)} %param.11) | copy-start | bytes 589828
  79.1 16.4 %copy-start.7 = (f32[24,49]{1,0:T(8,128)S(1)}, f32[24,49]{1,0:T(8,128)}, u32[]{:S(2)}) copy-start(f32[24,49]{1,0:T(8,128)} %kernel.3) | copy-start | bytes 14116
  79.1 16.4 %copy-start.9 = (s32[8,16]{1,0:T(8,128)S(1)}, s32[8,16]{1,0:T(8,128)}, u32[]{:S(2)}) copy-start(s32[8,16]{1,0:T(8,128)} %neighbours.3) | copy-start | bytes 1540
  79.1 20.4 %all-to-all-start.2 = ((bf16[16,104,384]{2,1,0:T(8,128)(2,1)}), bf16[16,104,384]{2,1,0:T(8,128)(2,1)S(1)}, u32[]{:S(2)}, u32[]{:S(2)}) async-start(bf16[16,104,384]{2,1,0:T(8,128)(2,1)} %get-tuple-element.55), calls=%async_computation.2 | async-start | bytes 2555904 | tf_op jit(solution)/shard_map/all_to_all | solution.py:547
  83.0 9.6 %collective-permute-start.9 = (bf16[384,256]{1,0:T(8,128)(2,1)S(1)}, bf16[384,256]{1,0:T(8,128)(2,1)S(1)}, u32[]{:S(2)}, u32[]{:S(2)}) collective-permute-start(bf16[384,256]{1,0:T(8,128)(2,1)S(1)} %get-tuple-element.57.own), channel_id=1, source_target_pairs={{0,16},{16,0},{32,48},{48,32},{64,80},{80,64},{96,112},{112,96},{1... | collective-permute-start | bytes 589832 | tf_op jit(solution)/shard_map/ppermute | solution.py:426
  88.0 7.4 %collective-permute-start.10 = (bf16[384,256]{1,0:T(8,128)(2,1)S(1)}, bf16[384,256]{1,0:T(8,128)(2,1)S(1)}, u32[]{:S(2)}, u32[]{:S(2)}) collective-permute-start(bf16[384,256]{1,0:T(8,128)(2,1)S(1)} %get-tuple-element.57.own), channel_id=1, source_target_pairs={{16,32},{32,16},{48,64},{64,48},{80,96},{96,80},{112,128},{128,112... | collective-permute-start | bytes 589832 | tf_op jit(solution)/shard_map/ppermute | solution.py:426
  90.6 8.9 %collective-permute-start.7 = (f32[8,192]{1,0:T(8,128)S(1)}, f32[8,192]{1,0:T(8,128)S(1)}, u32[]{:S(2)}, u32[]{:S(2)}) collective-permute-start(f32[8,192]{1,0:T(8,128)S(1)} %get-tuple-element.56), channel_id=1, source_target_pairs={{0,32},{16,48},{32,0},{48,16},{64,96},{80,112},{96,64},{112,80},{1... | collective-permute-start | bytes 18440 | tf_op jit(solution)/shard_map/ppermute | solution.py:439
  90.9 8.6 %collective-permute-start.8 = (f32[8,192]{1,0:T(8,128)S(1)}, f32[8,192]{1,0:T(8,128)S(1)}, u32[]{:S(2)}, u32[]{:S(2)}) collective-permute-start(f32[8,192]{1,0:T(8,128)S(1)} %get-tuple-element.56), channel_id=1, source_target_pairs={{0,48},{16,32},{32,16},{48,0},{64,112},{80,96},{96,80},{112,64},{1... | collective-permute-start | bytes 18440 | tf_op jit(solution)/shard_map/ppermute | solution.py:439
  91.9 7.7 %collective-permute-start.6 = (f32[8,192]{1,0:T(8,128)S(1)}, f32[8,192]{1,0:T(8,128)S(1)}, u32[]{:S(2)}, u32[]{:S(2)}) collective-permute-start(f32[8,192]{1,0:T(8,128)S(1)} %get-tuple-element.56), channel_id=1, source_target_pairs={{0,16},{16,0},{32,48},{48,32},{64,80},{80,64},{96,112},{112,96},{1... | collective-permute-start | bytes 18440 | tf_op jit(solution)/shard_map/ppermute | solution.py:439
  99.5 6.9 %collective-permute-start.11 = (bf16[16,104,384]{2,1,0:T(8,128)(2,1)S(1)}, bf16[16,104,384]{2,1,0:T(8,128)(2,1)S(1)}, u32[]{:S(2)}, u32[]{:S(2)}) collective-permute-start(bf16[16,104,384]{2,1,0:T(8,128)(2,1)S(1)} %all-to-all-done.2.ref), channel_id=1, source_target_pairs={{0,16},{16,0},{32,48},{48,32},{64,80},{80,64},{96,112},{112,96},{1... | collective-permute-start | bytes 3833864 | tf_op jit(solution)/shard_map/ppermute | solution.py:563

commit v5 on v4

--- a/solution.py
+++ b/solution.py
@@ -61,12 +61,19 @@
 
 
 def fill_padded(pad, own, low, high, picks):
+    apart = jnp.concatenate([picks[0:128, :], picks[256:384, :]], axis=0)
     for g in range(3):
         lanes = slice(g * 128, (g + 1) * 128)
-        table = jnp.concatenate([low[:, lanes], own[:, lanes], high[:, lanes]], axis=1)
-        top = dot(table[208:256], picks[:, 0:384])
-        bottom = dot(table[0:48], picks[:, 384:768])
-        side = dot(table, picks[:, 768:1024])
+        mine = own[:, lanes]
+        sides = jnp.concatenate([low[lanes, :], high[lanes, :]], axis=0)
+
+        def take(span, first, last):
+            spread = dot(sides[:, span], apart[:, first:last], TN)
+            return spread + dot(mine[span], picks[128:256, first:last])
+
+        top = take(slice(128, 256), 0, 384)[80:128]
+        bottom = take(slice(0, 128), 384, 768)[0:48]
+        side = take(slice(0, 256), 768, 1024)
         pad[g, 3:19, 3:19, :] = own[:, lanes].astype(F32).reshape(16, 16, 128)
         pad[g, 0:3, 3:19, :] = top[:, 0:128].reshape(3, 16, 128)
         pad[g, 0:3, 0:3, :] = top[:, 128:256].reshape(3, 16, 128)[:, 13:16]
@@ -95,7 +102,7 @@
 
 
 def convolve(pad, weights, result, flip):
-    def group(g, carry):
+    def group(g):
         for half in range(2):
             total = [None] * TS
             for b in range(7):
@@ -113,9 +120,9 @@
                             total[i] = term if total[i] is None else total[i] + term
             for i in range(TS):
                 result[g, i, pl.ds(8 * half, 8), :] = total[i]
-        return carry
-
-    lax.fori_loop(0, 3, group, 0)
+
+    for g in range(3):
+        group(g)
 
 
 def rows_of(result):
@@ -134,10 +141,8 @@
 
 def sides_of(region, near, far):
     first = region[0] & 1 == 0
-    near_t = dot(eye(PIX), near[...], NT)
-    far_t = dot(eye(PIX), far[...], NT)
-    low = jnp.where(first, far_t, near_t).astype(BF)
-    high = jnp.where(first, near_t, far_t).astype(BF)
+    low = jnp.where(first, far[...], near[...])
+    high = jnp.where(first, near[...], far[...])
     return low, high
 
 
@@ -177,7 +182,7 @@
     sums[...] = jnp.zeros_like(sums)
     pad[...] = pad_x[...].astype(F32)
 
-    def group(g, carry):
+    def group(g):
         for b in range(7):
             total = [None] * 7
             for half in range(2):
@@ -191,9 +196,9 @@
                             total[a] = term if total[a] is None else total[a] + term
             for a in range(7):
                 sums[g, pl.ds(7 * a + b, 1), :] = jnp.sum(total[a], axis=0, keepdims=True)
-        return carry
-
-    lax.fori_loop(0, 3, group, 0)
+
+    for g in range(3):
+        group(g)
     spread = jnp.concatenate([sums[g] for g in range(3)], axis=1)
     member = (iota((32, ROWS), 0) == (iota((32, ROWS), 1) >> 4)).astype(F32)
     total = lax.dot_general(

time: 109 us -> 108 us (level)
  Pallas kernels: 20.6 us -> 18.8 us
    pallas_call x13, Pallas kernels: 20.6 us -> 18.8 us  [call(): pl.pallas_call(body, out_shape=[jax.ShapeDtypeStruct(s, d) for s, d in sh...]
where the time goes in v5:
time: 108 us; the launch traced here: 107 us
  starting transfers between devices  41.2 us (38%)
  blocking collectives  24.6 us (23%)
  Pallas kernels  18.8 us (17%)
  waiting for transfers between devices  14.9 us (14%)
  local copies, waits for them, and re-layouts  5.95 us (6%)
    all_to_all x1, blocking collectives, per_device(): lax.all_to_all(travel, 'chan', split_axis=0, concat_axis=0, tiled=True)  24.6 us
    pallas_call x13, Pallas kernels, call(): pl.pallas_call(body, out_shape=[jax.ShapeDtypeStruct(s, d) for s, d in sh...  18.8 us
    ppermute x2, starting transfers between devices, both_sides(): lax.ppermute(field, 'region', near)  8.21 us
    unnamed x28, local copies, waits for them, and re-layouts  5.82 us
    all_to_all x1, starting transfers between devices, per_device(): lax.all_to_all(columns, 'chan', split_axis=0, concat_axis=0, tiled=True)  5.32 us
    all_to_all x1, waiting for transfers between devices, per_device(): lax.all_to_all(columns, 'chan', split_axis=0, concat_axis=0, tiled=True)  5.19 us
    ppermute x1, starting transfers between devices, per_device(): other = lax.ppermute(mine, 'region', swap)  5.13 us
    ppermute x2, starting transfers between devices, both_sides(): lax.ppermute(field, 'region', far)  4.55 us
  transfers between devices with their start and end apart: 14, of which 7 were waited for; matrix products, arithmetic and copies ran while one was open for 1% of the time, Pallas kernels for 10%

profile of v5, /device:TPU:1, one launch (start us, length us, event | category | flops | bytes accessed | tf_op | source)
XLA Modules:
  0.0 107.3 jit_solution(6509074856689591868)
XLA Ops:
  0.6 3.3 %collective-permute-start = (bf16[384,256]{1,0:T(8,128)(2,1)}, bf16[384,256]{1,0:T(8,128)(2,1)S(1)}, u32[]{:S(2)}, u32[]{:S(2)}) collective-permute-start(bf16[384,256]{1,0:T(8,128)(2,1)} %bitcast.18), channel_id=1, source_target_pairs={{0,16},{16,0},{32,48},{48,32},{64,80},{80,64},{96,112},{112,96},{1... | collective-permute-start | bytes 589832 | tf_op jit(solution)/shard_map/ppermute | solution.py:431
  4.0 1.9 %collective-permute-start.1 = (bf16[384,256]{1,0:T(8,128)(2,1)}, bf16[384,256]{1,0:T(8,128)(2,1)S(1)}, u32[]{:S(2)}, u32[]{:S(2)}) collective-permute-start(bf16[384,256]{1,0:T(8,128)(2,1)} %bitcast.19), channel_id=1, source_target_pairs={{16,32},{32,16},{48,64},{64,48},{80,96},{96,80},{112,128},{128,112... | collective-permute-start | bytes 589832 | tf_op jit(solution)/shard_map/ppermute | solution.py:431
  5.9 0.0 copy-start.2
  5.9 0.9 copy-done.2
  6.8 0.9 copy-done.4
  7.8 0.7 copy-done.6
  8.5 0.7 copy-done.8
  9.1 0.7 prepare.1
  9.9 1.3 %collective-permute-done.1.far = bf16[384,256]{1,0:T(8,128)(2,1)S(1)} collective-permute-done((bf16[384,256]{1,0:T(8,128)(2,1)}, bf16[384,256]{1,0:T(8,128)(2,1)S(1)}, u32[]{:S(2)}, u32[]{:S(2)}) %collective-permute-start.1) | collective-permute-done | bytes 196640 | tf_op jit(solution)/shard_map/ppermute | solution.py:431
  11.2 2.9 %forward_conv.1 = (bf16[384,512]{1,0:T(8,128)(2,1)}, bf16[3,22,24,128]{3,2,1,0:T(8,128)(2,1)S(1)}) custom-call(s32[1]{0:T(128)} %bitcast.region, bf16[384,256]{1,0:T(8,128)(2,1)S(1)} %collective-permute-done.near, bf16[384,256]{1,0:T(8,128)(2,1)S(1)} %collective-permute-done.1.far, bf16[256,384]{1,0:T(8,128)(2,1)S(1)} %get-tuple-element.39.own_t, ...), custom_call_target="tpu_custom_call" | custom-call | flops 400000000 | bytes 2741764 | tf_op jit(solution)/shard_map/forward_conv/pallas_call | solution.py:412
  14.0 5.3 %all-to-all-start = ((bf16[16,24,512]{2,1,0:T(8,128)(2,1)}), bf16[16,24,512]{2,1,0:T(8,128)(2,1)S(1)}, u32[]{:S(2)}, u32[]{:S(2)}) async-start(bf16[16,24,512]{2,1,0:T(8,128)(2,1)} %bitcast.3), calls=%async_computation | async-start | bytes 786432 | tf_op jit(solution)/shard_map/all_to_all | solution.py:495
  19.5 1.3 %copy-done = bf16[1536,384]{1,0:T(8,128)(2,1)S(1)} copy-done((bf16[1536,384]{1,0:T(8,128)(2,1)S(1)}, bf16[1536,384]{1,0:T(8,128)(2,1)}, u32[]{:S(2)}) %copy-start) | copy-done | bytes 1179672
  20.8 1.3 %copy-done.1 = bf16[384,1536]{1,0:T(8,128)(2,1)S(1)} copy-done((bf16[384,1536]{1,0:T(8,128)(2,1)S(1)}, bf16[384,1536]{1,0:T(8,128)(2,1)}, u32[]{:S(2)}) %copy-start.1) | copy-done | bytes 1179672
  22.0 0.2 stage.1.matrices
  22.2 5.2 %all-to-all-done = bf16[16,24,512]{2,1,0:T(8,128)(2,1)S(1)} async-done(((bf16[16,24,512]{2,1,0:T(8,128)(2,1)}), bf16[16,24,512]{2,1,0:T(8,128)(2,1)S(1)}, u32[]{:S(2)}, u32[]{:S(2)}) %all-to-all-start) | async-done | bytes 393248 | tf_op jit(solution)/shard_map/all_to_all | solution.py:495
  27.4 2.3 %pixels_first.1 = (bf16[16,96,384]{2,1,0:T(8,128)(2,1)S(1)}, f32[384,256]{1,0:T(8,128)S(1)}, f32[384,256]{1,0:T(8,128)S(1)}, f32[384,128]{1,0:T(8,128)S(1)}) custom-call(s32[1]{0:T(128)} %bitcast.region, bf16[384,512]{1,0:T(8,128)(2,1)S(1)} %bitcast.16, f32[8,384]{1,0:T(8,128)S(1)} %concatenate.6.vectors, bf16[3072,384]{1,0:T(8,128)(2,1)S(1)} %stage.1.matrices), custom_call_target="tpu_custom_call" | custom-call | flops 1000000000 | bytes 4927492 | tf_op jit(solution)/shard_map/pixels_first/pallas_call | solution.py:412
  29.8 0.1 collective-permute-start.2
  29.9 2.3 %pixels_second.1 = (bf16[16,32,384]{2,1,0:T(8,128)(2,1)S(1)}, bf16[16,96,384]{2,1,0:T(8,128)(2,1)S(1)}, bf16[8,384]{1,0:T(8,128)(2,1)S(1)}) custom-call(s32[1]{0:T(128)} %bitcast.region, bf16[384,512]{1,0:T(8,128)(2,1)S(1)} %bitcast.17, f32[8,384]{1,0:T(8,128)S(1)} %concatenate.6.vectors, bf16[3072,384]{1,0:T(8,128)(2,1)S(1)} %stage.1.matrices, ...), custom_call_target="tpu_custom_call" | custom-call | flops 1000000000 | bytes 5326852 | tf_op jit(solution)/shard_map/pixels_second/pallas_call | solution.py:412
  32.1 0.6 collective-permute-done.2.second
  32.7 0.3 add_cores.1
  33.0 24.6 %all_to_all.21.received = bf16[16,128,384]{2,1,0:T(8,128)(2,1)S(1)} all-to-all(bf16[16,128,384]{2,1,0:T(8,128)(2,1)S(1)} %add_cores.1), channel_id=1, replica_groups=mesh['region'=16,'chan'=16] {'chan'}, dimensions={0} | all-to-all | bytes 3145728 | tf_op jit(solution)/shard_map/all_to_all | solution.py:529
  57.7 0.2 slice_reduce_fusion
  57.9 4.3 %collective-permute-start.3 = (bf16[104,384]{1,0:T(8,128)(2,1)S(1)}, bf16[104,384]{1,0:T(8,128)(2,1)S(1)}, u32[]{:S(2)}, u32[]{:S(2)}) collective-permute-start(bf16[104,384]{1,0:T(8,128)(2,1)S(1)} %pad_maximum_fusion.sent), channel_id=1, source_target_pairs={{0,32},{16,48},{32,0},{48,16},{64,96},{80,112},{96,64},{112,80},{1... | collective-permute-start | bytes 239624 | tf_op jit(solution)/shard_map/ppermute | solution.py:533
  62.2 2.2 %kernel_taps.1 = (bf16[384,256]{1,0:T(8,128)(2,1)}, bf16[384,256]{1,0:T(8,128)(2,1)S(1)}, bf16[8,384]{1,0:T(8,128)(2,1)S(1)}) custom-call(bf16[16,128,384]{2,1,0:T(8,128)(2,1)S(1)} %all_to_all.21.received, bf16[384,256]{1,0:T(8,128)(2,1)S(1)} %bitcast.21, bf16[3,22,24,128]{3,2,1,0:T(8,128)(2,1)S(1)} %get-tuple-element.51.pad_x), custom_call_target="tpu_custom_call" | custom-call | flops 400000000 | bytes 2574336 | tf_op jit(solution)/shard_map/kernel_taps/pallas_call | solution.py:412
  64.4 0.1 step.2.sent
  64.5 4.0 %collective-permute-start.4 = (bf16[112,384]{1,0:T(8,128)(2,1)S(1)}, bf16[112,384]{1,0:T(8,128)(2,1)S(1)}, u32[]{:S(2)}, u32[]{:S(2)}) collective-permute-start(bf16[112,384]{1,0:T(8,128)(2,1)S(1)} %step.2.sent), channel_id=1, source_target_pairs={{0,96},{16,112},{32,64},{48,80},{64,32},{80,48},{96,0},{112,16},{1... | collective-permute-start | bytes 258056 | tf_op jit(solution)/shard_map/ppermute | solution.py:545
  68.5 2.0 %collective-permute-done.4.got = bf16[112,384]{1,0:T(8,128)(2,1)S(1)} collective-permute-done((bf16[112,384]{1,0:T(8,128)(2,1)S(1)}, bf16[112,384]{1,0:T(8,128)(2,1)S(1)}, u32[]{:S(2)}, u32[]{:S(2)}) %collective-permute-start.4) | collective-permute-done | bytes 86048 | tf_op jit(solution)/shard_map/ppermute | solution.py:545
  70.5 0.1 step.3.sent
  70.6 3.8 %collective-permute-start.5 = (bf16[112,384]{1,0:T(8,128)(2,1)S(1)}, bf16[112,384]{1,0:T(8,128)(2,1)S(1)}, u32[]{:S(2)}, u32[]{:S(2)}) collective-permute-start(bf16[112,384]{1,0:T(8,128)(2,1)S(1)} %step.3.sent), channel_id=1, source_target_pairs={{0,224},{16,240},{32,192},{48,208},{64,160},{80,176},{96,128},{112... | collective-permute-start | bytes 258056 | tf_op jit(solution)/shard_map/ppermute | solution.py:547
  74.4 2.6 %collective-permute-done.5.got = bf16[112,384]{1,0:T(8,128)(2,1)S(1)} collective-permute-done((bf16[112,384]{1,0:T(8,128)(2,1)S(1)}, bf16[112,384]{1,0:T(8,128)(2,1)S(1)}, u32[]{:S(2)}, u32[]{:S(2)}) %collective-permute-start.5) | collective-permute-done | bytes 86048 | tf_op jit(solution)/shard_map/ppermute | solution.py:547
  77.0 1.2 %spread.1 = (bf16[16,104,384]{2,1,0:T(8,128)(2,1)}, f32[8,192]{1,0:T(8,128)S(1)}) custom-call(bf16[112,384]{1,0:T(8,128)(2,1)S(1)} %step.3.sent, bf16[112,384]{1,0:T(8,128)(2,1)S(1)} %collective-permute-done.5.got), custom_call_target="tpu_custom_call" | custom-call | flops 1000000 | bytes 1456128 | tf_op jit(solution)/shard_map/spread/pallas_call | solution.py:412
  78.2 0.0 copy-start.5
  78.2 0.0 copy-start.7
  78.2 0.0 copy-start.9
  78.3 3.8 %all-to-all-start.2 = ((bf16[16,104,384]{2,1,0:T(8,128)(2,1)}), bf16[16,104,384]{2,1,0:T(8,128)(2,1)S(1)}, u32[]{:S(2)}, u32[]{:S(2)}) async-start(bf16[16,104,384]{2,1,0:T(8,128)(2,1)} %get-tuple-element.55), calls=%async_computation.2 | async-start | bytes 2555904 | tf_op jit(solution)/shard_map/all_to_all | solution.py:552
  82.1 4.9 %collective-permute-start.9 = (bf16[384,256]{1,0:T(8,128)(2,1)S(1)}, bf16[384,256]{1,0:T(8,128)(2,1)S(1)}, u32[]{:S(2)}, u32[]{:S(2)}) collective-permute-start(bf16[384,256]{1,0:T(8,128)(2,1)S(1)} %get-tuple-element.57.own), channel_id=1, source_target_pairs={{0,16},{16,0},{32,48},{48,32},{64,80},{80,64},{96,112},{112,96},{1... | collective-permute-start | bytes 589832 | tf_op jit(solution)/shard_map/ppermute | solution.py:431
  87.0 2.6 %collective-permute-start.10 = (bf16[384,256]{1,0:T(8,128)(2,1)S(1)}, bf16[384,256]{1,0:T(8,128)(2,1)S(1)}, u32[]{:S(2)}, u32[]{:S(2)}) collective-permute-start(bf16[384,256]{1,0:T(8,128)(2,1)S(1)} %get-tuple-element.57.own), channel_id=1, source_target_pairs={{16,32},{32,16},{48,64},{64,48},{80,96},{96,80},{112,128},{128,112... | collective-permute-start | bytes 589832 | tf_op jit(solution)/shard_map/ppermute | solution.py:431
  89.6 0.2 collective-permute-start.7
  89.9 1.0 collective-permute-start.8
  90.8 0.8 collective-permute-start.6
  91.6 2.8 %collective-permute-done.10.far = bf16[384,256]{1,0:T(8,128)(2,1)S(1)} collective-permute-done((bf16[384,256]{1,0:T(8,128)(2,1)S(1)}, bf16[384,256]{1,0:T(8,128)(2,1)S(1)}, u32[]{:S(2)}, u32[]{:S(2)}) %collective-permute-start.10) | collective-permute-done | bytes 196640 | tf_op jit(solution)/shard_map/ppermute | solution.py:431
  94.5 3.4 %backward_conv.1 = bf16[384,256]{1,0:T(8,128)(2,1)} custom-call(s32[1]{0:T(128)} %bitcast.region, s32[8,16]{1,0:T(8,128)S(1)} %copy-done.9, bf16[384,256]{1,0:T(8,128)(2,1)S(1)} %get-tuple-element.57.own, bf16[384,256]{1,0:T(8,128)(2,1)S(1)} %collective-permute-done.9.near, bf16[384,256]{1,0:T(8,128)(2,1)S(1)} %collective-permute-done.10.far, ...), custom_call_target="tpu_custom_call" | custom-call | flops 400000000 | bytes 988260 | tf_op jit(solution)/shard_map/backward_conv/pallas_call | solution.py:412
  97.9 5.1 %collective-permute-start.11 = (bf16[16,104,384]{2,1,0:T(8,128)(2,1)S(1)}, bf16[16,104,384]{2,1,0:T(8,128)(2,1)S(1)}, u32[]{:S(2)}, u32[]{:S(2)}) collective-permute-start(bf16[16,104,384]{2,1,0:T(8,128)(2,1)S(1)} %all-to-all-done.2.ref), channel_id=1, source_target_pairs={{0,16},{16,0},{32,48},{48,32},{64,80},{80,64},{96,112},{112,96},{1... | collective-permute-start | bytes 3833864 | tf_op jit(solution)/shard_map/ppermute | solution.py:568
  103.0 0.1 reshape.81
  103.1 1.5 %place_own.1 = (f32[1536,384]{1,0:T(8,128)}, f32[384,1536]{1,0:T(8,128)}) custom-call(s32[1]{0:T(128)} %bitcast.region, bf16[16,104,384]{2,1,0:T(8,128)(2,1)S(1)} %all-to-all-done.2.ref), custom_call_target="tpu_custom_call" | custom-call | flops 1000000 | bytes 5996548 | tf_op jit(solution)/shard_map/place_own/pallas_call | solution.py:412
  104.6 0.6 slice_multiply_fusion
  105.2 0.4 collective-permute-done.11.ref
  105.6 1.6 %place_other.1 = (f32[1536,384]{1,0:T(8,128)}, f32[384,1536]{1,0:T(8,128)}, f32[1536]{0:T(1024)}, f32[384]{0:T(512)}, f32[384]{0:T(512)}, /*index=5*/f32[384]{0:T(512)}) custom-call(s32[1]{0:T(128)} %bitcast.region, bf16[16,104,384]{2,1,0:T(8,128)(2,1)S(1)} %collective-permute-done.11.ref, ...), custom_call_target="tpu_custom_call", output_to_operand_aliasing={{0}: (2, {}), {1}: (3, {})} | custom-call | flops 1000000 | bytes 10738180 | tf_op jit(solution)/shard_map/place_other/pallas_call | solution.py:412
  (35 shorter events, 0.1 us)
Async XLA Ops:
  0.6 9.2 %collective-permute-start = (bf16[384,256]{1,0:T(8,128)(2,1)}, bf16[384,256]{1,0:T(8,128)(2,1)S(1)}, u32[]{:S(2)}, u32[]{:S(2)}) collective-permute-start(bf16[384,256]{1,0:T(8,128)(2,1)} %bitcast.18), channel_id=1, source_target_pairs={{0,16},{16,0},{32,48},{48,32},{64,80},{80,64},{96,112},{112,96},{1... | collective-permute-start | bytes 589832 | tf_op jit(solution)/shard_map/ppermute | solution.py:431
  4.0 7.2 %collective-permute-start.1 = (bf16[384,256]{1,0:T(8,128)(2,1)}, bf16[384,256]{1,0:T(8,128)(2,1)S(1)}, u32[]{:S(2)}, u32[]{:S(2)}) collective-permute-start(bf16[384,256]{1,0:T(8,128)(2,1)} %bitcast.19), channel_id=1, source_target_pairs={{16,32},{32,16},{48,64},{64,48},{80,96},{96,80},{112,128},{128,112... | collective-permute-start | bytes 589832 | tf_op jit(solution)/shard_map/ppermute | solution.py:431
  5.9 0.9 copy-start.2
  6.8 0.9 copy-start.4
  7.8 0.7 copy-start.6
  8.5 0.7 copy-start.8
  11.2 8.2 %copy-start.10 = (f32[1536]{0:T(1024)S(1)}, f32[1536]{0:T(1024)}, u32[]{:S(2)}) copy-start(f32[1536]{0:T(1024)} %param.17) | copy-start | bytes 18436
  11.2 8.2 %copy-start.11 = (f32[384]{0:T(512)S(1)}, f32[384]{0:T(512)}, u32[]{:S(2)}) copy-start(f32[384]{0:T(512)} %param.14) | copy-start | bytes 4612
  11.2 8.3 %copy-start.12 = (f32[384]{0:T(512)S(1)}, f32[384]{0:T(512)}, u32[]{:S(2)}) copy-start(f32[384]{0:T(512)} %param.15) | copy-start | bytes 4612
  11.2 8.3 %copy-start.13 = (f32[384]{0:T(512)S(1)}, f32[384]{0:T(512)}, u32[]{:S(2)}) copy-start(f32[384]{0:T(512)} %param.19) | copy-start | bytes 4612
  14.0 13.4 %all-to-all-start = ((bf16[16,24,512]{2,1,0:T(8,128)(2,1)}), bf16[16,24,512]{2,1,0:T(8,128)(2,1)S(1)}, u32[]{:S(2)}, u32[]{:S(2)}) async-start(bf16[16,24,512]{2,1,0:T(8,128)(2,1)} %bitcast.3), calls=%async_computation | async-start | bytes 786432 | tf_op jit(solution)/shard_map/all_to_all | solution.py:495
  19.5 1.3 %copy-start = (bf16[1536,384]{1,0:T(8,128)(2,1)S(1)}, bf16[1536,384]{1,0:T(8,128)(2,1)}, u32[]{:S(2)}) copy-start(bf16[1536,384]{1,0:T(8,128)(2,1)} %weight_in.1) | copy-start | bytes 3538948
  20.8 1.3 %copy-start.1 = (bf16[384,1536]{1,0:T(8,128)(2,1)S(1)}, bf16[384,1536]{1,0:T(8,128)(2,1)}, u32[]{:S(2)}) copy-start(bf16[384,1536]{1,0:T(8,128)(2,1)} %weight_out.1) | copy-start | bytes 3538948
  29.8 2.9 %collective-permute-start.2 = (bf16[16,96,384]{2,1,0:T(8,128)(2,1)S(1)}, bf16[16,96,384]{2,1,0:T(8,128)(2,1)S(1)}, u32[]{:S(2)}, u32[]{:S(2)}) collective-permute-start(bf16[16,96,384]{2,1,0:T(8,128)(2,1)S(1)} %get-tuple-element.50), channel_id=1, source_target_pairs={{0,16},{16,0},{32,48},{48,32},{64,80},{80,64},{96,112},{112,96},{1... | collective-permute-start | bytes 3538952 | tf_op jit(solution)/shard_map/ppermute | solution.py:515
  57.7 4.5 %copy-start.3 = (bf16[24,16,256]{2,1,0:T(8,128)(2,1)S(1)}, bf16[24,16,256]{2,1,0:T(8,128)(2,1)}, u32[]{:S(2)}) copy-start(bf16[24,16,256]{2,1,0:T(8,128)(2,1)} %param.10) | copy-start | bytes 589828
  57.9 6.5 %collective-permute-start.3 = (bf16[104,384]{1,0:T(8,128)(2,1)S(1)}, bf16[104,384]{1,0:T(8,128)(2,1)S(1)}, u32[]{:S(2)}, u32[]{:S(2)}) collective-permute-start(bf16[104,384]{1,0:T(8,128)(2,1)S(1)} %pad_maximum_fusion.sent), channel_id=1, source_target_pairs={{0,32},{16,48},{32,0},{48,16},{64,96},{80,112},{96,64},{112,80},{1... | collective-permute-start | bytes 239624 | tf_op jit(solution)/shard_map/ppermute | solution.py:533
  64.5 6.0 %collective-permute-start.4 = (bf16[112,384]{1,0:T(8,128)(2,1)S(1)}, bf16[112,384]{1,0:T(8,128)(2,1)S(1)}, u32[]{:S(2)}, u32[]{:S(2)}) collective-permute-start(bf16[112,384]{1,0:T(8,128)(2,1)S(1)} %step.2.sent), channel_id=1, source_target_pairs={{0,96},{16,112},{32,64},{48,80},{64,32},{80,48},{96,0},{112,16},{1... | collective-permute-start | bytes 258056 | tf_op jit(solution)/shard_map/ppermute | solution.py:545
  70.6 6.4 %collective-permute-start.5 = (bf16[112,384]{1,0:T(8,128)(2,1)S(1)}, bf16[112,384]{1,0:T(8,128)(2,1)S(1)}, u32[]{:S(2)}, u32[]{:S(2)}) collective-permute-start(bf16[112,384]{1,0:T(8,128)(2,1)S(1)} %step.3.sent), channel_id=1, source_target_pairs={{0,224},{16,240},{32,192},{48,208},{64,160},{80,176},{96,128},{112... | collective-permute-start | bytes 258056 | tf_op jit(solution)/shard_map/ppermute | solution.py:547
  78.2 16.2 %copy-start.5 = (bf16[24,16,256]{2,1,0:T(8,128)(2,1)S(1)}, bf16[24,16,256]{2,1,0:T(8,128)(2,1)}, u32[]{:S(2)}) copy-start(bf16[24,16,256]{2,1,0:T(8,128)(2,1)} %param.11) | copy-start | bytes 589828
  78.2 16.2 %copy-start.7 = (f32[24,49]{1,0:T(8,128)S(1)}, f32[24,49]{1,0:T(8,128)}, u32[]{:S(2)}) copy-start(f32[24,49]{1,0:T(8,128)} %kernel.3) | copy-start | bytes 14116
  78.2 16.2 %copy-start.9 = (s32[8,16]{1,0:T(8,128)S(1)}, s32[8,16]{1,0:T(8,128)}, u32[]{:S(2)}) copy-start(s32[8,16]{1,0:T(8,128)} %neighbours.3) | copy-start | bytes 1540
  78.3 19.6 %all-to-all-start.2 = ((bf16[16,104,384]{2,1,0:T(8,128)(2,1)}), bf16[16,104,384]{2,1,0:T(8,128)(2,1)S(1)}, u32[]{:S(2)}, u32[]{:S(2)}) async-start(bf16[16,104,384]{2,1,0:T(8,128)(2,1)} %get-tuple-element.55), calls=%async_computation.2 | async-start | bytes 2555904 | tf_op jit(solution)/shard_map/all_to_all | solution.py:552
  82.1 9.5 %collective-permute-start.9 = (bf16[384,256]{1,0:T(8,128)(2,1)S(1)}, bf16[384,256]{1,0:T(8,128)(2,1)S(1)}, u32[]{:S(2)}, u32[]{:S(2)}) collective-permute-start(bf16[384,256]{1,0:T(8,128)(2,1)S(1)} %get-tuple-element.57.own), channel_id=1, source_target_pairs={{0,16},{16,0},{32,48},{48,32},{64,80},{80,64},{96,112},{112,96},{1... | collective-permute-start | bytes 589832 | tf_op jit(solution)/shard_map/ppermute | solution.py:431
  87.0 7.4 %collective-permute-start.10 = (bf16[384,256]{1,0:T(8,128)(2,1)S(1)}, bf16[384,256]{1,0:T(8,128)(2,1)S(1)}, u32[]{:S(2)}, u32[]{:S(2)}) collective-permute-start(bf16[384,256]{1,0:T(8,128)(2,1)S(1)} %get-tuple-element.57.own), channel_id=1, source_target_pairs={{16,32},{32,16},{48,64},{64,48},{80,96},{96,80},{112,128},{128,112... | collective-permute-start | bytes 589832 | tf_op jit(solution)/shard_map/ppermute | solution.py:431
  89.6 8.2 %collective-permute-start.7 = (f32[8,192]{1,0:T(8,128)S(1)}, f32[8,192]{1,0:T(8,128)S(1)}, u32[]{:S(2)}, u32[]{:S(2)}) collective-permute-start(f32[8,192]{1,0:T(8,128)S(1)} %get-tuple-element.56), channel_id=1, source_target_pairs={{0,32},{16,48},{32,0},{48,16},{64,96},{80,112},{96,64},{112,80},{1... | collective-permute-start | bytes 18440 | tf_op jit(solution)/shard_map/ppermute | solution.py:444
  89.9 8.0 %collective-permute-start.8 = (f32[8,192]{1,0:T(8,128)S(1)}, f32[8,192]{1,0:T(8,128)S(1)}, u32[]{:S(2)}, u32[]{:S(2)}) collective-permute-start(f32[8,192]{1,0:T(8,128)S(1)} %get-tuple-element.56), channel_id=1, source_target_pairs={{0,48},{16,32},{32,16},{48,0},{64,112},{80,96},{96,80},{112,64},{1... | collective-permute-start | bytes 18440 | tf_op jit(solution)/shard_map/ppermute | solution.py:444
  90.8 7.0 %collective-permute-start.6 = (f32[8,192]{1,0:T(8,128)S(1)}, f32[8,192]{1,0:T(8,128)S(1)}, u32[]{:S(2)}, u32[]{:S(2)}) collective-permute-start(f32[8,192]{1,0:T(8,128)S(1)} %get-tuple-element.56), channel_id=1, source_target_pairs={{0,16},{16,0},{32,48},{48,32},{64,80},{80,64},{96,112},{112,96},{1... | collective-permute-start | bytes 18440 | tf_op jit(solution)/shard_map/ppermute | solution.py:444
  97.9 7.7 %collective-permute-start.11 = (bf16[16,104,384]{2,1,0:T(8,128)(2,1)S(1)}, bf16[16,104,384]{2,1,0:T(8,128)(2,1)S(1)}, u32[]{:S(2)}, u32[]{:S(2)}) collective-permute-start(bf16[16,104,384]{2,1,0:T(8,128)(2,1)S(1)} %all-to-all-done.2.ref), channel_id=1, source_target_pairs={{0,16},{16,0},{32,48},{48,32},{64,80},{80,64},{96,112},{112,96},{1... | collective-permute-start | bytes 3833864 | tf_op jit(solution)/shard_map/ppermute | solution.py:568

commit v6 on v5

--- a/solution.py
+++ b/solution.py
@@ -85,8 +85,8 @@
         pad[g, 3:19, 19:22, :] = side[:, 128:256].reshape(16, 16, 128)[:, 0:3]
 
 
-def lookup_rows(region, neighbours, total):
-    raw = neighbours[...]
+def lookup_rows(region, tables, total):
+    raw = tables[CH:, 0:TILE].astype(jnp.int32)
     place = jnp.where(raw >= total, 3 * TILE, raw - (region[0] - 1) * TILE)
     repeat = ((iota((TILE, 128), 1) & 15) == iota((TILE, 128), 0)).astype(F32)
     return dot(place.astype(F32), repeat).astype(jnp.int32)
@@ -130,10 +130,10 @@
 
 
 def prepare_kernel(
-    total, region, neighbours, own, kernel, cotangent, own_t, upstream, weights, picks, order
-):
-    spread_taps(kernel[...], weights)
-    picks[...] = one_hots(lookup_rows(region, neighbours, total))
+    total, region, tables, own, cotangent, own_t, upstream, weights, picks, order
+):
+    spread_taps(tables[0:CH, 0:49], weights)
+    picks[...] = one_hots(lookup_rows(region, tables, total))
     order[...] = tile_major()
     own_t[...] = dot(eye(PIX), own[...], NT).astype(BF)
     upstream[...] = dot(order[...], cotangent[...]).astype(BF)
@@ -163,7 +163,7 @@
 
 
 def taps_kernel(
-    received, features, pad_x, output, grad, kernel_grad, unpacked, gradient, sums, pad
+    received, pad_x, branch, grad, kernel_grad, unpacked, gradient, sums, pad
 ):
     for t in range(TILE):
         part = received[t, 0:BRANCH, :].astype(F32)
@@ -173,7 +173,7 @@
             piece = part[CH:, i * 128 : (i + 1) * 128]
             unpacked[t * CH + 8 * i : t * CH + 8 * (i + 1), 384:512] = piece
     both = dot(chan_major(), unpacked[...].astype(BF))
-    output[...] = (features[...].astype(F32) + both[:, :PIX]).astype(BF)
+    branch[...] = both[:, :PIX].astype(BF)
     own_grad = both[:, PIX:].astype(BF)
     grad[...] = own_grad
     own = dot(eye(PIX), own_grad, NT)
@@ -213,11 +213,12 @@
 
 
 def backward_kernel(
-    total, region, neighbours, own, near, far, kernel, cotangent, input_grad,
-    pad, result, weights, picks,
-):
-    spread_taps(kernel[...], weights)
-    picks[...] = one_hots(lookup_rows(region, neighbours, total))
+    total, region, tables, own, near, far, cotangent, features, branch,
+    input_grad, output, pad, result, weights, picks,
+):
+    output[...] = (features[...].astype(F32) + branch[...].astype(F32)).astype(BF)
+    spread_taps(tables[0:CH, 0:49], weights)
+    picks[...] = one_hots(lookup_rows(region, tables, total))
     own_t = dot(eye(PIX), own[...], NT).astype(BF)
     fill_padded(pad, own_t, *sides_of(region, near, far), picks)
     convolve(pad, weights, result, True)
@@ -272,12 +273,14 @@
 
 def first_half_kernel(
     region, columns, vectors, matrices,
-    parts, mixed_sum, grad_sum, small_sum, bias,
+    parts, mixed_sum, grad_sum, small_sum, inputs_ref, mixed_ref, bias,
 ):
     table = jnp.transpose(vectors[...])
     normed, _ = normalize(columns)
     inputs = (normed * table[:, 4:5] + table[:, 5:6]).astype(BF)
     grad_mixed = (table[:, 6:7] * columns[:, PIX:].astype(F32)).astype(BF)
+    inputs_ref[...] = inputs
+    mixed_ref[...] = grad_mixed
     zeros = jnp.zeros((C, PIX), F32)
     mixed_sum[...], grad_sum[...], small_sum[...] = hidden_blocks(
         1 - (region[0] & 1), table, inputs, grad_mixed, bias,
@@ -287,19 +290,17 @@
 
 def second_half_kernel(
     region, columns, vectors, matrices,
-    mixed_sum, grad_sum, small_sum, out, parts, extra, bias,
+    mixed_sum, grad_sum, small_sum, inputs, grad_mixed, out, parts, extra, bias,
 ):
     table = jnp.transpose(vectors[...])
     gain = table[:, 4:5]
     scale = table[:, 6:7]
+    mixed_out, grad_inputs, small = hidden_blocks(
+        region[0] & 1, table, inputs[...], grad_mixed[...], bias,
+        matrices, parts, mixed_sum[...], grad_sum[...], small_sum[...],
+    )
     normed, inv_std = normalize(columns)
-    inputs = (normed * gain + table[:, 5:6]).astype(BF)
     upstream = columns[:, PIX:].astype(F32)
-    grad_mixed = (scale * upstream).astype(BF)
-    mixed_out, grad_inputs, small = hidden_blocks(
-        region[0] & 1, table, inputs, grad_mixed, bias,
-        matrices, parts, mixed_sum[...], grad_sum[...], small_sum[...],
-    )
     branch = scale * mixed_out
     grad_scale = jnp.sum(upstream * mixed_out, axis=1, keepdims=True)
     grad_gain = jnp.sum(grad_inputs * normed, axis=1, keepdims=True)
@@ -428,7 +429,8 @@
     count = lax.axis_size("region")
     near = [(i, i ^ 1) for i in range(count)]
     far = [(i, ((i + 1) ^ 1) - 1) for i in range(1, count - 1)]
-    return lax.ppermute(field, "region", near), lax.ppermute(field, "region", far)
+    across = lax.ppermute(field, "region", far)
+    return lax.ppermute(field, "region", near), across
 
 
 def cube_pairs(count, bit, core=0):
@@ -471,11 +473,14 @@
     square = ((3, 16, 16, 128), F32)
     taps = ((3, 49, 128), F32)
     block = ((ROWS, PIX), BF)
+    tables = jnp.pad(kernel, ((0, 8), (0, 0))) + jnp.pad(
+        neighbours, ((CH, 0), (0, 49 - TILE))
+    ).astype(F32)
     ready = call(
         functools.partial(prepare_kernel, total_tiles),
         [((PIX, ROWS), BF), block, taps, ((ROWS, 1024), BF), ((ROWS, ROWS), BF)],
         [],
-        (region, neighbours, x, kernel, upstream),
+        (region, tables, x, upstream),
         "prepare",
         200_000_000,
         16,
@@ -501,7 +506,7 @@
     halves = (16, PART, C)
     pixels = (region, columns, vectors, *staged)
     scratch = [((HID, 1), F32)]
-    sums = [((C, PIX), F32), ((C, PIX), F32), ((C, 128), F32)]
+    sums = [((C, PIX), F32), ((C, PIX), F32), ((C, 128), F32), ((C, PIX), BF), ((C, PIX), BF)]
     send, *partial = call(
         first_half_kernel,
         [(halves, BF)] + sums,
@@ -531,11 +536,11 @@
     sent = jnp.sum(travel[:, BRANCH:].astype(F32), axis=0).astype(BF)
     sent = jnp.concatenate([sent, extra], axis=0)
     got = lax.ppermute(sent, "region", cube_pairs(count, 1))
-    output, grad, kernel_part = call(
+    branch, grad, kernel_part = call(
         taps_kernel,
         [((ROWS, PIX), BF), ((ROWS, PIX), BF), ((8, C), BF)],
         [((ROWS, 2 * PIX), F32), square, ((3, 64, 128), F32), padded],
-        (travel, x, pad_x),
+        (travel, pad_x),
         "kernel_taps",
         400_000_000,
         16,
@@ -553,11 +558,11 @@
 
     grad_near, grad_far = both_sides(grad)
     kernel_part = sum_four(kernel_part, swap, cube_pairs(count, 1), cube_pairs(count, 1, 1))
-    (input_grad,) = call(
+    input_grad, output = call(
         functools.partial(backward_kernel, total_tiles),
-        [block],
+        [block, block],
         [padded, square, taps, ((ROWS, 1024), BF)],
-        (region, neighbours, grad, grad_near, grad_far, kernel, upstream),
+        (region, tables, grad, grad_near, grad_far, upstream, x, branch),
         "backward_conv",
         400_000_000,
         16,

time: 108 us -> 108 us (level)
  local copies, waits for them, and re-layouts: 5.95 us -> 4.55 us
    unnamed x28 -> x20, local copies, waits for them, and re-layouts: 5.82 us -> 4.41 us
where the time goes in v6:
time: 108 us; the launch traced here: 107 us
  starting transfers between devices  41.2 us (38%)
  blocking collectives  24.6 us (23%)
  Pallas kernels  18.8 us (17%)
  waiting for transfers between devices  15.6 us (14%)
  local copies, waits for them, and re-layouts  4.55 us (4%)
  other arithmetic  1.53 us (1%)
    all_to_all x1, blocking collectives, per_device(): lax.all_to_all(travel, 'chan', split_axis=0, concat_axis=0, tiled=True)  24.6 us
    pallas_call x13, Pallas kernels, call(): pl.pallas_call(body, out_shape=[jax.ShapeDtypeStruct(s, d) for s, d in sh...  18.8 us
    ppermute x2, starting transfers between devices, both_sides(): return (lax.ppermute(field, 'region', near), across)  8.21 us
    all_to_all x1, waiting for transfers between devices, per_device(): lax.all_to_all(columns, 'chan', split_axis=0, concat_axis=0, tiled=True)  5.1 us
    ppermute x1, starting transfers between devices, per_device(): other = lax.ppermute(mine, 'region', swap)  5.04 us
    all_to_all x1, starting transfers between devices, per_device(): lax.all_to_all(columns, 'chan', split_axis=0, concat_axis=0, tiled=True)  5.03 us
    ppermute x2, waiting for transfers between devices, both_sides(): across = lax.ppermute(field, 'region', far)  4.81 us
    ppermute x2, starting transfers between devices, both_sides(): across = lax.ppermute(field, 'region', far)  4.55 us
  transfers between devices with their start and end apart: 14, of which 7 were waited for; matrix products, arithmetic and copies ran while one was open for 1% of the time, Pallas kernels for 10%

profile of v6, /device:TPU:1, one launch (start us, length us, event | category | flops | bytes accessed | tf_op | source)
XLA Modules:
  0.0 107.3 jit_solution(6762391421806347397)
XLA Ops:
  0.6 3.3 %collective-permute-start = (bf16[384,256]{1,0:T(8,128)(2,1)}, bf16[384,256]{1,0:T(8,128)(2,1)S(1)}, u32[]{:S(2)}, u32[]{:S(2)}) collective-permute-start(bf16[384,256]{1,0:T(8,128)(2,1)} %bitcast.18), channel_id=1, source_target_pairs={{0,16},{16,0},{32,48},{48,32},{64,80},{80,64},{96,112},{112,96},{1... | collective-permute-start | bytes 589832 | tf_op jit(solution)/shard_map/ppermute | solution.py:433
  4.0 1.9 %collective-permute-start.1 = (bf16[384,256]{1,0:T(8,128)(2,1)}, bf16[384,256]{1,0:T(8,128)(2,1)S(1)}, u32[]{:S(2)}, u32[]{:S(2)}) collective-permute-start(bf16[384,256]{1,0:T(8,128)(2,1)} %bitcast.19), channel_id=1, source_target_pairs={{16,32},{32,16},{48,64},{64,48},{80,96},{96,80},{112,128},{128,112... | collective-permute-start | bytes 589832 | tf_op jit(solution)/shard_map/ppermute | solution.py:432
  5.9 0.7 convert_add_fusion.tables
  6.6 0.9 copy-done.2
  7.6 0.9 copy-done.4
  8.5 0.7 prepare.1
  9.2 0.0 collective-permute-done.near
  9.2 2.0 %collective-permute-done.1.far = bf16[384,256]{1,0:T(8,128)(2,1)S(1)} collective-permute-done((bf16[384,256]{1,0:T(8,128)(2,1)}, bf16[384,256]{1,0:T(8,128)(2,1)S(1)}, u32[]{:S(2)}, u32[]{:S(2)}) %collective-permute-start.1) | collective-permute-done | bytes 196640 | tf_op jit(solution)/shard_map/ppermute | solution.py:432
  11.2 2.9 %forward_conv.1 = (bf16[384,512]{1,0:T(8,128)(2,1)}, bf16[3,22,24,128]{3,2,1,0:T(8,128)(2,1)S(1)}) custom-call(s32[1]{0:T(128)} %bitcast.region, bf16[384,256]{1,0:T(8,128)(2,1)S(1)} %collective-permute-done.near, bf16[384,256]{1,0:T(8,128)(2,1)S(1)} %collective-permute-done.1.far, bf16[256,384]{1,0:T(8,128)(2,1)S(1)} %get-tuple-element.43.own_t, ...), custom_call_target="tpu_custom_call" | custom-call | flops 400000000 | bytes 2741764 | tf_op jit(solution)/shard_map/forward_conv/pallas_call | solution.py:413
  14.0 5.0 %all-to-all-start = ((bf16[16,24,512]{2,1,0:T(8,128)(2,1)}), bf16[16,24,512]{2,1,0:T(8,128)(2,1)S(1)}, u32[]{:S(2)}, u32[]{:S(2)}) async-start(bf16[16,24,512]{2,1,0:T(8,128)(2,1)} %bitcast.3), calls=%async_computation | async-start | bytes 786432 | tf_op jit(solution)/shard_map/all_to_all | solution.py:500
  19.2 1.3 %copy-done = bf16[1536,384]{1,0:T(8,128)(2,1)S(1)} copy-done((bf16[1536,384]{1,0:T(8,128)(2,1)S(1)}, bf16[1536,384]{1,0:T(8,128)(2,1)}, u32[]{:S(2)}) %copy-start) | copy-done | bytes 1179672
  20.5 1.3 %copy-done.1 = bf16[384,1536]{1,0:T(8,128)(2,1)S(1)} copy-done((bf16[384,1536]{1,0:T(8,128)(2,1)S(1)}, bf16[384,1536]{1,0:T(8,128)(2,1)}, u32[]{:S(2)}) %copy-start.1) | copy-done | bytes 1179672
  21.8 0.2 stage.1.matrices
  22.0 5.1 %all-to-all-done = bf16[16,24,512]{2,1,0:T(8,128)(2,1)S(1)} async-done(((bf16[16,24,512]{2,1,0:T(8,128)(2,1)}), bf16[16,24,512]{2,1,0:T(8,128)(2,1)S(1)}, u32[]{:S(2)}, u32[]{:S(2)}) %all-to-all-start) | async-done | bytes 393248 | tf_op jit(solution)/shard_map/all_to_all | solution.py:500
  27.1 2.3 %pixels_first.1 = (bf16[16,96,384]{2,1,0:T(8,128)(2,1)S(1)}, f32[384,256]{1,0:T(8,128)S(1)}, f32[384,256]{1,0:T(8,128)S(1)}, f32[384,128]{1,0:T(8,128)S(1)}, bf1...) custom-call(s32[1]{0:T(128)} %bitcast.region, bf16[384,512]{1,0:T(8,128)(2,1)S(1)} %bitcast.16, ...), custom_call_target="tpu_custom_call" | custom-call | flops 1000000000 | bytes 5320708 | tf_op jit(solution)/shard_map/pixels_first/pallas_call | solution.py:413
  29.4 0.1 collective-permute-start.2
  29.5 2.2 %pixels_second.1 = (bf16[16,32,384]{2,1,0:T(8,128)(2,1)S(1)}, bf16[16,96,384]{2,1,0:T(8,128)(2,1)S(1)}, bf16[8,384]{1,0:T(8,128)(2,1)S(1)}) custom-call(s32[1]{0:T(128)} %bitcast.region, bf16[384,512]{1,0:T(8,128)(2,1)S(1)} %bitcast.17, f32[8,384]{1,0:T(8,128)S(1)} %concatenate.6.vectors, bf16[3072,384]{1,0:T(8,128)(2,1)S(1)} %stage.1.matrices, ...), custom_call_target="tpu_custom_call" | custom-call | flops 1000000000 | bytes 5720068 | tf_op jit(solution)/shard_map/pixels_second/pallas_call | solution.py:413
  31.7 0.6 collective-permute-done.2.second
  32.3 0.3 add_cores.1
  32.7 24.6 %all_to_all.21.received = bf16[16,128,384]{2,1,0:T(8,128)(2,1)S(1)} all-to-all(bf16[16,128,384]{2,1,0:T(8,128)(2,1)S(1)} %add_cores.1), channel_id=1, replica_groups=mesh['region'=16,'chan'=16] {'chan'}, dimensions={0} | all-to-all | bytes 3145728 | tf_op jit(solution)/shard_map/all_to_all | solution.py:534
  57.3 0.2 slice_reduce_fusion
  57.5 4.4 %collective-permute-start.5 = (bf16[104,384]{1,0:T(8,128)(2,1)S(1)}, bf16[104,384]{1,0:T(8,128)(2,1)S(1)}, u32[]{:S(2)}, u32[]{:S(2)}) collective-permute-start(bf16[104,384]{1,0:T(8,128)(2,1)S(1)} %pad_maximum_fusion.sent), channel_id=1, source_target_pairs={{0,32},{16,48},{32,0},{48,16},{64,96},{80,112},{96,64},{112,80},{1... | collective-permute-start | bytes 239624 | tf_op jit(solution)/shard_map/ppermute | solution.py:538
  61.9 2.2 %kernel_taps.1 = (bf16[384,256]{1,0:T(8,128)(2,1)S(1)}, bf16[384,256]{1,0:T(8,128)(2,1)S(1)}, bf16[8,384]{1,0:T(8,128)(2,1)S(1)}) custom-call(bf16[16,128,384]{2,1,0:T(8,128)(2,1)S(1)} %all_to_all.21.received, bf16[3,22,24,128]{3,2,1,0:T(8,128)(2,1)S(1)} %get-tuple-element.57.pad_x), custom_call_target="tpu_custom_call" | custom-call | flops 400000000 | bytes 2377728 | tf_op jit(solution)/shard_map/kernel_taps/pallas_call | solution.py:413
  64.1 0.1 step.2.sent
  64.2 4.4 %collective-permute-start.6 = (bf16[112,384]{1,0:T(8,128)(2,1)S(1)}, bf16[112,384]{1,0:T(8,128)(2,1)S(1)}, u32[]{:S(2)}, u32[]{:S(2)}) collective-permute-start(bf16[112,384]{1,0:T(8,128)(2,1)S(1)} %step.2.sent), channel_id=1, source_target_pairs={{0,96},{16,112},{32,64},{48,80},{64,32},{80,48},{96,0},{112,16},{1... | collective-permute-start | bytes 258056 | tf_op jit(solution)/shard_map/ppermute | solution.py:550
  68.5 2.0 %collective-permute-done.6.got = bf16[112,384]{1,0:T(8,128)(2,1)S(1)} collective-permute-done((bf16[112,384]{1,0:T(8,128)(2,1)S(1)}, bf16[112,384]{1,0:T(8,128)(2,1)S(1)}, u32[]{:S(2)}, u32[]{:S(2)}) %collective-permute-start.6) | collective-permute-done | bytes 86048 | tf_op jit(solution)/shard_map/ppermute | solution.py:550
  70.5 0.1 step.3.sent
  70.7 3.7 %collective-permute-start.7 = (bf16[112,384]{1,0:T(8,128)(2,1)S(1)}, bf16[112,384]{1,0:T(8,128)(2,1)S(1)}, u32[]{:S(2)}, u32[]{:S(2)}) collective-permute-start(bf16[112,384]{1,0:T(8,128)(2,1)S(1)} %step.3.sent), channel_id=1, source_target_pairs={{0,224},{16,240},{32,192},{48,208},{64,160},{80,176},{96,128},{112... | collective-permute-start | bytes 258056 | tf_op jit(solution)/shard_map/ppermute | solution.py:552
  74.4 2.6 %collective-permute-done.7.got = bf16[112,384]{1,0:T(8,128)(2,1)S(1)} collective-permute-done((bf16[112,384]{1,0:T(8,128)(2,1)S(1)}, bf16[112,384]{1,0:T(8,128)(2,1)S(1)}, u32[]{:S(2)}, u32[]{:S(2)}) %collective-permute-start.7) | collective-permute-done | bytes 86048 | tf_op jit(solution)/shard_map/ppermute | solution.py:552
  77.0 1.2 %spread.1 = (bf16[16,104,384]{2,1,0:T(8,128)(2,1)}, f32[8,192]{1,0:T(8,128)S(1)}) custom-call(bf16[112,384]{1,0:T(8,128)(2,1)S(1)} %step.3.sent, bf16[112,384]{1,0:T(8,128)(2,1)S(1)} %collective-permute-done.7.got), custom_call_target="tpu_custom_call" | custom-call | flops 1000000 | bytes 1456128 | tf_op jit(solution)/shard_map/spread/pallas_call | solution.py:413
  78.2 0.0 copy-start.3
  78.2 0.0 copy-start.5
  78.2 3.8 %all-to-all-start.2 = ((bf16[16,104,384]{2,1,0:T(8,128)(2,1)}), bf16[16,104,384]{2,1,0:T(8,128)(2,1)S(1)}, u32[]{:S(2)}, u32[]{:S(2)}) async-start(bf16[16,104,384]{2,1,0:T(8,128)(2,1)} %get-tuple-element.63), calls=%async_computation.2 | async-start | bytes 2555904 | tf_op jit(solution)/shard_map/all_to_all | solution.py:557
  82.1 4.9 %collective-permute-start.3 = (bf16[384,256]{1,0:T(8,128)(2,1)S(1)}, bf16[384,256]{1,0:T(8,128)(2,1)S(1)}, u32[]{:S(2)}, u32[]{:S(2)}) collective-permute-start(bf16[384,256]{1,0:T(8,128)(2,1)S(1)} %get-tuple-element.58.own), channel_id=1, source_target_pairs={{0,16},{16,0},{32,48},{48,32},{64,80},{80,64},{96,112},{112,96},{1... | collective-permute-start | bytes 589832 | tf_op jit(solution)/shard_map/ppermute | solution.py:433
  87.0 2.6 %collective-permute-start.4 = (bf16[384,256]{1,0:T(8,128)(2,1)S(1)}, bf16[384,256]{1,0:T(8,128)(2,1)S(1)}, u32[]{:S(2)}, u32[]{:S(2)}) collective-permute-start(bf16[384,256]{1,0:T(8,128)(2,1)S(1)} %get-tuple-element.58.own), channel_id=1, source_target_pairs={{16,32},{32,16},{48,64},{64,48},{80,96},{96,80},{112,128},{128,112... | collective-permute-start | bytes 589832 | tf_op jit(solution)/shard_map/ppermute | solution.py:432
  89.6 0.2 collective-permute-start.9
  89.8 1.0 collective-permute-start.10
  90.8 0.8 collective-permute-start.8
  91.6 0.0 collective-permute-done.3.near
  91.6 2.8 %collective-permute-done.4.far = bf16[384,256]{1,0:T(8,128)(2,1)S(1)} collective-permute-done((bf16[384,256]{1,0:T(8,128)(2,1)S(1)}, bf16[384,256]{1,0:T(8,128)(2,1)S(1)}, u32[]{:S(2)}, u32[]{:S(2)}) %collective-permute-start.4) | collective-permute-done | bytes 196640 | tf_op jit(solution)/shard_map/ppermute | solution.py:432
  94.4 3.5 %backward_conv.1 = (bf16[384,256]{1,0:T(8,128)(2,1)}, bf16[384,256]{1,0:T(8,128)(2,1)}) custom-call(s32[1]{0:T(128)} %bitcast.region, f32[32,49]{1,0:T(8,128)S(1)} %convert_add_fusion.tables, bf16[384,256]{1,0:T(8,128)(2,1)S(1)} %get-tuple-element.58.own, bf16[384,256]{1,0:T(8,128)(2,1)S(1)} %collective-permute-done.3.near, ...), custom_call_target="tpu_custom_call" | custom-call | flops 400000000 | bytes 1579140 | tf_op jit(solution)/shard_map/backward_conv/pallas_call | solution.py:413
  97.9 0.0 collective-permute-done.9
  97.9 5.0 %collective-permute-start.11 = (bf16[16,104,384]{2,1,0:T(8,128)(2,1)S(1)}, bf16[16,104,384]{2,1,0:T(8,128)(2,1)S(1)}, u32[]{:S(2)}, u32[]{:S(2)}) collective-permute-start(bf16[16,104,384]{2,1,0:T(8,128)(2,1)S(1)} %all-to-all-done.2.ref), channel_id=1, source_target_pairs={{0,16},{16,0},{32,48},{48,32},{64,80},{80,64},{96,112},{112,96},{1... | collective-permute-start | bytes 3833864 | tf_op jit(solution)/shard_map/ppermute | solution.py:573
  103.0 0.1 reshape.81
  103.1 1.5 %place_own.1 = (f32[1536,384]{1,0:T(8,128)}, f32[384,1536]{1,0:T(8,128)}) custom-call(s32[1]{0:T(128)} %bitcast.region, bf16[16,104,384]{2,1,0:T(8,128)(2,1)S(1)} %all-to-all-done.2.ref), custom_call_target="tpu_custom_call" | custom-call | flops 1000000 | bytes 5996548 | tf_op jit(solution)/shard_map/place_own/pallas_call | solution.py:413
  104.6 0.6 slice_multiply_fusion
  105.2 0.4 collective-permute-done.11.ref
  105.6 1.6 %place_other.1 = (f32[1536,384]{1,0:T(8,128)}, f32[384,1536]{1,0:T(8,128)}, f32[1536]{0:T(1024)}, f32[384]{0:T(512)}, f32[384]{0:T(512)}, /*index=5*/f32[384]{0:T(512)}) custom-call(s32[1]{0:T(128)} %bitcast.region, bf16[16,104,384]{2,1,0:T(8,128)(2,1)S(1)} %collective-permute-done.11.ref, ...), custom_call_target="tpu_custom_call", output_to_operand_aliasing={{0}: (2, {}), {1}: (3, {})} | custom-call | flops 1000000 | bytes 10738180 | tf_op jit(solution)/shard_map/place_other/pallas_call | solution.py:413
  (28 shorter events, 0.1 us)
Async XLA Ops:
  0.6 8.5 %collective-permute-start = (bf16[384,256]{1,0:T(8,128)(2,1)}, bf16[384,256]{1,0:T(8,128)(2,1)S(1)}, u32[]{:S(2)}, u32[]{:S(2)}) collective-permute-start(bf16[384,256]{1,0:T(8,128)(2,1)} %bitcast.18), channel_id=1, source_target_pairs={{0,16},{16,0},{32,48},{48,32},{64,80},{80,64},{96,112},{112,96},{1... | collective-permute-start | bytes 589832 | tf_op jit(solution)/shard_map/ppermute | solution.py:433
  4.0 7.2 %collective-permute-start.1 = (bf16[384,256]{1,0:T(8,128)(2,1)}, bf16[384,256]{1,0:T(8,128)(2,1)S(1)}, u32[]{:S(2)}, u32[]{:S(2)}) collective-permute-start(bf16[384,256]{1,0:T(8,128)(2,1)} %bitcast.19), channel_id=1, source_target_pairs={{16,32},{32,16},{48,64},{64,48},{80,96},{96,80},{112,128},{128,112... | collective-permute-start | bytes 589832 | tf_op jit(solution)/shard_map/ppermute | solution.py:432
  6.6 0.9 copy-start.2
  7.5 0.9 copy-start.4
  11.2 7.9 %copy-start.6 = (f32[1536]{0:T(1024)S(1)}, f32[1536]{0:T(1024)}, u32[]{:S(2)}) copy-start(f32[1536]{0:T(1024)} %param.17) | copy-start | bytes 18436
  11.2 7.9 %copy-start.7 = (f32[384]{0:T(512)S(1)}, f32[384]{0:T(512)}, u32[]{:S(2)}) copy-start(f32[384]{0:T(512)} %param.14) | copy-start | bytes 4612
  11.2 8.0 %copy-start.8 = (f32[384]{0:T(512)S(1)}, f32[384]{0:T(512)}, u32[]{:S(2)}) copy-start(f32[384]{0:T(512)} %param.15) | copy-start | bytes 4612
  11.2 8.0 %copy-start.9 = (f32[384]{0:T(512)S(1)}, f32[384]{0:T(512)}, u32[]{:S(2)}) copy-start(f32[384]{0:T(512)} %param.19) | copy-start | bytes 4612
  14.0 13.0 %all-to-all-start = ((bf16[16,24,512]{2,1,0:T(8,128)(2,1)}), bf16[16,24,512]{2,1,0:T(8,128)(2,1)S(1)}, u32[]{:S(2)}, u32[]{:S(2)}) async-start(bf16[16,24,512]{2,1,0:T(8,128)(2,1)} %bitcast.3), calls=%async_computation | async-start | bytes 786432 | tf_op jit(solution)/shard_map/all_to_all | solution.py:500
  19.2 1.3 %copy-start = (bf16[1536,384]{1,0:T(8,128)(2,1)S(1)}, bf16[1536,384]{1,0:T(8,128)(2,1)}, u32[]{:S(2)}) copy-start(bf16[1536,384]{1,0:T(8,128)(2,1)} %weight_in.1) | copy-start | bytes 3538948
  20.5 1.3 %copy-start.1 = (bf16[384,1536]{1,0:T(8,128)(2,1)S(1)}, bf16[384,1536]{1,0:T(8,128)(2,1)}, u32[]{:S(2)}) copy-start(bf16[384,1536]{1,0:T(8,128)(2,1)} %weight_out.1) | copy-start | bytes 3538948
  29.4 2.9 %collective-permute-start.2 = (bf16[16,96,384]{2,1,0:T(8,128)(2,1)S(1)}, bf16[16,96,384]{2,1,0:T(8,128)(2,1)S(1)}, u32[]{:S(2)}, u32[]{:S(2)}) collective-permute-start(bf16[16,96,384]{2,1,0:T(8,128)(2,1)S(1)} %get-tuple-element.56), channel_id=1, source_target_pairs={{0,16},{16,0},{32,48},{48,32},{64,80},{80,64},{96,112},{112,96},{1... | collective-permute-start | bytes 3538952 | tf_op jit(solution)/shard_map/ppermute | solution.py:520
  57.5 6.6 %collective-permute-start.5 = (bf16[104,384]{1,0:T(8,128)(2,1)S(1)}, bf16[104,384]{1,0:T(8,128)(2,1)S(1)}, u32[]{:S(2)}, u32[]{:S(2)}) collective-permute-start(bf16[104,384]{1,0:T(8,128)(2,1)S(1)} %pad_maximum_fusion.sent), channel_id=1, source_target_pairs={{0,32},{16,48},{32,0},{48,16},{64,96},{80,112},{96,64},{112,80},{1... | collective-permute-start | bytes 239624 | tf_op jit(solution)/shard_map/ppermute | solution.py:538
  64.2 6.4 %collective-permute-start.6 = (bf16[112,384]{1,0:T(8,128)(2,1)S(1)}, bf16[112,384]{1,0:T(8,128)(2,1)S(1)}, u32[]{:S(2)}, u32[]{:S(2)}) collective-permute-start(bf16[112,384]{1,0:T(8,128)(2,1)S(1)} %step.2.sent), channel_id=1, source_target_pairs={{0,96},{16,112},{32,64},{48,80},{64,32},{80,48},{96,0},{112,16},{1... | collective-permute-start | bytes 258056 | tf_op jit(solution)/shard_map/ppermute | solution.py:550
  70.7 6.3 %collective-permute-start.7 = (bf16[112,384]{1,0:T(8,128)(2,1)S(1)}, bf16[112,384]{1,0:T(8,128)(2,1)S(1)}, u32[]{:S(2)}, u32[]{:S(2)}) collective-permute-start(bf16[112,384]{1,0:T(8,128)(2,1)S(1)} %step.3.sent), channel_id=1, source_target_pairs={{0,224},{16,240},{32,192},{48,208},{64,160},{80,176},{96,128},{112... | collective-permute-start | bytes 258056 | tf_op jit(solution)/shard_map/ppermute | solution.py:552
  78.2 16.2 %copy-start.3 = (bf16[24,16,256]{2,1,0:T(8,128)(2,1)S(1)}, bf16[24,16,256]{2,1,0:T(8,128)(2,1)}, u32[]{:S(2)}) copy-start(bf16[24,16,256]{2,1,0:T(8,128)(2,1)} %param.10) | copy-start | bytes 589828
  78.2 16.2 %copy-start.5 = (bf16[24,16,256]{2,1,0:T(8,128)(2,1)S(1)}, bf16[24,16,256]{2,1,0:T(8,128)(2,1)}, u32[]{:S(2)}) copy-start(bf16[24,16,256]{2,1,0:T(8,128)(2,1)} %param.11) | copy-start | bytes 589828
  78.2 19.7 %all-to-all-start.2 = ((bf16[16,104,384]{2,1,0:T(8,128)(2,1)}), bf16[16,104,384]{2,1,0:T(8,128)(2,1)S(1)}, u32[]{:S(2)}, u32[]{:S(2)}) async-start(bf16[16,104,384]{2,1,0:T(8,128)(2,1)} %get-tuple-element.63), calls=%async_computation.2 | async-start | bytes 2555904 | tf_op jit(solution)/shard_map/all_to_all | solution.py:557
  82.1 9.5 %collective-permute-start.3 = (bf16[384,256]{1,0:T(8,128)(2,1)S(1)}, bf16[384,256]{1,0:T(8,128)(2,1)S(1)}, u32[]{:S(2)}, u32[]{:S(2)}) collective-permute-start(bf16[384,256]{1,0:T(8,128)(2,1)S(1)} %get-tuple-element.58.own), channel_id=1, source_target_pairs={{0,16},{16,0},{32,48},{48,32},{64,80},{80,64},{96,112},{112,96},{1... | collective-permute-start | bytes 589832 | tf_op jit(solution)/shard_map/ppermute | solution.py:433
  87.0 7.4 %collective-permute-start.4 = (bf16[384,256]{1,0:T(8,128)(2,1)S(1)}, bf16[384,256]{1,0:T(8,128)(2,1)S(1)}, u32[]{:S(2)}, u32[]{:S(2)}) collective-permute-start(bf16[384,256]{1,0:T(8,128)(2,1)S(1)} %get-tuple-element.58.own), channel_id=1, source_target_pairs={{16,32},{32,16},{48,64},{64,48},{80,96},{96,80},{112,128},{128,112... | collective-permute-start | bytes 589832 | tf_op jit(solution)/shard_map/ppermute | solution.py:432
  89.6 8.3 %collective-permute-start.9 = (f32[8,192]{1,0:T(8,128)S(1)}, f32[8,192]{1,0:T(8,128)S(1)}, u32[]{:S(2)}, u32[]{:S(2)}) collective-permute-start(f32[8,192]{1,0:T(8,128)S(1)} %get-tuple-element.64), channel_id=1, source_target_pairs={{0,32},{16,48},{32,0},{48,16},{64,96},{80,112},{96,64},{112,80},{1... | collective-permute-start | bytes 18440 | tf_op jit(solution)/shard_map/ppermute | solution.py:446
  89.8 8.1 %collective-permute-start.10 = (f32[8,192]{1,0:T(8,128)S(1)}, f32[8,192]{1,0:T(8,128)S(1)}, u32[]{:S(2)}, u32[]{:S(2)}) collective-permute-start(f32[8,192]{1,0:T(8,128)S(1)} %get-tuple-element.64), channel_id=1, source_target_pairs={{0,48},{16,32},{32,16},{48,0},{64,112},{80,96},{96,80},{112,64},{1... | collective-permute-start | bytes 18440 | tf_op jit(solution)/shard_map/ppermute | solution.py:446
  90.8 7.1 %collective-permute-start.8 = (f32[8,192]{1,0:T(8,128)S(1)}, f32[8,192]{1,0:T(8,128)S(1)}, u32[]{:S(2)}, u32[]{:S(2)}) collective-permute-start(f32[8,192]{1,0:T(8,128)S(1)} %get-tuple-element.64), channel_id=1, source_target_pairs={{0,16},{16,0},{32,48},{48,32},{64,80},{80,64},{96,112},{112,96},{1... | collective-permute-start | bytes 18440 | tf_op jit(solution)/shard_map/ppermute | solution.py:446
  97.9 7.7 %collective-permute-start.11 = (bf16[16,104,384]{2,1,0:T(8,128)(2,1)S(1)}, bf16[16,104,384]{2,1,0:T(8,128)(2,1)S(1)}, u32[]{:S(2)}, u32[]{:S(2)}) collective-permute-start(bf16[16,104,384]{2,1,0:T(8,128)(2,1)S(1)} %all-to-all-done.2.ref), channel_id=1, source_target_pairs={{0,16},{16,0},{32,48},{48,32},{64,80},{80,64},{96,112},{112,96},{1... | collective-permute-start | bytes 3833864 | tf_op jit(solution)/shard_map/ppermute | solution.py:573
